TPU v7x, 256 devices: a whole 4x4x8 slice. The times are simulated.
256 devices in a mesh: ax: 16 (over z, core), xs: 16 (over x, y).
Axes of the slice: x: 4, y: 4, z: 8, core: 2. Of those that a mesh axis runs over, the one named last changes fastest.
Arguments:
- scalar: float32 [128, 256, 1024], P('ax', 'xs'), may hold values from 0 to 1
- axial_rate: float32 [128, 256, 1024], P('ax', 'xs'), may hold values from 1.1 to 2.4
- swirl_rate: float32 [128, 256, 1024], P('ax', 'xs'), may hold values from -4 to 4
Outputs:
- transported: float32 [128, 256, 1024], P('ax', 'xs')
All inputs are finite; a program needn't handle non-finite values.
Results may differ from a plain program's by a relative error of at most 0.00014.
Values sent between devices are 32-bit elements; how exact they have to be, the bound alone decides.
No kernel may reach another device: no remote copies, remote signals or barrier semaphores. Data moves between devices by JAX's collectives and lax.ppermute only.
A program may use at most 64 MiB of HBM per device.

v0:
```python
import math

import jax
import jax.numpy as jnp
from jax import lax
from jax.sharding import PartitionSpec as P

CZ = 8
SUBSTEPS = 2


axial_weight = 0.2
azimuth_damp = 0.5
diffusion_number = 1.0
stencil_coeffs = (
    -1.0 / 560.0,
    8.0 / 315.0,
    -0.2,
    1.6,
    -205.0 / 72.0,
    1.6,
    -0.2,
    8.0 / 315.0,
    -1.0 / 560.0,
)


def with_halo(block, sides, width):
    for axis, dim in sides:
        count = lax.axis_size(axis)
        forward = [(i, i + 1) for i in range(count - 1)]
        backward = [(target, source) for source, target in forward]
        low = lax.ppermute(
            lax.slice_in_dim(block, block.shape[dim] - width, None, axis=dim), axis, forward
        )
        high = lax.ppermute(lax.slice_in_dim(block, 0, width, axis=dim), axis, backward)
        block = jnp.concatenate([low, block, high], axis=dim)
    return block


def from_behind(value, axis, steps):
    count = lax.axis_size(axis)
    initial, last = (max(0, -steps), min(count, count - steps))
    return lax.ppermute(value, axis, [(source, source + steps) for source in range(initial, last)])


def radial_bands(cell_count, diffusion_value):
    cell_index = jnp.arange(cell_count, dtype=jnp.float32)
    radius = cell_index + 0.5
    upper_face = jnp.where(cell_index < cell_count - 1, cell_index + 1.0, 0.0)
    sub_diag = -diffusion_value * cell_index / radius
    super_diag = -diffusion_value * upper_face / radius
    main_diag = 1.0 - sub_diag - super_diag
    return (sub_diag, main_diag, super_diag)


def azimuth_tables(point_count):
    nyquist = point_count // 2
    column = jnp.arange(point_count, dtype=jnp.int32)
    cosine_cols = column <= nyquist
    wavenum = jnp.where(cosine_cols, column, column - nyquist)
    grid_point = jnp.arange(point_count, dtype=jnp.int32)
    phase_index = grid_point[:, None] * wavenum[None, :] % point_count
    angle_rad = phase_index.astype(jnp.float32) * (2.0 * math.pi / point_count)
    cosine = jnp.cos(angle_rad)
    sine_table = jnp.sin(angle_rad)
    forward = jnp.where(cosine_cols[None, :], cosine, sine_table)
    weight = jnp.where((wavenum == 0) | (wavenum == nyquist), 1.0, 2.0) / point_count
    inverse_smooth = jnp.transpose(forward * weight[None, :])
    slope_rate = wavenum.astype(jnp.float32) * (2.0 * math.pi / point_count) * (2.0 / point_count)
    slope_rate = jnp.where(cosine_cols & (wavenum == nyquist), 0.0, slope_rate)
    derivative = jnp.where(
        cosine_cols[None, :], -slope_rate[None, :] * sine_table, slope_rate[None, :] * cosine
    )
    inverse = jnp.concatenate([inverse_smooth, jnp.transpose(derivative)], axis=1)
    return (forward, inverse, wavenum)


def combine_pairs(earlier, later):
    return (earlier[0] * later[0], later[0] * earlier[1] + later[1])


def apply_lines(matrix, lines):
    return jnp.einsum(
        "ri,zic->zrc",
        matrix,
        lines,
        precision=lax.Precision.HIGHEST,
        preferred_element_type=jnp.float32,
    )


def body(scalar, axial_rate, swirl_rate):
    plane_count, radial_rows, azimuth_points = scalar.shape
    group_count = lax.axis_size("xs")
    radii_all = radial_rows * group_count
    forward, inverse, wavenum = azimuth_tables(azimuth_points)
    group_index = lax.axis_index("xs")
    first_row = group_index * radial_rows
    radius = (first_row + jnp.arange(radial_rows, dtype=jnp.int32)).astype(jnp.float32) + 0.5
    damping = 1.0 / (
        1.0
        + azimuth_damp
        * jnp.square(wavenum.astype(jnp.float32))[None, :]
        / jnp.square(radius)[:, None]
    )
    courant = CZ * axial_rate
    factor = courant / (1.0 + courant)
    sub_diag, main_diag, super_diag = radial_bands(radii_all, diffusion_number)
    green = lax.linalg.tridiagonal_solve(
        sub_diag, main_diag, super_diag, jnp.eye(radii_all, dtype=jnp.float32)
    )
    field_now = scalar
    for substep in range(SUBSTEPS):
        padded = with_halo(field_now, (("ax", 0),), 4)
        stencil_sum = jnp.zeros_like(field_now)
        for offset in range(9):
            stencil_sum = (
                stencil_sum + stencil_coeffs[offset] * padded[offset : offset + plane_count]
            )
        explicit_field = field_now + axial_weight * stencil_sum
        result = apply_lines(
            green, lax.all_to_all(explicit_field, "xs", split_axis=2, concat_axis=1, tiled=True)
        )
        solved = lax.all_to_all(result, "xs", split_axis=1, concat_axis=2, tiled=True)
        spectrum = jnp.dot(
            solved, forward, precision=lax.Precision.HIGHEST, preferred_element_type=jnp.float32
        )
        spectrum = spectrum * damping
        physical = jnp.dot(
            spectrum, inverse, precision=lax.Precision.HIGHEST, preferred_element_type=jnp.float32
        )
        smooth = physical[..., :azimuth_points]
        azimuth_slope = physical[..., azimuth_points:]
        source = smooth - swirl_rate * azimuth_slope
        scaled = source / (1.0 + courant)
        decay_prod, partial_value = lax.associative_scan(combine_pairs, (factor, scaled), axis=0)
        total_decay = decay_prod[-1]
        total_value = partial_value[-1]

        def relay_turn(turn_index, entering):
            return from_behind(total_decay * entering + total_value, "ax", 1)

        incoming = lax.fori_loop(
            0, lax.axis_size("ax") - 1, relay_turn, jnp.zeros_like(total_value)
        )
        field_now = partial_value + decay_prod * incoming
    return field_now


def solution(mesh):
    return jax.shard_map(
        body,
        mesh=mesh,
        in_specs=(P("ax", "xs", None), P("ax", "xs", None), P("ax", "xs", None)),
        out_specs=P("ax", "xs", None),
        check_vma=False,
    )
```

profile of v0, /device:TPU:128, one launch (start us, length us, event | category | flops | bytes accessed | tf_op | source)
XLA Modules:
  0.0 1247.1 jit_solution(8745229380887297586)
XLA Ops:
  11.9 592.6 %while.52 = (s32[]{:T(128)}, f32[]{:T(128)}, f32[256]{0:T(256)S(1)}, f32[7,32]{1,0:T(8,128)S(1)}, f32[7,32,256]{2,1,0:T(8,128)S(1)}, /*index=5*/f32[7,32]{1,0:T(...) while((s32[]{:T(128)}, f32[]{:T(128)}, ...), condition=%wide.region_1.2_spmd, body=%wide.region_0.1_spmd.sunk | while | flops 24705 | bytes 269565 | solution.py:110
  76.4 19.8 %subtract_divide_fusion.125 = (f32[256]{0:T(256)S(1)}, f32[256]{0:T(256)S(1)}, f32[256]{0:T(256)S(1)}, f32[256]{0:T(256)S(1)}, f32[256]{0:T(256)S(1)}, /*index=5...) fusion(f32[256]{0:T(256)S(1)} %bitcast.1286, ...), kind=kLoop, calls=%fused_computation.36.clone.1 | loop fusion | flops 24576 | bytes 66816 | tf_op jit(solution)/shard_map/while/body/eval_jaxpr/div | solution.py:110
  161.1 19.8 %subtract_divide_fusion.125 = (f32[256]{0:T(256)S(1)}, f32[256]{0:T(256)S(1)}, f32[256]{0:T(256)S(1)}, f32[256]{0:T(256)S(1)}, f32[256]{0:T(256)S(1)}, /*index=5...) fusion(f32[256]{0:T(256)S(1)} %bitcast.1286, ...), kind=kLoop, calls=%fused_computation.36.clone.1 | loop fusion | flops 24576 | bytes 66816 | tf_op jit(solution)/shard_map/while/body/eval_jaxpr/div | solution.py:110
  245.7 19.8 %subtract_divide_fusion.125 = (f32[256]{0:T(256)S(1)}, f32[256]{0:T(256)S(1)}, f32[256]{0:T(256)S(1)}, f32[256]{0:T(256)S(1)}, f32[256]{0:T(256)S(1)}, /*index=5...) fusion(f32[256]{0:T(256)S(1)} %bitcast.1286, ...), kind=kLoop, calls=%fused_computation.36.clone.1 | loop fusion | flops 24576 | bytes 66816 | tf_op jit(solution)/shard_map/while/body/eval_jaxpr/div | solution.py:110
  330.4 19.8 %subtract_divide_fusion.125 = (f32[256]{0:T(256)S(1)}, f32[256]{0:T(256)S(1)}, f32[256]{0:T(256)S(1)}, f32[256]{0:T(256)S(1)}, f32[256]{0:T(256)S(1)}, /*index=5...) fusion(f32[256]{0:T(256)S(1)} %bitcast.1286, ...), kind=kLoop, calls=%fused_computation.36.clone.1 | loop fusion | flops 24576 | bytes 66816 | tf_op jit(solution)/shard_map/while/body/eval_jaxpr/div | solution.py:110
  415.0 19.8 %subtract_divide_fusion.125 = (f32[256]{0:T(256)S(1)}, f32[256]{0:T(256)S(1)}, f32[256]{0:T(256)S(1)}, f32[256]{0:T(256)S(1)}, f32[256]{0:T(256)S(1)}, /*index=5...) fusion(f32[256]{0:T(256)S(1)} %bitcast.1286, ...), kind=kLoop, calls=%fused_computation.36.clone.1 | loop fusion | flops 24576 | bytes 66816 | tf_op jit(solution)/shard_map/while/body/eval_jaxpr/div | solution.py:110
  499.7 19.8 %subtract_divide_fusion.125 = (f32[256]{0:T(256)S(1)}, f32[256]{0:T(256)S(1)}, f32[256]{0:T(256)S(1)}, f32[256]{0:T(256)S(1)}, f32[256]{0:T(256)S(1)}, /*index=5...) fusion(f32[256]{0:T(256)S(1)} %bitcast.1286, ...), kind=kLoop, calls=%fused_computation.36.clone.1 | loop fusion | flops 24576 | bytes 66816 | tf_op jit(solution)/shard_map/while/body/eval_jaxpr/div | solution.py:110
  584.4 19.8 %subtract_divide_fusion.125 = (f32[256]{0:T(256)S(1)}, f32[256]{0:T(256)S(1)}, f32[256]{0:T(256)S(1)}, f32[256]{0:T(256)S(1)}, f32[256]{0:T(256)S(1)}, /*index=5...) fusion(f32[256]{0:T(256)S(1)} %bitcast.1286, ...), kind=kLoop, calls=%fused_computation.36.clone.1 | loop fusion | flops 24576 | bytes 66816 | tf_op jit(solution)/shard_map/while/body/eval_jaxpr/div | solution.py:110
  666.5 19.6 %subtract_divide_fusion.32 = (f32[256]{0:T(256)S(1)}, f32[256]{0:T(256)S(1)}, f32[256]{0:T(256)S(1)}, f32[256]{0:T(256)S(1)}, f32[256]{0:T(256)S(1)}, /*index=5*...) fusion(f32[256]{0:T(256)S(1)} %bitcast.1491, ...), kind=kLoop, calls=%fused_computation.335 | loop fusion | flops 23808 | bytes 64760 | tf_op jit(solution)/shard_map/eval_jaxpr/div | solution.py:110
  686.5 153.5 %while.53 = (s32[]{:T(128)}, f32[256]{0:T(256)S(1)}, f32[7,32,256]{2,1,0:T(8,128)S(1)}, f32[7,32,256]{2,1,0:T(8,128)S(1)}, f32[7,32]{1,0:T(8,128)S(1)}, /*index=...) while((s32[]{:T(128)}, f32[256]{0:T(256)S(1)}, ...), condition=%wide.region_3.4_spmd, body=%wide.region_2.3_spmd.sunk | while | flops 16418 | bytes 266721 | solution.py:110
  688.2 20.1 %multiply_subtract_fusion.125 = (f32[256]{0:T(256)S(1)}, f32[256]{0:T(256)S(1)}, f32[256]{0:T(256)S(1)}, f32[256]{0:T(256)S(1)}, f32[256]{0:T(256)S(1)}, /*index...) fusion(f32[256]{0:T(256)S(1)} %bitcast.1353, ...), kind=kLoop, calls=%fused_computation.102.clone.1 | loop fusion | flops 16384 | bytes 66688 | tf_op jit(solution)/shard_map/while/body/eval_jaxpr/sub | solution.py:110
  710.1 20.1 %multiply_subtract_fusion.125 = (f32[256]{0:T(256)S(1)}, f32[256]{0:T(256)S(1)}, f32[256]{0:T(256)S(1)}, f32[256]{0:T(256)S(1)}, f32[256]{0:T(256)S(1)}, /*index...) fusion(f32[256]{0:T(256)S(1)} %bitcast.1353, ...), kind=kLoop, calls=%fused_computation.102.clone.1 | loop fusion | flops 16384 | bytes 66688 | tf_op jit(solution)/shard_map/while/body/eval_jaxpr/sub | solution.py:110
  732.1 20.1 %multiply_subtract_fusion.125 = (f32[256]{0:T(256)S(1)}, f32[256]{0:T(256)S(1)}, f32[256]{0:T(256)S(1)}, f32[256]{0:T(256)S(1)}, f32[256]{0:T(256)S(1)}, /*index...) fusion(f32[256]{0:T(256)S(1)} %bitcast.1353, ...), kind=kLoop, calls=%fused_computation.102.clone.1 | loop fusion | flops 16384 | bytes 66688 | tf_op jit(solution)/shard_map/while/body/eval_jaxpr/sub | solution.py:110
  754.0 20.1 %multiply_subtract_fusion.125 = (f32[256]{0:T(256)S(1)}, f32[256]{0:T(256)S(1)}, f32[256]{0:T(256)S(1)}, f32[256]{0:T(256)S(1)}, f32[256]{0:T(256)S(1)}, /*index...) fusion(f32[256]{0:T(256)S(1)} %bitcast.1353, ...), kind=kLoop, calls=%fused_computation.102.clone.1 | loop fusion | flops 16384 | bytes 66688 | tf_op jit(solution)/shard_map/while/body/eval_jaxpr/sub | solution.py:110
  775.9 20.1 %multiply_subtract_fusion.125 = (f32[256]{0:T(256)S(1)}, f32[256]{0:T(256)S(1)}, f32[256]{0:T(256)S(1)}, f32[256]{0:T(256)S(1)}, f32[256]{0:T(256)S(1)}, /*index...) fusion(f32[256]{0:T(256)S(1)} %bitcast.1353, ...), kind=kLoop, calls=%fused_computation.102.clone.1 | loop fusion | flops 16384 | bytes 66688 | tf_op jit(solution)/shard_map/while/body/eval_jaxpr/sub | solution.py:110
  797.8 20.1 %multiply_subtract_fusion.125 = (f32[256]{0:T(256)S(1)}, f32[256]{0:T(256)S(1)}, f32[256]{0:T(256)S(1)}, f32[256]{0:T(256)S(1)}, f32[256]{0:T(256)S(1)}, /*index...) fusion(f32[256]{0:T(256)S(1)} %bitcast.1353, ...), kind=kLoop, calls=%fused_computation.102.clone.1 | loop fusion | flops 16384 | bytes 66688 | tf_op jit(solution)/shard_map/while/body/eval_jaxpr/sub | solution.py:110
  819.8 20.1 %multiply_subtract_fusion.125 = (f32[256]{0:T(256)S(1)}, f32[256]{0:T(256)S(1)}, f32[256]{0:T(256)S(1)}, f32[256]{0:T(256)S(1)}, f32[256]{0:T(256)S(1)}, /*index...) fusion(f32[256]{0:T(256)S(1)} %bitcast.1353, ...), kind=kLoop, calls=%fused_computation.102.clone.1 | loop fusion | flops 16384 | bytes 66688 | tf_op jit(solution)/shard_map/while/body/eval_jaxpr/sub | solution.py:110
  840.0 19.4 %multiply_subtract_fusion.32 = (f32[256]{0:T(256)S(1)}, f32[256]{0:T(256)S(1)}, f32[256]{0:T(256)S(1)}, f32[256]{0:T(256)S(1)}, f32[256]{0:T(256)S(1)}, /*index=...) fusion(f32[256]{0:T(256)S(1)} %bitcast.1441, ...), kind=kLoop, calls=%fused_computation.304 | loop fusion | flops 15872 | bytes 64636 | tf_op jit(solution)/shard_map/eval_jaxpr/sub | solution.py:110
  866.9 7.2 all-to-all-start
  874.4 9.8 all-to-all-done
  899.7 20.0 %select_multiply_fusion = (f32[1024,1024]{1,0:T(8,128)}, f32[1024,1024]{1,0:T(8,128)}) fusion(f32[1024]{0:T(1024)S(1)} %get-tuple-element.794, s32[1024]{0:T(1024)S(1)} %add_select_fusion.2, pred[1024]{0:T(1024)(128)(4,1)S(1)} %iota_compare_fusion.1, f32[1024]{0:T(1024)S(1)} %get-tuple-element.793, f32[1024]{0:T(1024)S(1)} %fusion.81), kind=kLoop, calls=%fused_computation.156 | loop fusion | flops 19922944 | bytes 8406016 | tf_op jit(solution)/shard_map/mul | solution.py:69
  922.9 19.8 %fusion.20 = f32[8,16,1024]{2,1,0:T(8,128)S(1)} fusion(f32[8,16,1024]{2,1,0:T(8,128)S(1)} %all_to_all.59, s32[1024]{0:T(1024)S(1)} %add_select_fusion.2, pred[1024]{0:T(1024)(128)(4,1)S(1)} %iota_compare_fusion.1, f32[16,1024]{1,0:T(8,128)S(1)} %fusion.67), kind=kOutput, calls=%fused_computation.168 | convolution fusion | flops 1626472448 | bytes 1119232 | tf_op jit(solution)/shard_map/dot_general | solution.py:126
  952.5 102.2 %while.54 = (s32[]{:T(128)}, f32[16,1024]{1,0:T(8,128)S(1)}, f32[16,1024]{1,0:T(8,128)S(1)}, f32[16,1024]{1,0:T(8,128)S(1)}, s32[]{:T(128)}) while((s32[]{:T(128)}, f32[16,1024]{1,0:T(8,128)S(1)}, f32[16,1024]{1,0:T(8,128)S(1)}, f32[16,1024]{1,0:T(8,128)S(1)}, s32[]{:T(128)}) %tuple.606), condition=%wide.region_5.6_spmd, body=%wide.region_4.5_spmd.sunk | while | flops 32770 | bytes 524389 | solution.py:144
  954.5 4.9 collective-permute-done
  968.1 4.9 collective-permute-done
  974.9 4.9 collective-permute-done
  981.8 4.9 collective-permute-done
  988.6 4.9 collective-permute-done
  995.4 4.9 collective-permute-done
  1002.2 4.9 collective-permute-done
  1009.0 4.9 collective-permute-done
  1015.8 4.9 collective-permute-done
  1022.6 4.9 collective-permute-done
  1029.4 4.9 collective-permute-done
  1036.2 4.9 collective-permute-done
  1043.1 4.9 collective-permute-done
  1049.9 4.9 collective-permute-done
  1061.5 5.0 collective-permute-done.4
  1073.1 17.4 %all_to_all.72 = f32[16,1,8192]{2,1,0:T(1,128)S(1)} all-to-all(f32[16,1,8192]{2,1,0:T(1,128)S(1)} %reshape.504), channel_id=1, replica_groups=mesh['ax'=16,'xs'=16] {'xs'}, dimensions={0} | all-to-all | bytes 1048576 | tf_op jit(solution)/shard_map/all_to_all | solution.py:123
  1101.0 13.9 %all_to_all.73 = f32[16,1,8192]{2,1,0:T(1,128)S(1)} all-to-all(f32[16,1,8192]{2,1,0:T(1,128)S(1)} %reshape.506), channel_id=1, replica_groups=mesh['ax'=16,'xs'=16] {'xs'}, dimensions={0} | all-to-all | bytes 1048576 | tf_op jit(solution)/shard_map/all_to_all | solution.py:125
  1118.1 19.7 %fusion.23 = f32[8,16,1024]{2,1,0:T(8,128)S(1)} fusion(f32[8,16,1024]{2,1,0:T(8,128)S(1)} %all_to_all.67, s32[1024]{0:T(1024)S(1)} %add_select_fusion.2, pred[1024]{0:T(1024)(128)(4,1)S(1)} %iota_compare_fusion.1, f32[16,1024]{1,0:T(8,128)S(1)} %fusion.67), kind=kOutput, calls=%fused_computation.169 | convolution fusion | flops 1626472448 | bytes 1119232 | tf_op jit(solution)/shard_map/dot_general | solution.py:126
  1143.8 102.2 %while.55 = (s32[]{:T(128)}, f32[16,1024]{1,0:T(8,128)S(1)}, f32[16,1024]{1,0:T(8,128)S(1)}, f32[16,1024]{1,0:T(8,128)S(1)}, s32[]{:T(128)}) while((s32[]{:T(128)}, f32[16,1024]{1,0:T(8,128)S(1)}, f32[16,1024]{1,0:T(8,128)S(1)}, f32[16,1024]{1,0:T(8,128)S(1)}, s32[]{:T(128)}) %tuple.612), condition=%wide.region_7.8_spmd, body=%wide.region_6.7_spmd.sunk | while | flops 32770 | bytes 524389 | solution.py:144
  1145.8 4.9 collective-permute-done.1
  1152.6 4.9 collective-permute-done.1
  1159.4 4.9 collective-permute-done.1
  1173.0 4.9 collective-permute-done.1
  1179.9 4.9 collective-permute-done.1
  1186.7 4.9 collective-permute-done.1
  (384 shorter events, 237.1 us)
Async XLA Ops:
  1.1 858.4 %collective-permute-start.2 = (f32[4,16,1024]{2,1,0:T(8,128)S(1)}, f32[4,16,1024]{2,1,0:T(8,128)S(1)}, u32[]{:S(2)}, u32[]{:S(2)}) collective-permute-start(f32[4,16,1024]{2,1,0:T(8,128)S(1)} %get-tuple-element.587), channel_id=1, source_target_pairs={{0,16},{16,32},{32,48},{48,64},{64,80},{80,96},{96,112},{112,128},... | collective-permute-start | bytes 786440 | tf_op jit(solution)/shard_map/ppermute | solution.py:33
  3.0 856.6 %collective-permute-start.3 = (f32[4,16,1024]{2,1,0:T(8,128)S(1)}, f32[4,16,1024]{2,1,0:T(8,128)S(1)}, u32[]{:S(2)}, u32[]{:S(2)}) collective-permute-start(f32[4,16,1024]{2,1,0:T(8,128)S(1)} %get-tuple-element.588), channel_id=1, source_target_pairs={{16,0},{32,16},{48,32},{64,48},{80,64},{96,80},{112,96},{128,112},... | collective-permute-start | bytes 786440 | tf_op jit(solution)/shard_map/ppermute | solution.py:36
  604.5 255.0 %copy-start.4 = (f32[8,16,1024]{2,1,0:T(8,128)S(1)}, f32[8,16,1024]{2,1,0:T(8,128)}, u32[]{:S(2)}) copy-start(f32[8,16,1024]{2,1,0:T(8,128)} %param.11) | copy-start | bytes 1572868
  866.9 17.3 %all-to-all-start = ((f32[16,1,8192]{2,1,0:T(1,128)}), f32[16,1,8192]{2,1,0:T(1,128)S(1)}, u32[]{:S(2)}, u32[]{:S(2)}) async-start(f32[16,1,8192]{2,1,0:T(1,128)} %reshape.500), calls=%async_computation | async-start | bytes 1048576 | tf_op jit(solution)/shard_map/all_to_all | solution.py:123
  895.9 23.7 %all-to-all-start.1 = ((f32[16,1,8192]{2,1,0:T(1,128)}), f32[16,1,8192]{2,1,0:T(1,128)S(1)}, u32[]{:S(2)}, u32[]{:S(2)}) async-start(f32[16,1,8192]{2,1,0:T(1,128)} %reshape.502), calls=%async_computation.1 | async-start | bytes 1048576 | tf_op jit(solution)/shard_map/all_to_all | solution.py:125
  922.9 19.8 %copy-start = (f32[1024,1024]{1,0:T(8,128)S(1)}, f32[1024,1024]{1,0:T(8,128)}, u32[]{:S(2)}) copy-start(f32[1024,1024]{1,0:T(8,128)} %get-tuple-element.666) | copy-start | bytes 12582916
  922.9 19.8 %copy-start.2 = (f32[1024,1024]{1,0:T(8,128)S(1)}, f32[1024,1024]{1,0:T(8,128)}, u32[]{:S(2)}) copy-start(f32[1024,1024]{1,0:T(8,128)} %get-tuple-element.667) | copy-start | bytes 12582916
  942.7 4.6 copy-start.5
  942.7 4.6 copy-start.7
  947.7 1.3 copy-start.10
  952.6 6.8 collective-permute-start
  959.4 6.8 collective-permute-start
  966.2 6.8 collective-permute-start
  973.0 6.8 collective-permute-start
  979.8 6.8 collective-permute-start
  986.6 6.8 collective-permute-start
  993.4 6.8 collective-permute-start
  1000.3 6.8 collective-permute-start
  1007.1 6.8 collective-permute-start
  1013.9 6.8 collective-permute-start
  1020.7 6.8 collective-permute-start
  1027.5 6.8 collective-permute-start
  1034.3 6.8 collective-permute-start
  1041.1 6.8 collective-permute-start
  1047.9 6.8 collective-permute-start
  1055.7 5.8 collective-permute-start.5
  1057.7 8.9 collective-permute-start.4
  1118.1 19.7 %copy-start.1 = (f32[1024,1024]{1,0:T(8,128)S(1)}, f32[1024,1024]{1,0:T(8,128)}, u32[]{:S(2)}) copy-start(f32[1024,1024]{1,0:T(8,128)} %get-tuple-element.666) | copy-start | bytes 12582916
  1118.1 19.7 %copy-start.3 = (f32[1024,1024]{1,0:T(8,128)S(1)}, f32[1024,1024]{1,0:T(8,128)}, u32[]{:S(2)}) copy-start(f32[1024,1024]{1,0:T(8,128)} %get-tuple-element.667) | copy-start | bytes 12582916
  1137.9 4.6 copy-start.6
  1137.9 4.6 copy-start.8
  1142.5 0.9 copy-start.11
  1142.7 103.3 %copy-start.9 = (f32[8,16,1024]{2,1,0:T(8,128)S(1)}, f32[8,16,1024]{2,1,0:T(8,128)}, u32[]{:S(2)}) copy-start(f32[8,16,1024]{2,1,0:T(8,128)} %get-tuple-element.320) | copy-start | bytes 1572868
  1143.9 6.8 collective-permute-start.1
  1150.7 6.8 collective-permute-start.1
  1157.5 6.8 collective-permute-start.1
  1164.3 6.8 collective-permute-start.1
  1171.1 6.8 collective-permute-start.1
  1177.9 6.8 collective-permute-start.1
  1184.7 6.8 collective-permute-start.1
  1191.6 6.8 collective-permute-start.1
  1198.4 6.8 collective-permute-start.1
  1205.2 6.8 collective-permute-start.1
  1212.0 6.8 collective-permute-start.1
  1218.8 6.8 collective-permute-start.1
  1225.6 6.8 collective-permute-start.1
  1232.4 6.8 collective-permute-start.1
  1239.2 6.8 collective-permute-start.1
where the time goes:
time: 1270 us; the launch traced here: 1250 us
  loops' own time  421 us (33%)
  other arithmetic  353 us (28%)
  waiting for transfers between devices  162 us (13%)
  local copies, waits for them, and re-layouts  87.2 us (7%)
  starting transfers between devices  79.7 us (6%)
  between operations  60 us (5%)
  matrix products  52.2 us (4%)
  blocking collectives  31.3 us (2%)
    another operation x2, loops' own time, body(): lax.linalg.tridiagonal_solve(sub_diag, main_diag, super_diag, jnp.eye(rad...  421 us
    sub x8, other arithmetic, body(): lax.linalg.tridiagonal_solve(sub_diag, main_diag, super_diag, jnp.eye(rad...  160 us
    div x8, other arithmetic, body(): lax.linalg.tridiagonal_solve(sub_diag, main_diag, super_diag, jnp.eye(rad...  158 us
    ppermute x30, waiting for transfers between devices, from_behind(): lax.ppermute(value, axis, [(source, source + steps) for source in range(i...  146 us
    ppermute x30, starting transfers between devices, from_behind(): lax.ppermute(value, axis, [(source, source + steps) for source in range(i...  57.6 us
    slice x101, local copies, waits for them, and re-layouts, body(): lax.linalg.tridiagonal_solve(sub_diag, main_diag, super_diag, jnp.eye(rad...  48.8 us
    dot_general x2, matrix products, body(): jnp.dot(solved, forward, precision=lax.Precision.HIGHEST, preferred_eleme...  39.5 us
  transfers between devices with their start and end apart: 36, of which 33 were waited for; matrix products, arithmetic and copies ran while one was open for 31% of the time, Pallas kernels for 0%

commit v1 on v0

v1 whole, which is shorter than its diff:
```python
import math

import jax
import jax.numpy as jnp
import ml_dtypes
import numpy as np
from jax import lax
from jax.sharding import PartitionSpec as P

CZ = 8
SUBSTEPS = 2
AXIAL_WEIGHT = 0.2
AZIMUTH_DAMP = 0.5
DIFFUSION = 1.0
STENCIL = (
    -1.0 / 560.0,
    8.0 / 315.0,
    -0.2,
    1.6,
    -205.0 / 72.0,
    1.6,
    -0.2,
    8.0 / 315.0,
    -1.0 / 560.0,
)
HALO = 4


def split_bf16(table):
    high = table.astype(ml_dtypes.bfloat16)
    low = (table - high.astype(np.float64)).astype(ml_dtypes.bfloat16)
    return high, low


def radial_tables(cells, groups):
    rows = cells // groups
    index = np.arange(cells, dtype=np.float64)
    radius = index + 0.5
    upper = np.where(index < cells - 1, index + 1.0, 0.0)
    sub = -DIFFUSION * index / radius
    sup = -DIFFUSION * upper / radius
    matrix = np.diag(1.0 - sub - sup) + np.diag(sub[1:], -1) + np.diag(sup[:-1], 1)
    green = np.linalg.inv(matrix)
    diag = np.diag(green)
    down = np.diag(green, -1) / diag[:-1]
    up = np.diag(green, 1) / diag[1:]
    local = np.zeros((groups, rows, rows))
    edges = np.zeros((groups, 2, rows))
    join = np.zeros((groups, rows, groups))
    for g in range(groups):
        first, last = g * rows, g * rows + rows - 1
        block = green[first : last + 1, first : last + 1]
        local[g] = block
        edges[g, 0] = block[-1]
        edges[g, 1] = block[0]
        for i in range(rows):
            for source in range(groups):
                if source < g:
                    join[g, i, source] = np.prod(down[source * rows + rows - 1 : first + i])
                elif source > g:
                    join[g, i, source] = np.prod(up[first + i : source * rows])
    return local, edges, join


def axial_tables(count, planes):
    table = np.zeros((count, planes, planes + 2 * HALO))
    for k in range(count):
        low, high = (0, planes + HALO) if k % 2 else (planes + HALO, 0)
        for plane in range(planes):
            for offset in range(-HALO, HALO + 1):
                value = AXIAL_WEIGHT * STENCIL[offset + HALO] + (1.0 if offset == 0 else 0.0)
                where = plane + offset
                if where < 0:
                    if k > 0:
                        table[k, plane, low + where + HALO] += value
                elif where >= planes:
                    if k < count - 1:
                        table[k, plane, high + where - planes] += value
                else:
                    table[k, plane, HALO + where] += value
    return table


def azimuth_tables(points):
    half = points // 2
    grid = np.arange(points)
    phase = (grid[:, None] * np.arange(half)[None, :]) % points
    angle = phase * (2.0 * math.pi / points)
    cosine, sine = np.cos(angle), np.sin(angle)
    sine[:, 0] = np.where(grid % 2 == 0, 1.0, -1.0)
    return np.concatenate([cosine, sine], axis=1)


def filter_tables(cells, points):
    half = points // 2
    radius = np.arange(cells) + 0.5
    wave = np.arange(half + 1.0)
    damp = 1.0 / (1.0 + AZIMUTH_DAMP * wave[None, :] ** 2 / radius[:, None] ** 2)
    weight = np.full(half + 1, 2.0 / points)
    weight[0] = weight[half] = 1.0 / points
    scaled = damp * weight
    rate = damp * (2.0 / points) * (wave * (2.0 * math.pi / points))
    smooth = np.concatenate([scaled[:, :half], scaled[:, half:], scaled[:, 1:half]], axis=1)
    slope = np.concatenate([rate[:, :half], -rate[:, :half]], axis=1)
    return smooth.astype(np.float32), slope.astype(np.float32)


def split_dot(values, high, low):
    coarse = lax.reduce_precision(values, 8, 7)
    fine = (values - coarse).astype(jnp.bfloat16)
    coarse = coarse.astype(jnp.bfloat16)
    out = jnp.dot(coarse, high, preferred_element_type=jnp.float32)
    out = out + jnp.dot(fine, high, preferred_element_type=jnp.float32)
    return out + jnp.dot(coarse, low, preferred_element_type=jnp.float32)


def exact_dot(matrix, values):
    return jnp.dot(
        matrix, values, precision=lax.Precision.HIGHEST, preferred_element_type=jnp.float32
    )


def swap(value, mask):
    count = lax.axis_size("ax")
    return lax.ppermute(value, "ax", [(i, i ^ mask) for i in range(count)])


def chain_swap(value):
    count = lax.axis_size("ax")
    pairs = [(i, (i + 1) % count if i % 2 else (i - 1) % count) for i in range(count)]
    return lax.ppermute(value, "ax", pairs)


def body(scalar, axial_rate, swirl_rate):
    planes, rows, points = scalar.shape
    half = points // 2
    groups = lax.axis_size("xs")
    count = lax.axis_size("ax")
    group = lax.axis_index("xs")
    place = lax.axis_index("ax")
    odd = place % 2 == 1
    upper = (place // 2) % 2 == 1
    quad = place // 4

    local, edges, join = radial_tables(rows * groups, groups)
    axial = axial_tables(count, planes)
    forward = azimuth_tables(points)
    fwd_high, fwd_low = split_bf16(forward)
    inv_high, inv_low = split_bf16(np.ascontiguousarray(forward.T))
    smooth_filter, slope_filter = filter_tables(rows * groups, points)

    def pick(table, index):
        return lax.dynamic_index_in_dim(jnp.asarray(table, jnp.float32), index, 0, keepdims=False)

    axial_here = pick(axial, place)
    local_here = pick(local, group)
    edges_here = pick(edges, group)
    join_here = pick(join, group)
    ext = planes + 2 * HALO
    solve_matrix = jnp.einsum("ze,ij->ziej", axial_here, local_here).reshape(
        planes * rows, ext * rows
    )
    edge_matrix = jnp.einsum("ze,sj->szej", axial_here, edges_here).reshape(
        2 * planes, ext * rows
    )
    join_matrix = jnp.einsum(
        "zy,is->zisy", jnp.eye(planes, dtype=jnp.float32), join_here
    ).reshape(planes * rows, groups * planes)
    smooth_here = lax.dynamic_slice_in_dim(jnp.asarray(smooth_filter), group * rows, rows, 0)
    slope_here = lax.dynamic_slice_in_dim(jnp.asarray(slope_filter), group * rows, rows, 0)

    courant = CZ * axial_rate
    inverse_rate = 1.0 / (1.0 + courant)
    factor = courant * inverse_rate
    swirl_scaled = swirl_rate * inverse_rate
    decays = [factor[0]]
    for plane in range(1, planes):
        decays.append(decays[-1] * factor[plane])
    decay = jnp.stack(decays)

    def pair_part(field):
        return jnp.where(odd, field[:HALO], field[planes - HALO :])

    def chain_part(field):
        return jnp.where(odd, field[planes - HALO :], field[:HALO])

    def own_half(value):
        return jnp.where(odd, value[:, half:], value[:, :half])

    def other_half(value):
        return jnp.where(odd, value[:, :half], value[:, half:])

    pair_field, chain_field = swap(pair_part(scalar), 1), chain_swap(chain_part(scalar))
    extended = jnp.concatenate([pair_field, scalar, chain_field], axis=0)
    pair_decay, chain_decay = swap(pair_part(decay), 1), chain_swap(chain_part(decay))
    pair_decay = jnp.where(odd, pair_decay / pair_decay[HALO - 1], pair_decay)
    chain_decay = jnp.where(odd, chain_decay, chain_decay / chain_decay[HALO - 1])

    field = scalar
    saved = None
    for substep in range(SUBSTEPS):
        flat = extended.reshape(ext * rows, points)
        carry = exact_dot(edge_matrix, flat).reshape(2, planes, points)
        ahead = (jnp.arange(groups) > group)[:, None, None]
        sent = jnp.where(ahead, carry[0][None], carry[1][None])
        got = lax.all_to_all(sent, "xs", split_axis=0, concat_axis=0, tiled=True)
        solved = exact_dot(solve_matrix, flat)
        solved = solved + exact_dot(join_matrix, got.reshape(groups * planes, points))
        spectrum = split_dot(solved, fwd_high, fwd_low).reshape(planes, rows, points)
        smooth_spec = spectrum * smooth_here
        slope_spec = (
            jnp.concatenate([spectrum[..., half:], spectrum[..., :half]], axis=-1) * slope_here
        )
        both = jnp.concatenate([smooth_spec, slope_spec], axis=0).reshape(-1, points)
        physical = split_dot(both, inv_high, inv_low).reshape(2, planes, rows, points)
        scaled = physical[0] * inverse_rate - swirl_scaled * physical[1]
        partials = [scaled[0]]
        for plane in range(1, planes):
            partials.append(factor[plane] * partials[-1] + scaled[plane])
        partial = jnp.stack(partials)
        last_step = substep == SUBSTEPS - 1
        if not last_step:
            pair_field, chain_field = swap(pair_part(partial), 1), chain_swap(chain_part(partial))

        total = partial[-1]
        if saved is None:
            span = decay[-1]
            got = swap(jnp.stack([other_half(total), other_half(span)]), 1)
            mine, span_mine = own_half(total), own_half(span)
            value0, value1 = jnp.where(odd, got[0], mine), jnp.where(odd, mine, got[0])
            span0, span1 = jnp.where(odd, got[1], span_mine), jnp.where(odd, span_mine, got[1])
            chip, chip_span = value1 + span1 * value0, span1 * span0
            got = swap(jnp.stack([chip, chip_span]), 2)
            behind_span = jnp.where(upper, got[1], 1.0)
            keep = jnp.where(upper, 1.0, got[1])
            take = jnp.where(upper, chip_span, 1.0)
            prefix = jnp.where(upper, got[0], 0.0)
            block = keep * chip + take * got[0]
            block_span = chip_span * got[1]
            pack = jnp.stack([block, block_span])
            got3, got2, got1 = swap(pack, 12), swap(pack, 8), swap(pack, 4)
            weight1 = jnp.where(quad % 2 == 1, behind_span, 0.0)
            weight2 = behind_span * jnp.where(
                quad == 2, got3[1], jnp.where(quad == 3, got1[1], 0.0)
            )
            weight3 = behind_span * jnp.where(
                quad == 2, 1.0, jnp.where(quad == 3, got1[1] * got2[1], 0.0)
            )
            got1, got2, got3 = got1[0], got2[0], got3[0]
            saved = (span0, span1, keep, take, weight1, weight2, weight3)
        else:
            span0, span1, keep, take, weight1, weight2, weight3 = saved
            got = swap(other_half(total), 1)
            mine = own_half(total)
            value0, value1 = jnp.where(odd, got, mine), jnp.where(odd, mine, got)
            chip = value1 + span1 * value0
            got = swap(chip, 2)
            prefix = jnp.where(upper, got, 0.0)
            block = keep * chip + take * got
            got3, got2, got1 = swap(block, 12), swap(block, 8), swap(block, 4)
        into0 = prefix + weight1 * got1 + weight2 * got2 + weight3 * got3
        into1 = span0 * into0 + value0
        mine, theirs = jnp.where(odd, into1, into0), jnp.where(odd, into0, into1)
        got = swap(theirs, 1)
        incoming = jnp.concatenate([jnp.where(odd, got, mine), jnp.where(odd, mine, got)], axis=1)
        field = partial + decay * incoming
        if not last_step:
            leaving = field[-1]
            pair_from = jnp.where(odd, incoming - pair_field[HALO - 1], leaving)
            chain_from = jnp.where(odd, leaving, incoming - chain_field[HALO - 1])
            extended = jnp.concatenate(
                [
                    pair_field + pair_decay * pair_from,
                    field,
                    chain_field + chain_decay * chain_from,
                ],
                axis=0,
            )
    return field


def solution(mesh):
    return jax.shard_map(
        body,
        mesh=mesh,
        in_specs=(P("ax", "xs", None), P("ax", "xs", None), P("ax", "xs", None)),
        out_specs=P("ax", "xs", None),
        check_vma=False,
    )
```

time: 1270 us -> 123 us (0.10)
  the two profiles are of different devices: /device:TPU:128 before, /device:TPU:1 now
where the time goes in v1:
time: 123 us; the launch traced here: 121 us
  starting transfers between devices  39.6 us (32%)
  waiting for transfers between devices  27.7 us (23%)
  local copies, waits for them, and re-layouts  16.8 us (14%)
  other arithmetic  12.5 us (10%)
  blocking collectives  12 us (10%)
  matrix products  11.9 us (10%)
    ppermute x15, starting transfers between devices, swap(): return lax.ppermute(value, 'ax', [(i, i ^ mask) for i in range(count)])  32.4 us
    ppermute x15, waiting for transfers between devices, swap(): return lax.ppermute(value, 'ax', [(i, i ^ mask) for i in range(count)])  13.6 us
    all_to_all x1, blocking collectives, body(): got = lax.all_to_all(sent, 'xs', split_axis=0, concat_axis=0, tiled=True)  12 us
    unnamed x76, local copies, waits for them, and re-layouts  11.1 us
    ppermute x3, waiting for transfers between devices, chain_swap(): return lax.ppermute(value, 'ax', pairs)  8.32 us
    all_to_all x1, waiting for transfers between devices, body(): got = lax.all_to_all(sent, 'xs', split_axis=0, concat_axis=0, tiled=True)  5.74 us
    dot_general x6, matrix products, exact_dot(): jnp.dot(matrix, values, precision=lax.Precision.HIGHEST, preferred_elemen...  4.95 us
    all_to_all x1, starting transfers between devices, body(): got = lax.all_to_all(sent, 'xs', split_axis=0, concat_axis=0, tiled=True)  4.78 us
  transfers between devices with their start and end apart: 19, of which 11 were waited for; matrix products, arithmetic and copies ran while one was open for 7% of the time, Pallas kernels for 0%

profile of v1, /device:TPU:1, one launch (start us, length us, event | category | flops | bytes accessed | tf_op | source)
XLA Modules:
  0.0 121.5 jit_solution(15369933626802205053)
XLA Ops:
  0.0 1.1 slice_select_fusion.1
  1.1 3.3 %collective-permute-start = (f32[4,16,1024]{2,1,0:T(8,128)S(1)}, f32[4,16,1024]{2,1,0:T(8,128)S(1)}, u32[]{:S(2)}, u32[]{:S(2)}) collective-permute-start(f32[4,16,1024]{2,1,0:T(8,128)S(1)} %get-tuple-element.79), channel_id=1, source_target_pairs={{0,16},{16,0},{32,48},{48,32},{64,80},{80,64},{96,112},{112,96},{1... | collective-permute-start | bytes 786440 | tf_op jit(solution)/shard_map/ppermute | solution.py:125
  6.9 3.7 %collective-permute-done.1 = f32[4,16,1024]{2,1,0:T(8,128)S(1)} collective-permute-done((f32[4,16,1024]{2,1,0:T(8,128)S(1)}, f32[4,16,1024]{2,1,0:T(8,128)S(1)}, u32[]{:S(2)}, u32[]{:S(2)}) %collective-permute-start.1) | collective-permute-done | bytes 262176 | tf_op jit(solution)/shard_map/ppermute | solution.py:131
  11.3 0.9 broadcast_select_fusion.1
  12.2 4.8 %all-to-all-start = ((f32[16,8,1024]{2,1,0:T(8,128)}), f32[16,8,1024]{2,1,0:T(8,128)}, u32[]{:S(2)}, u32[]{:S(2)}) async-start(f32[16,8,1024]{2,1,0:T(8,128)} %broadcast_select_fusion.1), calls=%async_computation | async-start | bytes 1048576 | tf_op jit(solution)/shard_map/all_to_all | solution.py:206
  18.5 1.0 constant_dynamic-slice_fusion.1
  19.5 0.9 constant_dynamic-slice_fusion
  20.3 5.7 %all-to-all-done = f32[16,8,1024]{2,1,0:T(8,128)} async-done(((f32[16,8,1024]{2,1,0:T(8,128)}), f32[16,8,1024]{2,1,0:T(8,128)}, u32[]{:S(2)}, u32[]{:S(2)}) %all-to-all-start) | async-done | bytes 524320 | tf_op jit(solution)/shard_map/all_to_all | solution.py:206
  26.1 1.7 %fusion.6 = f32[128,1024]{1,0:T(8,128)S(1)} fusion(f32[128,128]{0,1:T(8,128)S(1)} %reshape.89, f32[16,8,1024]{2,1,0:T(8,128)} %all-to-all-done), kind=kOutput, calls=%fused_computation.31 | convolution fusion | flops 201326592 | bytes 1114112 | tf_op jit(solution)/shard_map/dot_general | solution.py:118
  27.8 0.7 convolution_add_fusion.5
  29.4 1.1 copy-done.3
  31.4 1.3 %copy-done.1 = bf16[1024,1024]{1,0:T(8,128)(2,1)S(1)} copy-done((bf16[1024,1024]{1,0:T(8,128)(2,1)S(1)}, bf16[1024,1024]{1,0:T(8,128)(2,1)}, u32[]{:S(2)}) %copy-start.1) | copy-done | bytes 2097176
  33.5 0.7 convolution_add_fusion.3
  34.2 0.9 copy-done.5
  35.0 0.7 convolution_add_fusion.2
  35.9 0.9 copy-done.7
  39.6 5.6 %collective-permute-start.4 = (f32[2,16,512]{2,1,0:T(8,128)S(1)}, f32[2,16,512]{2,1,0:T(8,128)S(1)}, u32[]{:S(2)}, u32[]{:S(2)}) collective-permute-start(f32[2,16,512]{2,1,0:T(8,128)S(1)} %pad_maximum_fusion.8), channel_id=1, source_target_pairs={{0,16},{16,0},{32,48},{48,32},{64,80},{80,64},{96,112},{112,96},{1... | collective-permute-start | bytes 196616 | tf_op jit(solution)/shard_map/ppermute | solution.py:125
  45.2 0.9 collective-permute-done.4
  48.2 3.3 %collective-permute-done.5 = f32[2,16,512]{2,1,0:T(8,128)} collective-permute-done((f32[2,16,512]{2,1,0:T(8,128)}, f32[2,16,512]{2,1,0:T(8,128)}, u32[]{:S(2)}, u32[]{:S(2)}) %collective-permute-start.5) | collective-permute-done | bytes 65568 | tf_op jit(solution)/shard_map/ppermute | solution.py:125
  51.6 0.8 add_bitcast_fusion
  52.4 5.1 %collective-permute-start.8 = (f32[2,16,512]{2,1,0:T(8,128)S(1)}, f32[2,16,512]{2,1,0:T(8,128)S(1)}, u32[]{:S(2)}, u32[]{:S(2)}) collective-permute-start(f32[2,16,512]{2,1,0:T(8,128)S(1)} %pad_maximum_fusion.10), channel_id=1, source_target_pairs={{0,128},{16,144},{32,160},{48,176},{64,192},{80,208},{96,224},{112... | collective-permute-start | bytes 196616 | tf_op jit(solution)/shard_map/ppermute | solution.py:125
  58.5 1.1 fusion.17
  59.5 2.1 %collective-permute-start.2 = (f32[4,16,1024]{2,1,0:T(8,128)S(1)}, f32[4,16,1024]{2,1,0:T(8,128)S(1)}, u32[]{:S(2)}, u32[]{:S(2)}) collective-permute-start(f32[4,16,1024]{2,1,0:T(8,128)S(1)} %get-tuple-element.68), channel_id=1, source_target_pairs={{0,16},{16,0},{32,48},{48,32},{64,80},{80,64},{96,112},{112,96},{1... | collective-permute-start | bytes 786440 | tf_op jit(solution)/shard_map/ppermute | solution.py:125
  61.7 1.3 %collective-permute-start.10 = (f32[4,16,1024]{2,1,0:T(8,128)S(1)}, f32[4,16,1024]{2,1,0:T(8,128)S(1)}, u32[]{:S(2)}, u32[]{:S(2)}) collective-permute-start(f32[4,16,1024]{2,1,0:T(8,128)S(1)} %get-tuple-element.69), channel_id=1, source_target_pairs={{0,240},{16,32},{32,16},{48,64},{64,48},{80,96},{96,80},{112,128},... | collective-permute-start | bytes 786440 | tf_op jit(solution)/shard_map/ppermute | solution.py:131
  63.5 0.8 broadcast_select_fusion.8
  64.4 2.5 %collective-permute-start.9 = (f32[16,512]{1,0:T(8,128)S(1)}, f32[16,512]{1,0:T(8,128)S(1)}, u32[]{:S(2)}, u32[]{:S(2)}) collective-permute-start(f32[16,512]{1,0:T(8,128)S(1)} %get-tuple-element.17), channel_id=1, source_target_pairs={{0,16},{16,0},{32,48},{48,32},{64,80},{80,64},{96,112},{112,96},{1... | collective-permute-start | bytes 98312 | tf_op jit(solution)/shard_map/ppermute | solution.py:125
  66.9 1.1 fusion.15
  68.1 1.2 collective-permute-start.11
  69.6 4.7 %collective-permute-done.11 = f32[4,16,1024]{2,1,0:T(8,128)S(1)} collective-permute-done((f32[4,16,1024]{2,1,0:T(8,128)S(1)}, f32[4,16,1024]{2,1,0:T(8,128)S(1)}, u32[]{:S(2)}, u32[]{:S(2)}) %collective-permute-start.11) | collective-permute-done | bytes 262176 | tf_op jit(solution)/shard_map/ppermute | solution.py:131
  75.3 12.0 %all_to_all.10 = f32[16,8,1024]{2,1,0:T(8,128)S(1)} all-to-all(f32[16,8,1024]{2,1,0:T(8,128)S(1)} %broadcast_select_fusion), channel_id=1, replica_groups=mesh['ax'=16,'xs'=16] {'xs'}, dimensions={0} | all-to-all | bytes 1048576 | tf_op jit(solution)/shard_map/all_to_all | solution.py:206
  88.0 0.7 convolution_add_fusion.4
  89.6 1.1 copy-done.4
  92.0 1.3 %copy-done.2 = bf16[1024,1024]{1,0:T(8,128)(2,1)S(1)} copy-done((bf16[1024,1024]{1,0:T(8,128)(2,1)S(1)}, bf16[1024,1024]{1,0:T(8,128)(2,1)}, u32[]{:S(2)}) %copy-start.2) | copy-done | bytes 2097176
  94.0 0.7 convolution_add_fusion.1
  94.7 0.9 copy-done.6
  95.6 0.7 convolution_add_fusion
  96.5 0.9 copy-done.8
  97.9 3.6 %collective-permute-start.12 = (f32[16,512]{1,0:T(8,128)S(1)}, f32[16,512]{1,0:T(8,128)S(1)}, u32[]{:S(2)}, u32[]{:S(2)}) collective-permute-start(f32[16,512]{1,0:T(8,128)S(1)} %slice_select_fusion.3), channel_id=1, source_target_pairs={{0,16},{16,0},{32,48},{48,32},{64,80},{80,64},{96,112},{112,96},{1... | collective-permute-start | bytes 98312 | tf_op jit(solution)/shard_map/ppermute | solution.py:125
  101.6 0.9 collective-permute-done.12
  103.0 2.3 %collective-permute-done.13 = f32[16,512]{1,0:T(8,128)S(1)} collective-permute-done((f32[16,512]{1,0:T(8,128)S(1)}, f32[16,512]{1,0:T(8,128)S(1)}, u32[]{:S(2)}, u32[]{:S(2)}) %collective-permute-start.13) | collective-permute-done | bytes 32800 | tf_op jit(solution)/shard_map/ppermute | solution.py:125
  105.3 0.8 multiply_add_fusion.4
  106.1 3.1 %collective-permute-start.16 = (f32[16,512]{1,0:T(8,128)S(1)}, f32[16,512]{1,0:T(8,128)S(1)}, u32[]{:S(2)}, u32[]{:S(2)}) collective-permute-start(f32[16,512]{1,0:T(8,128)S(1)} %multiply_add_fusion.4), channel_id=1, source_target_pairs={{0,192},{16,208},{32,224},{48,240},{64,128},{80,144},{96,160},{112... | collective-permute-start | bytes 98312 | tf_op jit(solution)/shard_map/ppermute | solution.py:125
  109.2 2.4 %collective-permute-start.15 = (f32[16,512]{1,0:T(8,128)S(1)}, f32[16,512]{1,0:T(8,128)S(1)}, u32[]{:S(2)}, u32[]{:S(2)}) collective-permute-start(f32[16,512]{1,0:T(8,128)S(1)} %multiply_add_fusion.4), channel_id=1, source_target_pairs={{0,128},{16,144},{32,160},{48,176},{64,192},{80,208},{96,224},{112... | collective-permute-start | bytes 98312 | tf_op jit(solution)/shard_map/ppermute | solution.py:125
  111.8 4.5 %collective-permute-done.15 = f32[16,512]{1,0:T(8,128)S(1)} collective-permute-done((f32[16,512]{1,0:T(8,128)S(1)}, f32[16,512]{1,0:T(8,128)S(1)}, u32[]{:S(2)}, u32[]{:S(2)}) %collective-permute-start.15) | collective-permute-done | bytes 32800 | tf_op jit(solution)/shard_map/ppermute | solution.py:125
  116.3 0.8 fusion.40
  117.1 2.6 %collective-permute-start.17 = (f32[16,512]{1,0:T(8,128)S(1)}, f32[16,512]{1,0:T(8,128)S(1)}, u32[]{:S(2)}, u32[]{:S(2)}) collective-permute-start(f32[16,512]{1,0:T(8,128)S(1)} %get-tuple-element.7), channel_id=1, source_target_pairs={{0,16},{16,0},{32,48},{48,32},{64,80},{80,64},{96,112},{112,96},{1... | collective-permute-start | bytes 98312 | tf_op jit(solution)/shard_map/ppermute | solution.py:125
  119.7 0.9 collective-permute-done.17
  120.6 0.9 multiply_add_fusion
  (167 shorter events, 19.4 us)
Async XLA Ops:
  0.0 10.6 %copy-start.11 = (f32[8,16,1024]{2,1,0:T(8,128)S(1)}, f32[8,16,1024]{2,1,0:T(8,128)}, u32[]{:S(2)}) copy-start(f32[8,16,1024]{2,1,0:T(8,128)} %param.13) | copy-start | bytes 1572868
  1.1 5.7 %collective-permute-start = (f32[4,16,1024]{2,1,0:T(8,128)S(1)}, f32[4,16,1024]{2,1,0:T(8,128)S(1)}, u32[]{:S(2)}, u32[]{:S(2)}) collective-permute-start(f32[4,16,1024]{2,1,0:T(8,128)S(1)} %get-tuple-element.79), channel_id=1, source_target_pairs={{0,16},{16,0},{32,48},{48,32},{64,80},{80,64},{96,112},{112,96},{1... | collective-permute-start | bytes 786440 | tf_op jit(solution)/shard_map/ppermute | solution.py:125
  4.5 6.1 %collective-permute-start.1 = (f32[4,16,1024]{2,1,0:T(8,128)S(1)}, f32[4,16,1024]{2,1,0:T(8,128)S(1)}, u32[]{:S(2)}, u32[]{:S(2)}) collective-permute-start(f32[4,16,1024]{2,1,0:T(8,128)S(1)} %get-tuple-element.80), channel_id=1, source_target_pairs={{0,240},{16,32},{32,16},{48,64},{64,48},{80,96},{96,80},{112,128},... | collective-permute-start | bytes 786440 | tf_op jit(solution)/shard_map/ppermute | solution.py:131
  6.6 5.6 %copy-start.35 = (pred[16]{0:T(512)(128)(4,1)}, pred[16]{0:T(512)(128)(4,1)S(1)}, u32[]{:S(2)}) copy-start(pred[16]{0:T(512)(128)(4,1)S(1)} %iota_compare_fusion.1) | copy-start | bytes 52
  12.2 13.9 %all-to-all-start = ((f32[16,8,1024]{2,1,0:T(8,128)}), f32[16,8,1024]{2,1,0:T(8,128)}, u32[]{:S(2)}, u32[]{:S(2)}) async-start(f32[16,8,1024]{2,1,0:T(8,128)} %broadcast_select_fusion.1), calls=%async_computation | async-start | bytes 1048576 | tf_op jit(solution)/shard_map/all_to_all | solution.py:206
  18.5 10.0 %copy-start = (bf16[1024,1024]{1,0:T(8,128)(2,1)S(1)}, bf16[1024,1024]{1,0:T(8,128)(2,1)}, u32[]{:S(2)}) copy-start(bf16[1024,1024]{1,0:T(8,128)(2,1)} %constant.103.clone) | copy-start | bytes 6291460
  19.5 11.6 %copy-start.14 = (f32[16,1024]{1,0:T(8,128)}, f32[16,1024]{1,0:T(8,128)S(1)}, u32[]{:S(2)}) copy-start(f32[16,1024]{1,0:T(8,128)S(1)} %constant_dynamic-slice_fusion.1) | copy-start | bytes 196612
  28.9 1.6 %copy-start.3 = (bf16[1024,1024]{1,0:T(8,128)(2,1)S(1)}, bf16[1024,1024]{1,0:T(8,128)(2,1)}, u32[]{:S(2)}) copy-start(bf16[1024,1024]{1,0:T(8,128)(2,1)} %constant.104.clone) | copy-start | bytes 6291460
  31.1 1.6 %copy-start.1 = (bf16[1024,1024]{1,0:T(8,128)(2,1)S(1)}, bf16[1024,1024]{1,0:T(8,128)(2,1)}, u32[]{:S(2)}) copy-start(bf16[1024,1024]{1,0:T(8,128)(2,1)} %constant.105.clone) | copy-start | bytes 6291460
  33.4 1.6 %copy-start.5 = (bf16[1024,1024]{1,0:T(8,128)(2,1)S(1)}, bf16[1024,1024]{1,0:T(8,128)(2,1)}, u32[]{:S(2)}) copy-start(bf16[1024,1024]{1,0:T(8,128)(2,1)} %constant.106.clone) | copy-start | bytes 6291460
  35.8 1.0 copy-start.7
  35.8 1.2 copy-start.9
  37.4 1.4 %copy-start.21 = (f32[1,16,1024]{2,1,0:T(8,128)}, f32[1,16,1024]{2,1,0:T(8,128)S(1)}, u32[]{:S(2)}) copy-start(f32[1,16,1024]{2,1,0:T(8,128)S(1)} %get-tuple-element.43) | copy-start | bytes 196612
  38.7 0.8 copy-start.12
  38.7 0.8 copy-start.22
  38.7 0.8 copy-start.23
  38.8 0.8 copy-start.24
  38.8 0.7 copy-start.25
  39.6 6.5 %collective-permute-start.4 = (f32[2,16,512]{2,1,0:T(8,128)S(1)}, f32[2,16,512]{2,1,0:T(8,128)S(1)}, u32[]{:S(2)}, u32[]{:S(2)}) collective-permute-start(f32[2,16,512]{2,1,0:T(8,128)S(1)} %pad_maximum_fusion.8), channel_id=1, source_target_pairs={{0,16},{16,0},{32,48},{48,32},{64,80},{80,64},{96,112},{112,96},{1... | collective-permute-start | bytes 196616 | tf_op jit(solution)/shard_map/ppermute | solution.py:125
  46.1 1.9 %copy-start.34 = (f32[2,16,512]{2,1,0:T(8,128)}, f32[2,16,512]{2,1,0:T(8,128)S(1)}, u32[]{:S(2)}) copy-start(f32[2,16,512]{2,1,0:T(8,128)S(1)} %collective-permute-done.4) | copy-start | bytes 196612
  46.2 1.9 %copy-start.31 = (f32[16,512]{1,0:T(8,128)}, f32[16,512]{1,0:T(8,128)S(1)}, u32[]{:S(2)}) copy-start(f32[16,512]{1,0:T(8,128)S(1)} %get-tuple-element.23) | copy-start | bytes 98308
  46.2 1.9 %copy-start.33 = (f32[16,512]{1,0:T(8,128)}, f32[16,512]{1,0:T(8,128)S(1)}, u32[]{:S(2)}) copy-start(f32[16,512]{1,0:T(8,128)S(1)} %get-tuple-element.22) | copy-start | bytes 98308
  48.0 3.5 %collective-permute-start.5 = (f32[2,16,512]{2,1,0:T(8,128)}, f32[2,16,512]{2,1,0:T(8,128)}, u32[]{:S(2)}, u32[]{:S(2)}) collective-permute-start(f32[2,16,512]{2,1,0:T(8,128)} %pad_maximum_fusion.9), channel_id=1, source_target_pairs={{0,32},{16,48},{32,0},{48,16},{64,96},{80,112},{96,64},{112,80},{1... | collective-permute-start | bytes 196616 | tf_op jit(solution)/shard_map/ppermute | solution.py:125
  48.2 21.1 %copy-start.13 = (f32[8,16,1024]{2,1,0:T(8,128)S(1)}, f32[8,16,1024]{2,1,0:T(8,128)}, u32[]{:S(2)}) copy-start(f32[8,16,1024]{2,1,0:T(8,128)} %copy-done.12) | copy-start | bytes 1572868
  52.4 10.6 %collective-permute-start.8 = (f32[2,16,512]{2,1,0:T(8,128)S(1)}, f32[2,16,512]{2,1,0:T(8,128)S(1)}, u32[]{:S(2)}, u32[]{:S(2)}) collective-permute-start(f32[2,16,512]{2,1,0:T(8,128)S(1)} %pad_maximum_fusion.10), channel_id=1, source_target_pairs={{0,128},{16,144},{32,160},{48,176},{64,192},{80,208},{96,224},{112... | collective-permute-start | bytes 196616 | tf_op jit(solution)/shard_map/ppermute | solution.py:125
  57.5 5.4 %collective-permute-start.7 = (f32[2,16,512]{2,1,0:T(8,128)S(1)}, f32[2,16,512]{2,1,0:T(8,128)S(1)}, u32[]{:S(2)}, u32[]{:S(2)}) collective-permute-start(f32[2,16,512]{2,1,0:T(8,128)S(1)} %pad_maximum_fusion.10), channel_id=1, source_target_pairs={{0,192},{16,208},{32,224},{48,240},{64,128},{80,144},{96,160},{112... | collective-permute-start | bytes 196616 | tf_op jit(solution)/shard_map/ppermute | solution.py:125
  58.0 5.6 %collective-permute-start.6 = (f32[2,16,512]{2,1,0:T(8,128)S(1)}, f32[2,16,512]{2,1,0:T(8,128)S(1)}, u32[]{:S(2)}, u32[]{:S(2)}) collective-permute-start(f32[2,16,512]{2,1,0:T(8,128)S(1)} %pad_maximum_fusion.10), channel_id=1, source_target_pairs={{0,64},{16,80},{32,96},{48,112},{64,0},{80,16},{96,32},{112,48},{1... | collective-permute-start | bytes 196616 | tf_op jit(solution)/shard_map/ppermute | solution.py:125
  59.5 14.7 %collective-permute-start.2 = (f32[4,16,1024]{2,1,0:T(8,128)S(1)}, f32[4,16,1024]{2,1,0:T(8,128)S(1)}, u32[]{:S(2)}, u32[]{:S(2)}) collective-permute-start(f32[4,16,1024]{2,1,0:T(8,128)S(1)} %get-tuple-element.68), channel_id=1, source_target_pairs={{0,16},{16,0},{32,48},{48,32},{64,80},{80,64},{96,112},{112,96},{1... | collective-permute-start | bytes 786440 | tf_op jit(solution)/shard_map/ppermute | solution.py:125
  61.7 12.6 %collective-permute-start.10 = (f32[4,16,1024]{2,1,0:T(8,128)S(1)}, f32[4,16,1024]{2,1,0:T(8,128)S(1)}, u32[]{:S(2)}, u32[]{:S(2)}) collective-permute-start(f32[4,16,1024]{2,1,0:T(8,128)S(1)} %get-tuple-element.69), channel_id=1, source_target_pairs={{0,240},{16,32},{32,16},{48,64},{64,48},{80,96},{96,80},{112,128},... | collective-permute-start | bytes 786440 | tf_op jit(solution)/shard_map/ppermute | solution.py:131
  64.4 4.9 %collective-permute-start.9 = (f32[16,512]{1,0:T(8,128)S(1)}, f32[16,512]{1,0:T(8,128)S(1)}, u32[]{:S(2)}, u32[]{:S(2)}) collective-permute-start(f32[16,512]{1,0:T(8,128)S(1)} %get-tuple-element.17), channel_id=1, source_target_pairs={{0,16},{16,0},{32,48},{48,32},{64,80},{80,64},{96,112},{112,96},{1... | collective-permute-start | bytes 98312 | tf_op jit(solution)/shard_map/ppermute | solution.py:125
  68.0 1.6 %collective-permute-start.3 = (f32[4,16,1024]{2,1,0:T(8,128)S(1)}, f32[4,16,1024]{2,1,0:T(8,128)S(1)}, u32[]{:S(2)}, u32[]{:S(2)}) collective-permute-start(f32[4,16,1024]{2,1,0:T(8,128)S(1)} %get-tuple-element.66), channel_id=1, source_target_pairs={{0,16},{16,0},{32,48},{48,32},{64,80},{80,64},{96,112},{112,96},{1... | collective-permute-start | bytes 786440 | tf_op jit(solution)/shard_map/ppermute | solution.py:125
  68.1 6.2 %collective-permute-start.11 = (f32[4,16,1024]{2,1,0:T(8,128)S(1)}, f32[4,16,1024]{2,1,0:T(8,128)S(1)}, u32[]{:S(2)}, u32[]{:S(2)}) collective-permute-start(f32[4,16,1024]{2,1,0:T(8,128)S(1)} %get-tuple-element.67), channel_id=1, source_target_pairs={{0,240},{16,32},{32,16},{48,64},{64,48},{80,96},{96,80},{112,128},... | collective-permute-start | bytes 786440 | tf_op jit(solution)/shard_map/ppermute | solution.py:131
  74.4 0.8 copy-start.36
  89.1 1.6 %copy-start.4 = (bf16[1024,1024]{1,0:T(8,128)(2,1)S(1)}, bf16[1024,1024]{1,0:T(8,128)(2,1)}, u32[]{:S(2)}) copy-start(bf16[1024,1024]{1,0:T(8,128)(2,1)} %constant.104.clone) | copy-start | bytes 6291460
  90.7 0.8 copy-start.15
  91.7 1.6 %copy-start.2 = (bf16[1024,1024]{1,0:T(8,128)(2,1)S(1)}, bf16[1024,1024]{1,0:T(8,128)(2,1)}, u32[]{:S(2)}) copy-start(bf16[1024,1024]{1,0:T(8,128)(2,1)} %constant.105.clone) | copy-start | bytes 6291460
  94.0 1.6 %copy-start.6 = (bf16[1024,1024]{1,0:T(8,128)(2,1)S(1)}, bf16[1024,1024]{1,0:T(8,128)(2,1)}, u32[]{:S(2)}) copy-start(bf16[1024,1024]{1,0:T(8,128)(2,1)} %constant.106.clone) | copy-start | bytes 6291460
  96.3 1.0 copy-start.8
  96.3 1.2 copy-start.10
  97.5 4.9 %copy-start.32 = (f32[16,512]{1,0:T(8,128)S(1)}, f32[16,512]{1,0:T(8,128)}, u32[]{:S(2)}) copy-start(f32[16,512]{1,0:T(8,128)} %copy-done.31) | copy-start | bytes 98308
  97.7 7.6 %copy-start.29 = (f32[16,512]{1,0:T(8,128)S(1)}, f32[16,512]{1,0:T(8,128)}, u32[]{:S(2)}) copy-start(f32[16,512]{1,0:T(8,128)} %copy-done.28) | copy-start | bytes 98308
  97.7 18.6 %copy-start.30 = (f32[16,512]{1,0:T(8,128)S(1)}, f32[16,512]{1,0:T(8,128)}, u32[]{:S(2)}) copy-start(f32[16,512]{1,0:T(8,128)} %get-tuple-element.25) | copy-start | bytes 98308
  97.9 4.5 %collective-permute-start.12 = (f32[16,512]{1,0:T(8,128)S(1)}, f32[16,512]{1,0:T(8,128)S(1)}, u32[]{:S(2)}, u32[]{:S(2)}) collective-permute-start(f32[16,512]{1,0:T(8,128)S(1)} %slice_select_fusion.3), channel_id=1, source_target_pairs={{0,16},{16,0},{32,48},{48,32},{64,80},{80,64},{96,112},{112,96},{1... | collective-permute-start | bytes 98312 | tf_op jit(solution)/shard_map/ppermute | solution.py:125
  102.4 2.9 %collective-permute-start.13 = (f32[16,512]{1,0:T(8,128)S(1)}, f32[16,512]{1,0:T(8,128)S(1)}, u32[]{:S(2)}, u32[]{:S(2)}) collective-permute-start(f32[16,512]{1,0:T(8,128)S(1)} %multiply_add_fusion.5), channel_id=1, source_target_pairs={{0,32},{16,48},{32,0},{48,16},{64,96},{80,112},{96,64},{112,80},{1... | collective-permute-start | bytes 98312 | tf_op jit(solution)/shard_map/ppermute | solution.py:125
  106.1 5.7 %collective-permute-start.16 = (f32[16,512]{1,0:T(8,128)S(1)}, f32[16,512]{1,0:T(8,128)S(1)}, u32[]{:S(2)}, u32[]{:S(2)}) collective-permute-start(f32[16,512]{1,0:T(8,128)S(1)} %multiply_add_fusion.4), channel_id=1, source_target_pairs={{0,192},{16,208},{32,224},{48,240},{64,128},{80,144},{96,160},{112... | collective-permute-start | bytes 98312 | tf_op jit(solution)/shard_map/ppermute | solution.py:125
  109.2 7.2 %collective-permute-start.15 = (f32[16,512]{1,0:T(8,128)S(1)}, f32[16,512]{1,0:T(8,128)S(1)}, u32[]{:S(2)}, u32[]{:S(2)}) collective-permute-start(f32[16,512]{1,0:T(8,128)S(1)} %multiply_add_fusion.4), channel_id=1, source_target_pairs={{0,128},{16,144},{32,160},{48,176},{64,192},{80,208},{96,224},{112... | collective-permute-start | bytes 98312 | tf_op jit(solution)/shard_map/ppermute | solution.py:125
  111.6 4.8 %collective-permute-start.14 = (f32[16,512]{1,0:T(8,128)S(1)}, f32[16,512]{1,0:T(8,128)S(1)}, u32[]{:S(2)}, u32[]{:S(2)}) collective-permute-start(f32[16,512]{1,0:T(8,128)S(1)} %multiply_add_fusion.4), channel_id=1, source_target_pairs={{0,64},{16,80},{32,96},{48,112},{64,0},{80,16},{96,32},{112,48},{1... | collective-permute-start | bytes 98312 | tf_op jit(solution)/shard_map/ppermute | solution.py:125
  117.1 3.4 %collective-permute-start.17 = (f32[16,512]{1,0:T(8,128)S(1)}, f32[16,512]{1,0:T(8,128)S(1)}, u32[]{:S(2)}, u32[]{:S(2)}) collective-permute-start(f32[16,512]{1,0:T(8,128)S(1)} %get-tuple-element.7), channel_id=1, source_target_pairs={{0,16},{16,0},{32,48},{48,32},{64,80},{80,64},{96,112},{112,96},{1... | collective-permute-start | bytes 98312 | tf_op jit(solution)/shard_map/ppermute | solution.py:125
  (8 other events, 5.2 us)

commit v2 on v0

v2 whole, which is shorter than its diff:
```python
import math

import jax
import jax.numpy as jnp
import ml_dtypes
import numpy as np
from jax import lax
from jax.experimental import pallas as pl
from jax.experimental.pallas import tpu as pltpu
from jax.sharding import PartitionSpec as P

CZ = 8
SUBSTEPS = 2
AXIAL_WEIGHT = 0.2
AZIMUTH_DAMP = 0.5
DIFFUSION = 1.0
STENCIL = (
    -1.0 / 560.0,
    8.0 / 315.0,
    -0.2,
    1.6,
    -205.0 / 72.0,
    1.6,
    -0.2,
    8.0 / 315.0,
    -1.0 / 560.0,
)
HALO = 4


def split_bf16(table):
    high = table.astype(ml_dtypes.bfloat16)
    low = (table - high.astype(np.float64)).astype(ml_dtypes.bfloat16)
    return high, low


def radial_tables(cells, groups, planes):
    rows = cells // groups
    index = np.arange(cells, dtype=np.float64)
    radius = index + 0.5
    upper = np.where(index < cells - 1, index + 1.0, 0.0)
    sub = -DIFFUSION * index / radius
    sup = -DIFFUSION * upper / radius
    matrix = np.diag(1.0 - sub - sup) + np.diag(sub[1:], -1) + np.diag(sup[:-1], 1)
    green = np.linalg.inv(matrix)
    diag = np.diag(green)
    down = np.diag(green, -1) / diag[:-1]
    up = np.diag(green, 1) / diag[1:]
    same = np.eye(planes)
    lines = planes * rows
    out = np.zeros((groups, lines + 2 * planes, lines + groups * planes), np.float32)
    for g in range(groups):
        first, last = g * rows, g * rows + rows - 1
        block = green[first : last + 1, first : last + 1]
        join = np.zeros((rows, groups))
        for i in range(rows):
            for source in range(groups):
                if source < g:
                    join[i, source] = np.prod(down[source * rows + rows - 1 : first + i])
                elif source > g:
                    join[i, source] = np.prod(up[first + i : source * rows])
        out[g, :lines, :lines] = np.kron(same, block)
        out[g, :lines, lines:] = np.einsum("zy,is->zisy", same, join).reshape(lines, -1)
        out[g, lines : lines + planes, :lines] = np.kron(same, block[-1:])
        out[g, lines + planes :, :lines] = np.kron(same, block[:1])
    return out


def azimuth_tables(points):
    half = points // 2
    quarter = half // 2
    grid = np.arange(half)
    out = []
    for parity in range(2):
        wave = 2 * np.arange(quarter) + parity
        angle = ((grid[:, None] * wave[None, :]) % points) * (2.0 * math.pi / points)
        cosine, sine = np.cos(angle), np.sin(angle)
        if parity == 0:
            sine[:, 0] = np.where(grid % 2 == 0, 1.0, -1.0)
        out.append(np.concatenate([cosine, sine], axis=1))
    return out


def filter_tables(cells, points):
    half = points // 2
    quarter = half // 2
    radius = np.arange(cells) + 0.5
    out = []
    for parity in range(2):
        wave = np.tile(2.0 * np.arange(quarter) + parity, 2)
        rate = wave * (2.0 * math.pi / points)
        weight = np.full(half, 2.0 / points)
        sign = np.repeat([1.0, -1.0], quarter)
        if parity == 0:
            wave[quarter] = half
            weight[0] = weight[quarter] = 1.0 / points
        damp = 1.0 / (1.0 + AZIMUTH_DAMP * wave[None, :] ** 2 / radius[:, None] ** 2)
        out.append((damp * weight, damp * (sign * rate * (2.0 / points))))
    table = [out[0][0], out[1][0], out[0][1], out[1][1]]
    return np.concatenate(table, axis=1).astype(np.float32)


def swap(value, mask):
    count = lax.axis_size("ax")
    return lax.ppermute(value, "ax", [(i, i ^ mask) for i in range(count)])


def chain_swap(value):
    count = lax.axis_size("ax")
    pairs = [(i, (i + 1) % count if i % 2 else (i - 1) % count) for i in range(count)]
    return lax.ppermute(value, "ax", pairs)


def split(values):
    coarse = values.astype(jnp.bfloat16)
    return coarse, (values - coarse.astype(jnp.float32)).astype(jnp.bfloat16)


def split_dot(left, right):
    dot = lambda x, y: jnp.dot(x, y, preferred_element_type=jnp.float32)
    return dot(left[0], right[0]) + (dot(left[1], right[0]) + dot(left[0], right[1]))


def carry_kernel(field, pair, chain, edges, explicit, sent):
    planes, rows, points = field.shape
    groups = sent.shape[0]
    place = lax.axis_index("ax")
    group = lax.axis_index("xs")
    odd = place % 2 == 1
    low_scale = jnp.where(place > 0, 1.0, 0.0)
    high_scale = jnp.where(place < lax.axis_size("ax") - 1, 1.0, 0.0)
    quarter = points // 4
    for part in range(4):
        where = slice(part * quarter, (part + 1) * quarter)
        low = [jnp.where(odd, pair[j, :, where], chain[j, :, where]) for j in range(HALO)]
        high = [jnp.where(odd, chain[j, :, where], pair[j, :, where]) for j in range(HALO)]
        every = [low_scale * value for value in low]
        every += [field[plane, :, where] for plane in range(planes)]
        every += [high_scale * value for value in high]
        for plane in range(planes):
            value = (1.0 + AXIAL_WEIGHT * STENCIL[HALO]) * every[plane + HALO]
            for step in range(1, HALO + 1):
                both = every[plane + HALO - step] + every[plane + HALO + step]
                value = value + (AXIAL_WEIGHT * STENCIL[HALO + step]) * both
            explicit[plane, :, where] = value
    lines = explicit[...].reshape(planes * rows, points)
    carry = split_dot(split(edges[...]), split(lines))
    for target in range(groups):
        sent[target] = jnp.where(target > group, carry[:planes], carry[planes:])


def middle_kernel(
    explicit,
    got,
    matrix,
    forward,
    inverse,
    filters,
    axial_rate,
    swirl_rate,
    partial,
    decay,
    mine,
    other,
):
    planes, rows, points = partial.shape
    half = points // 2
    quarter = half // 2
    lines = planes * rows
    known = jnp.concatenate([explicit[...].reshape(lines, points), got[...]], axis=0)
    solved = split_dot(split(matrix[...]), split(known))
    sides = (solved[:, :half] + solved[:, half:], solved[:, :half] - solved[:, half:])
    periods = []
    for parity in range(2):
        table = (forward[parity, 0], forward[parity, 1])
        spectrum = split_dot(split(sides[parity]), table).reshape(planes, rows, half)
        swapped = jnp.concatenate([spectrum[..., quarter:], spectrum[..., :quarter]], axis=-1)
        smooth = spectrum * filters[:, parity * half : (parity + 1) * half]
        slope = swapped * filters[:, points + parity * half : points + (parity + 1) * half]
        both = jnp.concatenate([smooth, slope], axis=0).reshape(2 * planes * rows, half)
        table = (inverse[parity, 0], inverse[parity, 1])
        periods.append(split_dot(split(both), table).reshape(2, planes, rows, half))
    for side in range(2):
        where = slice(side * half, (side + 1) * half)
        value = fade = None
        for plane in range(planes):
            even, odd = periods[0][:, plane], periods[1][:, plane]
            both = even + odd if side == 0 else even - odd
            courant = CZ * axial_rate[plane, :, where]
            inverse_rate = 1.0 / (1.0 + courant)
            factor = courant * inverse_rate
            scaled = inverse_rate * (both[0] - swirl_rate[plane, :, where] * both[1])
            value = scaled if plane == 0 else factor * value + scaled
            fade = factor if plane == 0 else factor * fade
            partial[plane, :, where] = value
            decay[plane, :, where] = fade
        is_mine = lax.axis_index("ax") % 2 == side
        for index, last in enumerate((value, fade)[: mine.shape[0]]):

            @pl.when(is_mine)
            def _():
                mine[index] = last

            @pl.when(jnp.logical_not(is_mine))
            def _():
                other[index] = last


def ends_kernel(field, pair, chain):
    planes = field.shape[0]
    odd = lax.axis_index("ax") % 2 == 1
    for j in range(HALO):
        low, high = field[j], field[planes - HALO + j]
        pair[j] = jnp.where(odd, low, high)
        chain[j] = jnp.where(odd, high, low)


def chip_kernel(mine, got, *refs):
    odd = lax.axis_index("ax") % 2 == 1
    value0, value1 = jnp.where(odd, got[0], mine[0]), jnp.where(odd, mine[0], got[0])
    if mine.shape[0] == 2:
        block, behind, spans = refs
        span0, span1 = jnp.where(odd, got[1], mine[1]), jnp.where(odd, mine[1], got[1])
        block[1] = span0 * span1
        spans[0], spans[1] = span0, span1
    else:
        spans, block, behind = refs
        span1 = spans[1]
    block[0] = value1 + span1 * value0
    behind[...] = value0


def couple_kernel(block, got, *refs):
    upper = (lax.axis_index("ax") // 2) % 2 == 1
    if block.shape[0] == 2:
        joint, prefix, gains = refs
        joint[1] = block[1] * got[1]
        gains[0] = jnp.where(upper, 1.0, got[1])
        gains[1] = jnp.where(upper, block[1], 1.0)
        gains[2] = jnp.where(upper, got[1], 1.0)
    else:
        gains, joint, prefix = refs
    joint[0] = gains[0] * block[0] + gains[1] * got[0]
    prefix[...] = jnp.where(upper, got[0], 0.0)


def enter_kernel(got1, got2, got3, prefix, behind, spans, gains, *refs):
    place = lax.axis_index("ax")
    odd = place % 2 == 1
    quad = place // 4
    if got1.shape[0] == 2:
        mine, other, weights = refs
        before = gains[2]
        weights[0] = jnp.where(quad % 2 == 1, before, 0.0)
        weights[1] = before * jnp.where(quad == 2, got3[1], jnp.where(quad == 3, got1[1], 0.0))
        weights[2] = before * jnp.where(
            quad == 2, 1.0, jnp.where(quad == 3, got1[1] * got2[1], 0.0)
        )
    else:
        weights, mine, other = refs
    into0 = prefix[...] + weights[0] * got1[0] + weights[1] * got2[0] + weights[2] * got3[0]
    into1 = spans[0] * into0 + behind[...]
    mine[...] = jnp.where(odd, into1, into0)
    other[...] = jnp.where(odd, into0, into1)


def finish_kernel(partial, decay, mine, got, field, pair, chain):
    planes, rows, points = partial.shape
    half = points // 2
    odd = lax.axis_index("ax") % 2 == 1
    for side in range(2):
        where = slice(side * half, (side + 1) * half)
        incoming = jnp.where(odd == (side == 1), mine[...], got[...])
        ends = {}
        for plane in range(planes):
            value = partial[plane, :, where] + decay[plane, :, where] * incoming
            field[plane, :, where] = value
            ends[plane] = value
        for j in range(HALO):
            low, high = ends[j], ends[planes - HALO + j]
            pair[j, :, where] = jnp.where(odd, low, high)
            chain[j, :, where] = jnp.where(odd, high, low)


def call(kernel, out_shape, *args, vmem=4):
    return pl.pallas_call(
        kernel,
        out_shape=out_shape,
        in_specs=[pl.BlockSpec(memory_space=pltpu.VMEM)] * len(args),
        out_specs=jax.tree.map(lambda _: pl.BlockSpec(memory_space=pltpu.VMEM), out_shape),
        compiler_params=pltpu.CompilerParams(vmem_limit_bytes=vmem * 1024 * 1024),
    )(*args)


def body(scalar, axial_rate, swirl_rate):
    planes, rows, points = scalar.shape
    half = points // 2
    groups = lax.axis_size("xs")
    group = lax.axis_index("xs")
    place = lax.axis_index("ax")
    odd = place % 2 == 1
    lines = planes * rows
    tables = azimuth_tables(points)
    forward = jnp.asarray(np.stack([np.stack(split_bf16(t)) for t in tables]))
    inverse = jnp.asarray(np.stack([np.stack(split_bf16(t.T)) for t in tables]))
    radial = lax.dynamic_index_in_dim(
        jnp.asarray(radial_tables(rows * groups, groups, planes)), group, 0, keepdims=False
    )
    matrix, edges = radial[:lines], radial[lines:, :lines]
    filters = lax.dynamic_slice_in_dim(
        jnp.asarray(filter_tables(rows * groups, points)), group * rows, rows, 0
    )
    block = jax.ShapeDtypeStruct((planes, rows, points), jnp.float32)

    ends = jax.ShapeDtypeStruct((HALO, rows, points), jnp.float32)

    def halves(count):
        return jax.ShapeDtypeStruct((count, rows, half), jnp.float32)

    plane_half = jax.ShapeDtypeStruct((rows, half), jnp.float32)

    field = scalar
    pair_end, chain_end = call(ends_kernel, (ends, ends), scalar)
    saved = None
    for substep in range(SUBSTEPS):
        chain, pair = chain_swap(chain_end), swap(pair_end, 1)
        explicit, sent = call(
            carry_kernel,
            (block, jax.ShapeDtypeStruct((groups, planes, points), jnp.float32)),
            field,
            pair,
            chain,
            edges,
        )
        got = lax.all_to_all(sent, "xs", split_axis=0, concat_axis=0, tiled=True)
        first = saved is None
        parts = 2 if first else 1
        partial, decay, mine, other = call(
            middle_kernel,
            (block, block, halves(parts), halves(parts)),
            explicit,
            got.reshape(groups * planes, points),
            matrix,
            forward,
            inverse,
            filters,
            axial_rate,
            swirl_rate,
            vmem=16,
        )
        got = swap(other, 1)
        if first:
            value, behind, spans = call(
                chip_kernel, (halves(2), plane_half, halves(2)), mine, got
            )
        else:
            value, behind = call(chip_kernel, (halves(1), plane_half), mine, got, spans)
        got = swap(value, 2)
        if first:
            value, prefix, gains = call(
                couple_kernel, (halves(2), plane_half, halves(3)), value, got
            )
        else:
            value, prefix = call(couple_kernel, (halves(1), plane_half), value, got, gains)
        got3, got2, got1 = swap(value, 12), swap(value, 8), swap(value, 4)
        args = (got1, got2, got3, prefix, behind, spans, gains)
        if first:
            mine, other, saved = call(enter_kernel, (plane_half, plane_half, halves(3)), *args)
        else:
            mine, other = call(enter_kernel, (plane_half, plane_half), *args, saved)
        got = swap(other, 1)
        if substep < SUBSTEPS - 1:
            field, pair_end, chain_end = call(
                finish_kernel, (block, ends, ends), partial, decay, mine, got
            )
        else:
            incoming = jnp.concatenate(
                [jnp.where(odd, got, mine), jnp.where(odd, mine, got)], axis=1
            )
            field = partial + decay * incoming
    return field


def solution(mesh):
    return jax.shard_map(
        body,
        mesh=mesh,
        in_specs=(P("ax", "xs", None), P("ax", "xs", None), P("ax", "xs", None)),
        out_specs=P("ax", "xs", None),
        check_vma=False,
    )
```

time: 1270 us -> 106 us (0.08)
  the two profiles are of different devices: /device:TPU:128 before, /device:TPU:1 now
where the time goes in v2:
time: 106 us; the launch traced here: 105 us
  waiting for transfers between devices  38.1 us (36%)
  starting transfers between devices  33.5 us (32%)
  blocking collectives  12.8 us (12%)
  local copies, waits for them, and re-layouts  10 us (9%)
  Pallas kernels  8.47 us (8%)
  other arithmetic  2.09 us (2%)
    ppermute x14, starting transfers between devices, swap(): return lax.ppermute(value, 'ax', [(i, i ^ mask) for i in range(count)])  28 us
    ppermute x14, waiting for transfers between devices, swap(): return lax.ppermute(value, 'ax', [(i, i ^ mask) for i in range(count)])  20.9 us
    all_to_all x1, blocking collectives, body(): got = lax.all_to_all(sent, 'xs', split_axis=0, concat_axis=0, tiled=True)  12.8 us
    ppermute x2, waiting for transfers between devices, chain_swap(): return lax.ppermute(value, 'ax', pairs)  9.94 us
    pallas_call x12, Pallas kernels, call(): pl.pallas_call(kernel, out_shape=out_shape, in_specs=[pl.BlockSpec(memory...  8.47 us
    unnamed x22, local copies, waits for them, and re-layouts  7.25 us
    all_to_all x1, waiting for transfers between devices, body(): got = lax.all_to_all(sent, 'xs', split_axis=0, concat_axis=0, tiled=True)  7.25 us
    all_to_all x1, starting transfers between devices, body(): got = lax.all_to_all(sent, 'xs', split_axis=0, concat_axis=0, tiled=True)  4.78 us
  transfers between devices with their start and end apart: 17, of which 14 were waited for; matrix products, arithmetic and copies ran while one was open for 3% of the time, Pallas kernels for 0%

profile of v2, /device:TPU:1, one launch (start us, length us, event | category | flops | bytes accessed | tf_op | source)
XLA Modules:
  0.0 105.1 jit_solution(6919575994253505967)
XLA Ops:
  0.0 1.2 %copy-done.4 = f32[8,16,1024]{2,1,0:T(8,128)S(1)} copy-done((f32[8,16,1024]{2,1,0:T(8,128)S(1)}, f32[8,16,1024]{2,1,0:T(8,128)}, u32[]{:S(2)}) %copy-start.4) | copy-done | bytes 524312
  1.2 0.8 shard_map.73
  2.0 3.2 %collective-permute-start = (f32[4,16,1024]{2,1,0:T(8,128)}, f32[4,16,1024]{2,1,0:T(8,128)S(1)}, u32[]{:S(2)}, u32[]{:S(2)}) collective-permute-start(f32[4,16,1024]{2,1,0:T(8,128)} %get-tuple-element.37), channel_id=1, source_target_pairs={{0,16},{16,0},{32,48},{48,32},{64,80},{80,64},{96,112},{112,96},{1... | collective-permute-start | bytes 786440 | tf_op jit(solution)/shard_map/ppermute | solution.py:105
  5.3 0.9 dynamic-slice_bitcast_fusion
  6.2 0.4 collective-permute-done.pair
  6.6 5.0 %collective-permute-done.1.chain = f32[4,16,1024]{2,1,0:T(8,128)} collective-permute-done((f32[4,16,1024]{2,1,0:T(8,128)}, f32[4,16,1024]{2,1,0:T(8,128)}, u32[]{:S(2)}, u32[]{:S(2)}) %collective-permute-start.1) | collective-permute-done | bytes 262176 | tf_op jit(solution)/shard_map/ppermute | solution.py:111
  11.7 1.0 copy-done.5
  12.7 1.5 %shard_map.74 = (f32[8,16,1024]{2,1,0:T(8,128)S(1)}, f32[16,8,1024]{2,1,0:T(8,128)S(1)}) custom-call(f32[8,16,1024]{2,1,0:T(8,128)S(1)} %copy-done.5, f32[4,16,1024]{2,1,0:T(8,128)S(1)} %collective-permute-done.pair, f32[4,16,1024]{2,1,0:T(8,128)} %collective-permute-done.1.chain, f32[16,128]{1,0:T(8,128)S(1)} %slice.12.edges), custom_call_target="tpu_custom_call" | custom-call | tf_op jit(solution)/shard_map/pallas_call | solution.py:286
  14.3 0.8 copy-done.8
  15.0 0.8 copy-done.10
  15.9 4.8 %all-to-all-start = ((f32[16,8,1024]{2,1,0:T(8,128)}), f32[16,8,1024]{2,1,0:T(8,128)}, u32[]{:S(2)}, u32[]{:S(2)}) async-start(f32[16,8,1024]{2,1,0:T(8,128)} %copy-done.10), calls=%async_computation | async-start | bytes 1048576 | tf_op jit(solution)/shard_map/all_to_all | solution.py:335
  20.6 0.9 dynamic-slice_bitcast_fusion.1.matrix
  21.6 0.9 constant_dynamic-slice_fusion.filters
  22.5 7.3 %all-to-all-done = f32[16,8,1024]{2,1,0:T(8,128)} async-done(((f32[16,8,1024]{2,1,0:T(8,128)}), f32[16,8,1024]{2,1,0:T(8,128)}, u32[]{:S(2)}, u32[]{:S(2)}) %all-to-all-start) | async-done | bytes 524320 | tf_op jit(solution)/shard_map/all_to_all | solution.py:335
  29.8 1.6 %copy-done.1 = bf16[2,2,512,512]{3,2,1,0:T(8,128)(2,1)S(1)} copy-done((bf16[2,2,512,512]{3,2,1,0:T(8,128)(2,1)S(1)}, bf16[2,2,512,512]{3,2,1,0:T(8,128)(2,1)}, u32[]{:S(2)}) %copy-start.1) | copy-done | bytes 2097176
  31.4 1.0 copy-done.9
  32.4 3.2 %shard_map.75 = (f32[8,16,1024]{2,1,0:T(8,128)S(1)}, f32[8,16,1024]{2,1,0:T(8,128)S(1)}, f32[2,16,512]{2,1,0:T(8,128)S(1)}, f32[2,16,512]{2,1,0:T(8,128)S(1)}) custom-call(f32[8,16,1024]{2,1,0:T(8,128)S(1)} %copy-done.9, f32[128,1024]{1,0:T(8,128)} %bitcast.1.got, f32[128,256]{1,0:T(8,128)S(1)} %dynamic-slice_bitcast_fusion.1.matrix, ...), custom_call_target="tpu_custom_call" | custom-call | tf_op jit(solution)/shard_map/pallas_call | solution.py:286
  35.6 5.6 %collective-permute-start.2 = (f32[2,16,512]{2,1,0:T(8,128)S(1)}, f32[2,16,512]{2,1,0:T(8,128)S(1)}, u32[]{:S(2)}, u32[]{:S(2)}) collective-permute-start(f32[2,16,512]{2,1,0:T(8,128)S(1)} %get-tuple-element.44), channel_id=1, source_target_pairs={{0,16},{16,0},{32,48},{48,32},{64,80},{80,64},{96,112},{112,96},{1... | collective-permute-start | bytes 196616 | tf_op jit(solution)/shard_map/ppermute | solution.py:105
  41.3 0.9 collective-permute-done.2.got
  42.2 0.1 collective-permute-start.3
  42.3 3.1 %collective-permute-done.3.got = f32[2,16,512]{2,1,0:T(8,128)S(1)} collective-permute-done((f32[2,16,512]{2,1,0:T(8,128)S(1)}, f32[2,16,512]{2,1,0:T(8,128)S(1)}, u32[]{:S(2)}, u32[]{:S(2)}) %collective-permute-start.3) | collective-permute-done | bytes 65568 | tf_op jit(solution)/shard_map/ppermute | solution.py:105
  45.4 4.0 %collective-permute-start.6 = (f32[2,16,512]{2,1,0:T(8,128)S(1)}, f32[2,16,512]{2,1,0:T(8,128)S(1)}, u32[]{:S(2)}, u32[]{:S(2)}) collective-permute-start(f32[2,16,512]{2,1,0:T(8,128)S(1)} %get-tuple-element.46), channel_id=1, source_target_pairs={{0,192},{16,208},{32,224},{48,240},{64,128},{80,144},{96,160},{112... | collective-permute-start | bytes 196616 | tf_op jit(solution)/shard_map/ppermute | solution.py:105
  49.4 1.5 %collective-permute-start.5 = (f32[2,16,512]{2,1,0:T(8,128)S(1)}, f32[2,16,512]{2,1,0:T(8,128)S(1)}, u32[]{:S(2)}, u32[]{:S(2)}) collective-permute-start(f32[2,16,512]{2,1,0:T(8,128)S(1)} %get-tuple-element.46), channel_id=1, source_target_pairs={{0,128},{16,144},{32,160},{48,176},{64,192},{80,208},{96,224},{112... | collective-permute-start | bytes 196616 | tf_op jit(solution)/shard_map/ppermute | solution.py:105
  50.9 0.7 collective-permute-start.4
  51.5 6.0 %collective-permute-done.5.got2 = f32[2,16,512]{2,1,0:T(8,128)S(1)} collective-permute-done((f32[2,16,512]{2,1,0:T(8,128)S(1)}, f32[2,16,512]{2,1,0:T(8,128)S(1)}, u32[]{:S(2)}, u32[]{:S(2)}) %collective-permute-start.5) | collective-permute-done | bytes 65568 | tf_op jit(solution)/shard_map/ppermute | solution.py:105
  57.6 1.6 %collective-permute-done.4.got1 = f32[2,16,512]{2,1,0:T(8,128)S(1)} collective-permute-done((f32[2,16,512]{2,1,0:T(8,128)S(1)}, f32[2,16,512]{2,1,0:T(8,128)S(1)}, u32[]{:S(2)}, u32[]{:S(2)}) %collective-permute-start.4) | collective-permute-done | bytes 65568 | tf_op jit(solution)/shard_map/ppermute | solution.py:105
  59.2 1.3 %collective-permute-start.7 = (f32[16,512]{1,0:T(8,128)S(1)}, f32[16,512]{1,0:T(8,128)S(1)}, u32[]{:S(2)}, u32[]{:S(2)}) collective-permute-start(f32[16,512]{1,0:T(8,128)S(1)} %get-tuple-element.52), channel_id=1, source_target_pairs={{0,16},{16,0},{32,48},{48,32},{64,80},{80,64},{96,112},{112,96},{1... | collective-permute-start | bytes 98312 | tf_op jit(solution)/shard_map/ppermute | solution.py:105
  60.5 0.9 collective-permute-done.7.got
  61.3 0.1 shard_map.79
  61.4 0.4 collective-permute-start.8
  61.9 0.7 collective-permute-start.9
  62.6 0.5 collective-permute-done.8.pair
  63.1 4.9 %collective-permute-done.9.chain = f32[4,16,1024]{2,1,0:T(8,128)S(1)} collective-permute-done((f32[4,16,1024]{2,1,0:T(8,128)S(1)}, f32[4,16,1024]{2,1,0:T(8,128)S(1)}, u32[]{:S(2)}, u32[]{:S(2)}) %collective-permute-start.9) | collective-permute-done | bytes 262176 | tf_op jit(solution)/shard_map/ppermute | solution.py:111
  68.0 0.5 shard_map.80
  68.5 12.8 %all_to_all.10 = f32[16,8,1024]{2,1,0:T(8,128)S(1)} all-to-all(f32[16,8,1024]{2,1,0:T(8,128)S(1)} %get-tuple-element.57), channel_id=1, replica_groups=mesh['ax'=16,'xs'=16] {'xs'}, dimensions={0} | all-to-all | bytes 1048576 | tf_op jit(solution)/shard_map/all_to_all | solution.py:335
  81.3 2.1 %shard_map.81 = (f32[8,16,1024]{2,1,0:T(8,128)S(1)}, f32[8,16,1024]{2,1,0:T(8,128)S(1)}, f32[1,16,512]{2,1,0:T(8,128)S(1)}, f32[1,16,512]{2,1,0:T(8,128)S(1)}) custom-call(f32[8,16,1024]{2,1,0:T(8,128)S(1)} %get-tuple-element.56.explicit, f32[128,1024]{1,0:T(8,128)S(1)} %bitcast.6, f32[128,256]{1,0:T(8,128)S(1)} %dynamic-slice_bitcast_fusion.1.matrix, ...), custom_call_target="tpu_custom_call" | custom-call | tf_op jit(solution)/shard_map/pallas_call | solution.py:286
  83.5 0.8 copy-done.7
  84.2 2.3 %collective-permute-start.10 = (f32[1,16,512]{2,1,0:T(8,128)S(1)}, f32[1,16,512]{2,1,0:T(8,128)S(1)}, u32[]{:S(2)}, u32[]{:S(2)}) collective-permute-start(f32[1,16,512]{2,1,0:T(8,128)S(1)} %get-tuple-element.61), channel_id=1, source_target_pairs={{0,16},{16,0},{32,48},{48,32},{64,80},{80,64},{96,112},{112,96},{1... | collective-permute-start | bytes 98312 | tf_op jit(solution)/shard_map/ppermute | solution.py:105
  86.5 0.9 collective-permute-done.10.got
  87.4 0.7 collective-permute-start.11
  88.1 2.1 %collective-permute-done.11.got = f32[1,16,512]{2,1,0:T(8,128)S(1)} collective-permute-done((f32[1,16,512]{2,1,0:T(8,128)S(1)}, f32[1,16,512]{2,1,0:T(8,128)S(1)}, u32[]{:S(2)}, u32[]{:S(2)}) %collective-permute-start.11) | collective-permute-done | bytes 32800 | tf_op jit(solution)/shard_map/ppermute | solution.py:105
  90.3 2.6 %collective-permute-start.14 = (f32[1,16,512]{2,1,0:T(8,128)S(1)}, f32[1,16,512]{2,1,0:T(8,128)S(1)}, u32[]{:S(2)}, u32[]{:S(2)}) collective-permute-start(f32[1,16,512]{2,1,0:T(8,128)S(1)} %get-tuple-element.63), channel_id=1, source_target_pairs={{0,192},{16,208},{32,224},{48,240},{64,128},{80,144},{96,160},{112... | collective-permute-start | bytes 98312 | tf_op jit(solution)/shard_map/ppermute | solution.py:105
  92.9 1.9 %collective-permute-start.13 = (f32[1,16,512]{2,1,0:T(8,128)S(1)}, f32[1,16,512]{2,1,0:T(8,128)S(1)}, u32[]{:S(2)}, u32[]{:S(2)}) collective-permute-start(f32[1,16,512]{2,1,0:T(8,128)S(1)} %get-tuple-element.63), channel_id=1, source_target_pairs={{0,128},{16,144},{32,160},{48,176},{64,192},{80,208},{96,224},{112... | collective-permute-start | bytes 98312 | tf_op jit(solution)/shard_map/ppermute | solution.py:105
  94.8 1.2 %collective-permute-start.12 = (f32[1,16,512]{2,1,0:T(8,128)S(1)}, f32[1,16,512]{2,1,0:T(8,128)S(1)}, u32[]{:S(2)}, u32[]{:S(2)}) collective-permute-start(f32[1,16,512]{2,1,0:T(8,128)S(1)} %get-tuple-element.63), channel_id=1, source_target_pairs={{0,64},{16,80},{32,96},{48,112},{64,0},{80,16},{96,32},{112,48},{1... | collective-permute-start | bytes 98312 | tf_op jit(solution)/shard_map/ppermute | solution.py:105
  96.0 3.6 %collective-permute-done.13.got2 = f32[1,16,512]{2,1,0:T(8,128)S(1)} collective-permute-done((f32[1,16,512]{2,1,0:T(8,128)S(1)}, f32[1,16,512]{2,1,0:T(8,128)S(1)}, u32[]{:S(2)}, u32[]{:S(2)}) %collective-permute-start.13) | collective-permute-done | bytes 32800 | tf_op jit(solution)/shard_map/ppermute | solution.py:105
  99.7 2.4 %collective-permute-start.15 = (f32[16,512]{1,0:T(8,128)S(1)}, f32[16,512]{1,0:T(8,128)S(1)}, u32[]{:S(2)}, u32[]{:S(2)}) collective-permute-start(f32[16,512]{1,0:T(8,128)S(1)} %get-tuple-element.67), channel_id=1, source_target_pairs={{0,16},{16,0},{32,48},{48,32},{64,80},{80,64},{96,112},{112,96},{1... | collective-permute-start | bytes 98312 | tf_op jit(solution)/shard_map/ppermute | solution.py:105
  102.2 0.9 collective-permute-done.15
  103.0 2.1 %multiply_add_fusion = f32[8,16,1024]{2,1,0:T(8,128)} fusion(f32[8,16,1024]{2,1,0:T(8,128)} %copy-done.6, f32[8,16,1024]{2,1,0:T(8,128)} %copy-done.7, f32[16,1024]{1,0:T(8,128)S(1)} %pad_maximum_fusion), kind=kLoop, calls=%fused_computation | loop fusion | flops 262144 | bytes 1638400 | tf_op jit(solution)/shard_map/add | solution.py:380
  (28 shorter events, 0.2 us)
Async XLA Ops:
  0.0 29.7 %copy-start = (bf16[2,2,512,512]{3,2,1,0:T(8,128)(2,1)S(1)}, bf16[2,2,512,512]{3,2,1,0:T(8,128)(2,1)}, u32[]{:S(2)}) copy-start(bf16[2,2,512,512]{3,2,1,0:T(8,128)(2,1)} %constant.39.clone.inverse) | copy-start | bytes 6291460
  0.0 29.7 %copy-start.3 = (f32[8,16,1024]{2,1,0:T(8,128)S(1)}, f32[8,16,1024]{2,1,0:T(8,128)}, u32[]{:S(2)}) copy-start(f32[8,16,1024]{2,1,0:T(8,128)} %swirl_rate.3) | copy-start | bytes 1572868
  0.0 1.2 %copy-start.4 = (f32[8,16,1024]{2,1,0:T(8,128)S(1)}, f32[8,16,1024]{2,1,0:T(8,128)}, u32[]{:S(2)}) copy-start(f32[8,16,1024]{2,1,0:T(8,128)} %field.3) | copy-start | bytes 1572868
  1.2 28.6 %copy-start.2 = (f32[8,16,1024]{2,1,0:T(8,128)S(1)}, f32[8,16,1024]{2,1,0:T(8,128)}, u32[]{:S(2)}) copy-start(f32[8,16,1024]{2,1,0:T(8,128)} %axial_rate.3) | copy-start | bytes 1572868
  2.0 4.6 %collective-permute-start = (f32[4,16,1024]{2,1,0:T(8,128)}, f32[4,16,1024]{2,1,0:T(8,128)S(1)}, u32[]{:S(2)}, u32[]{:S(2)}) collective-permute-start(f32[4,16,1024]{2,1,0:T(8,128)} %get-tuple-element.37), channel_id=1, source_target_pairs={{0,16},{16,0},{32,48},{48,32},{64,80},{80,64},{96,112},{112,96},{1... | collective-permute-start | bytes 786440 | tf_op jit(solution)/shard_map/ppermute | solution.py:105
  5.3 6.4 %collective-permute-start.1 = (f32[4,16,1024]{2,1,0:T(8,128)}, f32[4,16,1024]{2,1,0:T(8,128)}, u32[]{:S(2)}, u32[]{:S(2)}) collective-permute-start(f32[4,16,1024]{2,1,0:T(8,128)} %get-tuple-element.38), channel_id=1, source_target_pairs={{0,240},{16,32},{32,16},{48,64},{64,48},{80,96},{96,80},{112,128},... | collective-permute-start | bytes 786440 | tf_op jit(solution)/shard_map/ppermute | solution.py:111
  11.7 1.0 copy-start.5
  14.2 0.8 copy-start.8
  15.0 0.8 copy-start.10
  15.9 13.9 %all-to-all-start = ((f32[16,8,1024]{2,1,0:T(8,128)}), f32[16,8,1024]{2,1,0:T(8,128)}, u32[]{:S(2)}, u32[]{:S(2)}) async-start(f32[16,8,1024]{2,1,0:T(8,128)} %copy-done.10), calls=%async_computation | async-start | bytes 1048576 | tf_op jit(solution)/shard_map/all_to_all | solution.py:335
  29.8 1.6 %copy-start.1 = (bf16[2,2,512,512]{3,2,1,0:T(8,128)(2,1)S(1)}, bf16[2,2,512,512]{3,2,1,0:T(8,128)(2,1)}, u32[]{:S(2)}) copy-start(bf16[2,2,512,512]{3,2,1,0:T(8,128)(2,1)} %constant.38.clone.forward) | copy-start | bytes 6291460
  31.4 1.0 copy-start.9
  35.6 6.5 %collective-permute-start.2 = (f32[2,16,512]{2,1,0:T(8,128)S(1)}, f32[2,16,512]{2,1,0:T(8,128)S(1)}, u32[]{:S(2)}, u32[]{:S(2)}) collective-permute-start(f32[2,16,512]{2,1,0:T(8,128)S(1)} %get-tuple-element.44), channel_id=1, source_target_pairs={{0,16},{16,0},{32,48},{48,32},{64,80},{80,64},{96,112},{112,96},{1... | collective-permute-start | bytes 196616 | tf_op jit(solution)/shard_map/ppermute | solution.py:105
  42.2 3.2 %collective-permute-start.3 = (f32[2,16,512]{2,1,0:T(8,128)S(1)}, f32[2,16,512]{2,1,0:T(8,128)S(1)}, u32[]{:S(2)}, u32[]{:S(2)}) collective-permute-start(f32[2,16,512]{2,1,0:T(8,128)S(1)} %get-tuple-element.45.block), channel_id=1, source_target_pairs={{0,32},{16,48},{32,0},{48,16},{64,96},{80,112},{96,64},{112,80},{1... | collective-permute-start | bytes 196616 | tf_op jit(solution)/shard_map/ppermute | solution.py:105
  45.4 6.1 %collective-permute-start.6 = (f32[2,16,512]{2,1,0:T(8,128)S(1)}, f32[2,16,512]{2,1,0:T(8,128)S(1)}, u32[]{:S(2)}, u32[]{:S(2)}) collective-permute-start(f32[2,16,512]{2,1,0:T(8,128)S(1)} %get-tuple-element.46), channel_id=1, source_target_pairs={{0,192},{16,208},{32,224},{48,240},{64,128},{80,144},{96,160},{112... | collective-permute-start | bytes 196616 | tf_op jit(solution)/shard_map/ppermute | solution.py:105
  49.4 8.2 %collective-permute-start.5 = (f32[2,16,512]{2,1,0:T(8,128)S(1)}, f32[2,16,512]{2,1,0:T(8,128)S(1)}, u32[]{:S(2)}, u32[]{:S(2)}) collective-permute-start(f32[2,16,512]{2,1,0:T(8,128)S(1)} %get-tuple-element.46), channel_id=1, source_target_pairs={{0,128},{16,144},{32,160},{48,176},{64,192},{80,208},{96,224},{112... | collective-permute-start | bytes 196616 | tf_op jit(solution)/shard_map/ppermute | solution.py:105
  50.9 8.3 %collective-permute-start.4 = (f32[2,16,512]{2,1,0:T(8,128)S(1)}, f32[2,16,512]{2,1,0:T(8,128)S(1)}, u32[]{:S(2)}, u32[]{:S(2)}) collective-permute-start(f32[2,16,512]{2,1,0:T(8,128)S(1)} %get-tuple-element.46), channel_id=1, source_target_pairs={{0,64},{16,80},{32,96},{48,112},{64,0},{80,16},{96,32},{112,48},{1... | collective-permute-start | bytes 196616 | tf_op jit(solution)/shard_map/ppermute | solution.py:105
  59.2 2.2 %collective-permute-start.7 = (f32[16,512]{1,0:T(8,128)S(1)}, f32[16,512]{1,0:T(8,128)S(1)}, u32[]{:S(2)}, u32[]{:S(2)}) collective-permute-start(f32[16,512]{1,0:T(8,128)S(1)} %get-tuple-element.52), channel_id=1, source_target_pairs={{0,16},{16,0},{32,48},{48,32},{64,80},{80,64},{96,112},{112,96},{1... | collective-permute-start | bytes 98312 | tf_op jit(solution)/shard_map/ppermute | solution.py:105
  61.4 1.6 %collective-permute-start.8 = (f32[4,16,1024]{2,1,0:T(8,128)S(1)}, f32[4,16,1024]{2,1,0:T(8,128)S(1)}, u32[]{:S(2)}, u32[]{:S(2)}) collective-permute-start(f32[4,16,1024]{2,1,0:T(8,128)S(1)} %get-tuple-element.54), channel_id=1, source_target_pairs={{0,16},{16,0},{32,48},{48,32},{64,80},{80,64},{96,112},{112,96},{1... | collective-permute-start | bytes 786440 | tf_op jit(solution)/shard_map/ppermute | solution.py:105
  61.9 6.1 %collective-permute-start.9 = (f32[4,16,1024]{2,1,0:T(8,128)S(1)}, f32[4,16,1024]{2,1,0:T(8,128)S(1)}, u32[]{:S(2)}, u32[]{:S(2)}) collective-permute-start(f32[4,16,1024]{2,1,0:T(8,128)S(1)} %get-tuple-element.55), channel_id=1, source_target_pairs={{0,240},{16,32},{32,16},{48,64},{64,48},{80,96},{96,80},{112,128},... | collective-permute-start | bytes 786440 | tf_op jit(solution)/shard_map/ppermute | solution.py:111
  83.5 0.8 copy-start.7
  84.2 15.5 %copy-start.6 = (f32[8,16,1024]{2,1,0:T(8,128)}, f32[8,16,1024]{2,1,0:T(8,128)S(1)}, u32[]{:S(2)}) copy-start(f32[8,16,1024]{2,1,0:T(8,128)S(1)} %get-tuple-element.58) | copy-start | bytes 1572868
  84.2 3.1 %collective-permute-start.10 = (f32[1,16,512]{2,1,0:T(8,128)S(1)}, f32[1,16,512]{2,1,0:T(8,128)S(1)}, u32[]{:S(2)}, u32[]{:S(2)}) collective-permute-start(f32[1,16,512]{2,1,0:T(8,128)S(1)} %get-tuple-element.61), channel_id=1, source_target_pairs={{0,16},{16,0},{32,48},{48,32},{64,80},{80,64},{96,112},{112,96},{1... | collective-permute-start | bytes 98312 | tf_op jit(solution)/shard_map/ppermute | solution.py:105
  87.4 2.9 %collective-permute-start.11 = (f32[1,16,512]{2,1,0:T(8,128)S(1)}, f32[1,16,512]{2,1,0:T(8,128)S(1)}, u32[]{:S(2)}, u32[]{:S(2)}) collective-permute-start(f32[1,16,512]{2,1,0:T(8,128)S(1)} %get-tuple-element.62.block), channel_id=1, source_target_pairs={{0,32},{16,48},{32,0},{48,16},{64,96},{80,112},{96,64},{112,80},{1... | collective-permute-start | bytes 98312 | tf_op jit(solution)/shard_map/ppermute | solution.py:105
  90.3 5.7 %collective-permute-start.14 = (f32[1,16,512]{2,1,0:T(8,128)S(1)}, f32[1,16,512]{2,1,0:T(8,128)S(1)}, u32[]{:S(2)}, u32[]{:S(2)}) collective-permute-start(f32[1,16,512]{2,1,0:T(8,128)S(1)} %get-tuple-element.63), channel_id=1, source_target_pairs={{0,192},{16,208},{32,224},{48,240},{64,128},{80,144},{96,160},{112... | collective-permute-start | bytes 98312 | tf_op jit(solution)/shard_map/ppermute | solution.py:105
  92.9 6.7 %collective-permute-start.13 = (f32[1,16,512]{2,1,0:T(8,128)S(1)}, f32[1,16,512]{2,1,0:T(8,128)S(1)}, u32[]{:S(2)}, u32[]{:S(2)}) collective-permute-start(f32[1,16,512]{2,1,0:T(8,128)S(1)} %get-tuple-element.63), channel_id=1, source_target_pairs={{0,128},{16,144},{32,160},{48,176},{64,192},{80,208},{96,224},{112... | collective-permute-start | bytes 98312 | tf_op jit(solution)/shard_map/ppermute | solution.py:105
  94.8 4.9 %collective-permute-start.12 = (f32[1,16,512]{2,1,0:T(8,128)S(1)}, f32[1,16,512]{2,1,0:T(8,128)S(1)}, u32[]{:S(2)}, u32[]{:S(2)}) collective-permute-start(f32[1,16,512]{2,1,0:T(8,128)S(1)} %get-tuple-element.63), channel_id=1, source_target_pairs={{0,64},{16,80},{32,96},{48,112},{64,0},{80,16},{96,32},{112,48},{1... | collective-permute-start | bytes 98312 | tf_op jit(solution)/shard_map/ppermute | solution.py:105
  99.7 3.3 %collective-permute-start.15 = (f32[16,512]{1,0:T(8,128)S(1)}, f32[16,512]{1,0:T(8,128)S(1)}, u32[]{:S(2)}, u32[]{:S(2)}) collective-permute-start(f32[16,512]{1,0:T(8,128)S(1)} %get-tuple-element.67), channel_id=1, source_target_pairs={{0,16},{16,0},{32,48},{48,32},{64,80},{80,64},{96,112},{112,96},{1... | collective-permute-start | bytes 98312 | tf_op jit(solution)/shard_map/ppermute | solution.py:105

commit v3 on v2

--- a/solution.py
+++ b/solution.py
@@ -116,13 +116,43 @@
     return coarse, (values - coarse.astype(jnp.float32)).astype(jnp.bfloat16)
 
 
-def split_dot(left, right):
-    dot = lambda x, y: jnp.dot(x, y, preferred_element_type=jnp.float32)
+def split_dot(left, right, depth=0):
+    def dot(x, y):
+        return lax.dot_general(
+            x, y, (((1,), (depth,)), ((), ())), preferred_element_type=jnp.float32
+        )
+
     return dot(left[0], right[0]) + (dot(left[1], right[0]) + dot(left[0], right[1]))
 
 
-def carry_kernel(field, pair, chain, edges, explicit, sent):
-    planes, rows, points = field.shape
+def setup_kernel(radial, damping, matrix, edges, filters, sems):
+    group = lax.axis_index("xs")
+    lines, columns = matrix.shape[0], edges.shape[1]
+    copies = [
+        pltpu.make_async_copy(
+            radial.at[group, pl.ds(lines, edges.shape[0]), pl.ds(0, columns)], edges, sems.at[0]
+        ),
+        pltpu.make_async_copy(radial.at[group, pl.ds(0, lines)], matrix, sems.at[1]),
+        pltpu.make_async_copy(damping.at[group], filters, sems.at[2]),
+    ]
+    for copy in copies:
+        copy.start()
+    for copy in copies:
+        copy.wait()
+
+
+def inner_kernel(field, inner):
+    planes = field.shape[0]
+    for plane in range(planes):
+        value = (1.0 + AXIAL_WEIGHT * STENCIL[HALO]) * field[plane]
+        for source in range(max(0, plane - HALO), min(planes, plane + HALO + 1)):
+            if source != plane:
+                value = value + (AXIAL_WEIGHT * STENCIL[HALO + source - plane]) * field[source]
+        inner[plane] = value
+
+
+def carry_kernel(inner, pair, chain, edges, explicit, sent):
+    planes, rows, points = inner.shape
     groups = sent.shape[0]
     place = lax.axis_index("ax")
     group = lax.axis_index("xs")
@@ -134,14 +164,15 @@
         where = slice(part * quarter, (part + 1) * quarter)
         low = [jnp.where(odd, pair[j, :, where], chain[j, :, where]) for j in range(HALO)]
         high = [jnp.where(odd, chain[j, :, where], pair[j, :, where]) for j in range(HALO)]
-        every = [low_scale * value for value in low]
-        every += [field[plane, :, where] for plane in range(planes)]
-        every += [high_scale * value for value in high]
+        low = [low_scale * value for value in low]
+        high = [high_scale * value for value in high]
         for plane in range(planes):
-            value = (1.0 + AXIAL_WEIGHT * STENCIL[HALO]) * every[plane + HALO]
-            for step in range(1, HALO + 1):
-                both = every[plane + HALO - step] + every[plane + HALO + step]
-                value = value + (AXIAL_WEIGHT * STENCIL[HALO + step]) * both
+            value = inner[plane, :, where]
+            for j in range(HALO):
+                if plane + HALO - j <= HALO:
+                    value = value + (AXIAL_WEIGHT * STENCIL[j - plane]) * low[j]
+                if planes + j - plane <= HALO:
+                    value = value + (AXIAL_WEIGHT * STENCIL[HALO + planes + j - plane]) * high[j]
             explicit[plane, :, where] = value
     lines = explicit[...].reshape(planes * rows, points)
     carry = split_dot(split(edges[...]), split(lines))
@@ -153,8 +184,7 @@
     explicit,
     got,
     matrix,
-    forward,
-    inverse,
+    azimuth,
     filters,
     axial_rate,
     swirl_rate,
@@ -172,14 +202,13 @@
     sides = (solved[:, :half] + solved[:, half:], solved[:, :half] - solved[:, half:])
     periods = []
     for parity in range(2):
-        table = (forward[parity, 0], forward[parity, 1])
+        table = (azimuth[parity, 0], azimuth[parity, 1])
         spectrum = split_dot(split(sides[parity]), table).reshape(planes, rows, half)
         swapped = jnp.concatenate([spectrum[..., quarter:], spectrum[..., :quarter]], axis=-1)
         smooth = spectrum * filters[:, parity * half : (parity + 1) * half]
         slope = swapped * filters[:, points + parity * half : points + (parity + 1) * half]
         both = jnp.concatenate([smooth, slope], axis=0).reshape(2 * planes * rows, half)
-        table = (inverse[parity, 0], inverse[parity, 1])
-        periods.append(split_dot(split(both), table).reshape(2, planes, rows, half))
+        periods.append(split_dot(split(both), table, 1).reshape(2, planes, rows, half))
     for side in range(2):
         where = slice(side * half, (side + 1) * half)
         value = fade = None
@@ -282,6 +311,26 @@
             chain[j, :, where] = jnp.where(odd, high, low)
 
 
+def last_kernel(partial, decay, mine, got, out, field, sems):
+    planes, rows, points = partial.shape
+    half = points // 2
+    odd = lax.axis_index("ax") % 2 == 1
+    incoming = [jnp.where(odd == (side == 1), mine[...], got[...]) for side in range(2)]
+    copies = []
+    for plane in range(planes):
+        for side in range(2):
+            where = slice(side * half, (side + 1) * half)
+            value = partial[plane, :, where] + decay[plane, :, where] * incoming[side]
+            field[plane, :, where] = value
+        if plane % 2 == 1:
+            pair = pl.ds(plane - 1, 2)
+            copy = pltpu.make_async_copy(field.at[pair], out.at[pair], sems.at[plane // 2])
+            copy.start()
+            copies.append(copy)
+    for copy in copies:
+        copy.wait()
+
+
 def call(kernel, out_shape, *args, vmem=4):
     return pl.pallas_call(
         kernel,
@@ -296,53 +345,47 @@
     planes, rows, points = scalar.shape
     half = points // 2
     groups = lax.axis_size("xs")
-    group = lax.axis_index("xs")
-    place = lax.axis_index("ax")
-    odd = place % 2 == 1
     lines = planes * rows
     tables = azimuth_tables(points)
-    forward = jnp.asarray(np.stack([np.stack(split_bf16(t)) for t in tables]))
-    inverse = jnp.asarray(np.stack([np.stack(split_bf16(t.T)) for t in tables]))
-    radial = lax.dynamic_index_in_dim(
-        jnp.asarray(radial_tables(rows * groups, groups, planes)), group, 0, keepdims=False
-    )
-    matrix, edges = radial[:lines], radial[lines:, :lines]
-    filters = lax.dynamic_slice_in_dim(
-        jnp.asarray(filter_tables(rows * groups, points)), group * rows, rows, 0
-    )
-    block = jax.ShapeDtypeStruct((planes, rows, points), jnp.float32)
-
-    ends = jax.ShapeDtypeStruct((HALO, rows, points), jnp.float32)
-
-    def halves(count):
-        return jax.ShapeDtypeStruct((count, rows, half), jnp.float32)
-
-    plane_half = jax.ShapeDtypeStruct((rows, half), jnp.float32)
-
-    field = scalar
+    azimuth = jnp.asarray(np.stack([np.stack(split_bf16(t)) for t in tables]))
+    radial = radial_tables(rows * groups, groups, planes)
+    damping = filter_tables(rows * groups, points).reshape(groups, rows, 2 * points)
+
+    def shape(*sizes):
+        return jax.ShapeDtypeStruct(sizes, jnp.float32)
+
+    block, ends, one = shape(planes, rows, points), shape(HALO, rows, points), shape(rows, half)
+
     pair_end, chain_end = call(ends_kernel, (ends, ends), scalar)
-    saved = None
+    chain, pair = chain_swap(chain_end), swap(pair_end, 1)
+    inner = call(inner_kernel, block, scalar)
+    matrix, edges, filters = pl.pallas_call(
+        setup_kernel,
+        out_shape=(
+            shape(lines, lines + groups * planes),
+            shape(2 * planes, lines),
+            shape(rows, 2 * points),
+        ),
+        in_specs=[pl.BlockSpec(memory_space=pltpu.HBM)] * 2,
+        out_specs=(pl.BlockSpec(memory_space=pltpu.VMEM),) * 3,
+        scratch_shapes=[pltpu.SemaphoreType.DMA((3,))],
+        compiler_params=pltpu.CompilerParams(vmem_limit_bytes=4 * 1024 * 1024),
+    )(jnp.asarray(radial), jnp.asarray(damping))
+
     for substep in range(SUBSTEPS):
-        chain, pair = chain_swap(chain_end), swap(pair_end, 1)
         explicit, sent = call(
-            carry_kernel,
-            (block, jax.ShapeDtypeStruct((groups, planes, points), jnp.float32)),
-            field,
-            pair,
-            chain,
-            edges,
+            carry_kernel, (block, shape(groups, planes, points)), inner, pair, chain, edges
         )
         got = lax.all_to_all(sent, "xs", split_axis=0, concat_axis=0, tiled=True)
-        first = saved is None
-        parts = 2 if first else 1
+        first = substep == 0
+        parts = shape(2 if first else 1, rows, half)
         partial, decay, mine, other = call(
             middle_kernel,
-            (block, block, halves(parts), halves(parts)),
+            (block, block, parts, parts),
             explicit,
             got.reshape(groups * planes, points),
             matrix,
-            forward,
-            inverse,
+            azimuth,
             filters,
             axial_rate,
             swirl_rate,
@@ -350,35 +393,39 @@
         )
         got = swap(other, 1)
         if first:
-            value, behind, spans = call(
-                chip_kernel, (halves(2), plane_half, halves(2)), mine, got
-            )
+            value, behind, spans = call(chip_kernel, (parts, one, parts), mine, got)
         else:
-            value, behind = call(chip_kernel, (halves(1), plane_half), mine, got, spans)
+            value, behind = call(chip_kernel, (parts, one), mine, got, spans)
         got = swap(value, 2)
         if first:
-            value, prefix, gains = call(
-                couple_kernel, (halves(2), plane_half, halves(3)), value, got
-            )
+            out = (parts, one, shape(3, rows, half))
+            value, prefix, gains = call(couple_kernel, out, value, got)
         else:
-            value, prefix = call(couple_kernel, (halves(1), plane_half), value, got, gains)
-        got3, got2, got1 = swap(value, 12), swap(value, 8), swap(value, 4)
-        args = (got1, got2, got3, prefix, behind, spans, gains)
+            value, prefix = call(couple_kernel, (parts, one), value, got, gains)
+        far3, far2, far1 = swap(value, 12), swap(value, 8), swap(value, 4)
+        args = (far1, far2, far3, prefix, behind, spans, gains)
         if first:
-            mine, other, saved = call(enter_kernel, (plane_half, plane_half, halves(3)), *args)
+            mine, other, weights = call(enter_kernel, (one, one, shape(3, rows, half)), *args)
         else:
-            mine, other = call(enter_kernel, (plane_half, plane_half), *args, saved)
+            mine, other = call(enter_kernel, (one, one), *args, weights)
         got = swap(other, 1)
         if substep < SUBSTEPS - 1:
             field, pair_end, chain_end = call(
                 finish_kernel, (block, ends, ends), partial, decay, mine, got
             )
-        else:
-            incoming = jnp.concatenate(
-                [jnp.where(odd, got, mine), jnp.where(odd, mine, got)], axis=1
-            )
-            field = partial + decay * incoming
-    return field
+            chain, pair = chain_swap(chain_end), swap(pair_end, 1)
+            inner = call(inner_kernel, block, field)
+    return pl.pallas_call(
+        last_kernel,
+        out_shape=block,
+        in_specs=[pl.BlockSpec(memory_space=pltpu.VMEM)] * 4,
+        out_specs=pl.BlockSpec(memory_space=pl.ANY),
+        scratch_shapes=[
+            pltpu.VMEM((planes, rows, points), jnp.float32),
+            pltpu.SemaphoreType.DMA((planes // 2,)),
+        ],
+        compiler_params=pltpu.CompilerParams(vmem_limit_bytes=4 * 1024 * 1024),
+    )(partial, decay, mine, got)
 
 
 def solution(mesh):

time: 106 us -> 94.2 us (0.89)
  blocking collectives: 12.8 us -> 25.2 us
  waiting for transfers between devices: 38.1 us -> 26.8 us
  local copies, waits for them, and re-layouts: 10 us -> 4.31 us
  starting transfers between devices: 33.5 us -> 30.4 us
  other arithmetic: 2.09 us -> 0 us
  Pallas kernels: 8.47 us -> 7.08 us
    all_to_all x1 -> x2, blocking collectives: 12.8 us -> 25.2 us  [body(): got = lax.all_to_all(sent, 'xs', split_axis=0, concat_axis=0, tiled=True)]
    all_to_all x1 -> x0, waiting for transfers between devices: 7.25 us -> none  [body(): got = lax.all_to_all(sent, 'xs', split_axis=0, concat_axis=0, tiled=True)]
    all_to_all x1 -> x0, starting transfers between devices: 4.78 us -> none  [body(): got = lax.all_to_all(sent, 'xs', split_axis=0, concat_axis=0, tiled=True)]
    unnamed x22 -> x12, local copies, waits for them, and re-layouts: 7.25 us -> 4.31 us
    ppermute x2, waiting for transfers between devices: 9.94 us -> 7.06 us  [chain_swap(): return lax.ppermute(value, 'ax', pairs)]
    pallas_call x12 -> x14, Pallas kernels: 8.47 us -> 5.88 us  [call(): pl.pallas_call(kernel, out_shape=out_shape, in_specs=[pl.BlockSpec(memory...]
    add x1 -> x0, other arithmetic: 2.07 us -> none  [body(): field = partial + decay * incoming]
    ppermute x14, starting transfers between devices: 28 us -> 29.4 us  [swap(): return lax.ppermute(value, 'ax', [(i, i ^ mask) for i in range(count)])]
  transfers between devices with their start and end apart: 17 -> 16, of which waited for: 14 -> 11; matrix products, arithmetic and copies ran while one was open for 3% -> 0% of each run, Pallas kernels for 0% -> 1%
where the time goes in v3:
time: 94.2 us; the launch traced here: 94 us
  starting transfers between devices  30.4 us (32%)
  waiting for transfers between devices  26.8 us (28%)
  blocking collectives  25.2 us (27%)
  Pallas kernels  7.08 us (8%)
  local copies, waits for them, and re-layouts  4.31 us (5%)
    ppermute x14, starting transfers between devices, swap(): return lax.ppermute(value, 'ax', [(i, i ^ mask) for i in range(count)])  29.4 us
    all_to_all x2, blocking collectives, body(): got = lax.all_to_all(sent, 'xs', split_axis=0, concat_axis=0, tiled=True)  25.2 us
    ppermute x14, waiting for transfers between devices, swap(): return lax.ppermute(value, 'ax', [(i, i ^ mask) for i in range(count)])  19.8 us
    ppermute x2, waiting for transfers between devices, chain_swap(): return lax.ppermute(value, 'ax', pairs)  7.06 us
    pallas_call x14, Pallas kernels, call(): pl.pallas_call(kernel, out_shape=out_shape, in_specs=[pl.BlockSpec(memory...  5.88 us
    unnamed x12, local copies, waits for them, and re-layouts  4.31 us
  transfers between devices with their start and end apart: 16, of which 11 were waited for; matrix products, arithmetic and copies ran while one was open for 0% of the time, Pallas kernels for 1%

profile of v3, /device:TPU:1, one launch (start us, length us, event | category | flops | bytes accessed | tf_op | source)
XLA Modules:
  0.0 94.0 jit_solution(11926800076987470930)
XLA Ops:
  0.0 1.0 %copy-done.5 = f32[8,16,1024]{2,1,0:T(8,128)S(1)} copy-done((f32[8,16,1024]{2,1,0:T(8,128)S(1)}, f32[8,16,1024]{2,1,0:T(8,128)}, u32[]{:S(2)}) %copy-start.5) | copy-done | bytes 524312
  1.1 3.3 %collective-permute-start = (f32[4,16,1024]{2,1,0:T(8,128)S(1)}, f32[4,16,1024]{2,1,0:T(8,128)S(1)}, u32[]{:S(2)}, u32[]{:S(2)}) collective-permute-start(f32[4,16,1024]{2,1,0:T(8,128)S(1)} %get-tuple-element.40), channel_id=1, source_target_pairs={{0,16},{16,0},{32,48},{48,32},{64,80},{80,64},{96,112},{112,96},{1... | collective-permute-start | bytes 786440 | tf_op jit(solution)/shard_map/ppermute | solution.py:105
  4.4 0.0 collective-permute-start.1
  4.4 0.2 shard_map.64.inner
  4.7 0.0 copy-start.1
  4.7 1.7 %copy-done.1 = f32[16,144,256]{2,1,0:T(8,128)S(1)} copy-done((f32[16,144,256]{2,1,0:T(8,128)S(1)}, f32[16,144,256]{2,1,0:T(8,128)}, u32[]{:S(2)}) %copy-start.1) | copy-done | bytes 2359320
  6.3 1.6 %copy-done.4 = f32[16,16,2048]{2,1,0:T(8,128)S(1)} copy-done((f32[16,16,2048]{2,1,0:T(8,128)S(1)}, f32[16,16,2048]{2,1,0:T(8,128)}, u32[]{:S(2)}) %copy-start.4) | copy-done | bytes 2097176
  7.9 0.4 shard_map.66
  8.3 0.0 copy-start
  8.3 0.0 collective-permute-done.pair
  8.3 2.2 %collective-permute-done.1.chain = f32[4,16,1024]{2,1,0:T(8,128)S(1)} collective-permute-done((f32[4,16,1024]{2,1,0:T(8,128)S(1)}, f32[4,16,1024]{2,1,0:T(8,128)S(1)}, u32[]{:S(2)}, u32[]{:S(2)}) %collective-permute-start.1) | collective-permute-done | bytes 262176 | tf_op jit(solution)/shard_map/ppermute | solution.py:111
  10.5 0.4 shard_map.67
  10.9 13.6 %all_to_all.10 = f32[16,8,1024]{2,1,0:T(8,128)S(1)} all-to-all(f32[16,8,1024]{2,1,0:T(8,128)S(1)} %get-tuple-element.44), channel_id=1, replica_groups=mesh['ax'=16,'xs'=16] {'xs'}, dimensions={0} | all-to-all | bytes 1048576 | tf_op jit(solution)/shard_map/all_to_all | solution.py:379
  24.5 2.2 %shard_map.68 = (f32[8,16,1024]{2,1,0:T(8,128)S(1)}, f32[8,16,1024]{2,1,0:T(8,128)S(1)}, f32[2,16,512]{2,1,0:T(8,128)S(1)}, f32[2,16,512]{2,1,0:T(8,128)S(1)}) custom-call(f32[8,16,1024]{2,1,0:T(8,128)S(1)} %get-tuple-element.43.explicit, f32[128,1024]{1,0:T(8,128)S(1)} %bitcast.3, f32[128,256]{1,0:T(8,128)S(1)} %get-tuple-element.45.matrix, ...), custom_call_target="tpu_custom_call" | custom-call | tf_op jit(solution)/shard_map/pallas_call | solution.py:335
  26.7 5.8 %collective-permute-start.2 = (f32[2,16,512]{2,1,0:T(8,128)S(1)}, f32[2,16,512]{2,1,0:T(8,128)S(1)}, u32[]{:S(2)}, u32[]{:S(2)}) collective-permute-start(f32[2,16,512]{2,1,0:T(8,128)S(1)} %get-tuple-element.50), channel_id=1, source_target_pairs={{0,16},{16,0},{32,48},{48,32},{64,80},{80,64},{96,112},{112,96},{1... | collective-permute-start | bytes 196616 | tf_op jit(solution)/shard_map/ppermute | solution.py:105
  32.5 0.9 collective-permute-done.2.got
  33.4 0.1 collective-permute-start.3
  33.5 3.1 %collective-permute-done.3.got = f32[2,16,512]{2,1,0:T(8,128)S(1)} collective-permute-done((f32[2,16,512]{2,1,0:T(8,128)S(1)}, f32[2,16,512]{2,1,0:T(8,128)S(1)}, u32[]{:S(2)}, u32[]{:S(2)}) %collective-permute-start.3) | collective-permute-done | bytes 65568 | tf_op jit(solution)/shard_map/ppermute | solution.py:105
  36.6 3.8 %collective-permute-start.6 = (f32[2,16,512]{2,1,0:T(8,128)S(1)}, f32[2,16,512]{2,1,0:T(8,128)S(1)}, u32[]{:S(2)}, u32[]{:S(2)}) collective-permute-start(f32[2,16,512]{2,1,0:T(8,128)S(1)} %get-tuple-element.52), channel_id=1, source_target_pairs={{0,192},{16,208},{32,224},{48,240},{64,128},{80,144},{96,160},{112... | collective-permute-start | bytes 196616 | tf_op jit(solution)/shard_map/ppermute | solution.py:105
  40.5 1.6 %collective-permute-start.5 = (f32[2,16,512]{2,1,0:T(8,128)S(1)}, f32[2,16,512]{2,1,0:T(8,128)S(1)}, u32[]{:S(2)}, u32[]{:S(2)}) collective-permute-start(f32[2,16,512]{2,1,0:T(8,128)S(1)} %get-tuple-element.52), channel_id=1, source_target_pairs={{0,128},{16,144},{32,160},{48,176},{64,192},{80,208},{96,224},{112... | collective-permute-start | bytes 196616 | tf_op jit(solution)/shard_map/ppermute | solution.py:105
  42.1 0.6 collective-permute-start.4
  42.6 0.0 collective-permute-done.6.got3
  42.6 6.0 %collective-permute-done.5.got2 = f32[2,16,512]{2,1,0:T(8,128)S(1)} collective-permute-done((f32[2,16,512]{2,1,0:T(8,128)S(1)}, f32[2,16,512]{2,1,0:T(8,128)S(1)}, u32[]{:S(2)}, u32[]{:S(2)}) %collective-permute-start.5) | collective-permute-done | bytes 65568 | tf_op jit(solution)/shard_map/ppermute | solution.py:105
  48.6 1.6 %collective-permute-done.4.got1 = f32[2,16,512]{2,1,0:T(8,128)S(1)} collective-permute-done((f32[2,16,512]{2,1,0:T(8,128)S(1)}, f32[2,16,512]{2,1,0:T(8,128)S(1)}, u32[]{:S(2)}, u32[]{:S(2)}) %collective-permute-start.4) | collective-permute-done | bytes 65568 | tf_op jit(solution)/shard_map/ppermute | solution.py:105
  50.3 1.2 %collective-permute-start.7 = (f32[16,512]{1,0:T(8,128)S(1)}, f32[16,512]{1,0:T(8,128)S(1)}, u32[]{:S(2)}, u32[]{:S(2)}) collective-permute-start(f32[16,512]{1,0:T(8,128)S(1)} %get-tuple-element.58), channel_id=1, source_target_pairs={{0,16},{16,0},{32,48},{48,32},{64,80},{80,64},{96,112},{112,96},{1... | collective-permute-start | bytes 98312 | tf_op jit(solution)/shard_map/ppermute | solution.py:105
  51.5 0.9 collective-permute-done.7.got
  52.3 0.1 shard_map.72
  52.4 0.4 collective-permute-start.8
  52.9 1.0 %collective-permute-start.9 = (f32[4,16,1024]{2,1,0:T(8,128)S(1)}, f32[4,16,1024]{2,1,0:T(8,128)S(1)}, u32[]{:S(2)}, u32[]{:S(2)}) collective-permute-start(f32[4,16,1024]{2,1,0:T(8,128)S(1)} %get-tuple-element.61), channel_id=1, source_target_pairs={{0,240},{16,32},{32,16},{48,64},{64,48},{80,96},{96,80},{112,128},... | collective-permute-start | bytes 786440 | tf_op jit(solution)/shard_map/ppermute | solution.py:111
  53.9 0.2 shard_map.73.inner
  54.1 0.0 collective-permute-done.8.pair
  54.1 4.9 %collective-permute-done.9.chain = f32[4,16,1024]{2,1,0:T(8,128)S(1)} collective-permute-done((f32[4,16,1024]{2,1,0:T(8,128)S(1)}, f32[4,16,1024]{2,1,0:T(8,128)S(1)}, u32[]{:S(2)}, u32[]{:S(2)}) %collective-permute-start.9) | collective-permute-done | bytes 262176 | tf_op jit(solution)/shard_map/ppermute | solution.py:111
  59.0 0.4 shard_map.74
  59.4 11.7 %all_to_all.11 = f32[16,8,1024]{2,1,0:T(8,128)S(1)} all-to-all(f32[16,8,1024]{2,1,0:T(8,128)S(1)} %get-tuple-element.63), channel_id=1, replica_groups=mesh['ax'=16,'xs'=16] {'xs'}, dimensions={0} | all-to-all | bytes 1048576 | tf_op jit(solution)/shard_map/all_to_all | solution.py:379
  71.0 2.2 %shard_map.75 = (f32[8,16,1024]{2,1,0:T(8,128)S(1)}, f32[8,16,1024]{2,1,0:T(8,128)S(1)}, f32[1,16,512]{2,1,0:T(8,128)S(1)}, f32[1,16,512]{2,1,0:T(8,128)S(1)}) custom-call(f32[8,16,1024]{2,1,0:T(8,128)S(1)} %get-tuple-element.62.explicit, f32[128,1024]{1,0:T(8,128)S(1)} %bitcast.2, f32[128,256]{1,0:T(8,128)S(1)} %get-tuple-element.45.matrix, ...), custom_call_target="tpu_custom_call" | custom-call | tf_op jit(solution)/shard_map/pallas_call | solution.py:335
  73.2 3.5 %collective-permute-start.10 = (f32[1,16,512]{2,1,0:T(8,128)S(1)}, f32[1,16,512]{2,1,0:T(8,128)S(1)}, u32[]{:S(2)}, u32[]{:S(2)}) collective-permute-start(f32[1,16,512]{2,1,0:T(8,128)S(1)} %get-tuple-element.67), channel_id=1, source_target_pairs={{0,16},{16,0},{32,48},{48,32},{64,80},{80,64},{96,112},{112,96},{1... | collective-permute-start | bytes 98312 | tf_op jit(solution)/shard_map/ppermute | solution.py:105
  76.7 0.9 collective-permute-done.10.got
  77.6 1.1 %collective-permute-start.11 = (f32[1,16,512]{2,1,0:T(8,128)S(1)}, f32[1,16,512]{2,1,0:T(8,128)S(1)}, u32[]{:S(2)}, u32[]{:S(2)}) collective-permute-start(f32[1,16,512]{2,1,0:T(8,128)S(1)} %get-tuple-element.68.block), channel_id=1, source_target_pairs={{0,32},{16,48},{32,0},{48,16},{64,96},{80,112},{96,64},{112,80},{1... | collective-permute-start | bytes 98312 | tf_op jit(solution)/shard_map/ppermute | solution.py:105
  78.7 1.7 %collective-permute-done.11.got = f32[1,16,512]{2,1,0:T(8,128)S(1)} collective-permute-done((f32[1,16,512]{2,1,0:T(8,128)S(1)}, f32[1,16,512]{2,1,0:T(8,128)S(1)}, u32[]{:S(2)}, u32[]{:S(2)}) %collective-permute-start.11) | collective-permute-done | bytes 32800 | tf_op jit(solution)/shard_map/ppermute | solution.py:105
  80.4 2.7 %collective-permute-start.14 = (f32[1,16,512]{2,1,0:T(8,128)S(1)}, f32[1,16,512]{2,1,0:T(8,128)S(1)}, u32[]{:S(2)}, u32[]{:S(2)}) collective-permute-start(f32[1,16,512]{2,1,0:T(8,128)S(1)} %get-tuple-element.69), channel_id=1, source_target_pairs={{0,192},{16,208},{32,224},{48,240},{64,128},{80,144},{96,160},{112... | collective-permute-start | bytes 98312 | tf_op jit(solution)/shard_map/ppermute | solution.py:105
  83.2 1.8 %collective-permute-start.13 = (f32[1,16,512]{2,1,0:T(8,128)S(1)}, f32[1,16,512]{2,1,0:T(8,128)S(1)}, u32[]{:S(2)}, u32[]{:S(2)}) collective-permute-start(f32[1,16,512]{2,1,0:T(8,128)S(1)} %get-tuple-element.69), channel_id=1, source_target_pairs={{0,128},{16,144},{32,160},{48,176},{64,192},{80,208},{96,224},{112... | collective-permute-start | bytes 98312 | tf_op jit(solution)/shard_map/ppermute | solution.py:105
  85.0 1.2 %collective-permute-start.12 = (f32[1,16,512]{2,1,0:T(8,128)S(1)}, f32[1,16,512]{2,1,0:T(8,128)S(1)}, u32[]{:S(2)}, u32[]{:S(2)}) collective-permute-start(f32[1,16,512]{2,1,0:T(8,128)S(1)} %get-tuple-element.69), channel_id=1, source_target_pairs={{0,64},{16,80},{32,96},{48,112},{64,0},{80,16},{96,32},{112,48},{1... | collective-permute-start | bytes 98312 | tf_op jit(solution)/shard_map/ppermute | solution.py:105
  86.2 0.0 collective-permute-done.14.got3
  86.2 3.8 %collective-permute-done.13.got2 = f32[1,16,512]{2,1,0:T(8,128)S(1)} collective-permute-done((f32[1,16,512]{2,1,0:T(8,128)S(1)}, f32[1,16,512]{2,1,0:T(8,128)S(1)}, u32[]{:S(2)}, u32[]{:S(2)}) %collective-permute-start.13) | collective-permute-done | bytes 32800 | tf_op jit(solution)/shard_map/ppermute | solution.py:105
  90.0 0.0 collective-permute-done.12.got1
  90.0 2.2 %collective-permute-start.15 = (f32[16,512]{1,0:T(8,128)S(1)}, f32[16,512]{1,0:T(8,128)S(1)}, u32[]{:S(2)}, u32[]{:S(2)}) collective-permute-start(f32[16,512]{1,0:T(8,128)S(1)} %get-tuple-element.74), channel_id=1, source_target_pairs={{0,16},{16,0},{32,48},{48,32},{64,80},{80,64},{96,112},{112,96},{1... | collective-permute-start | bytes 98312 | tf_op jit(solution)/shard_map/ppermute | solution.py:105
  92.3 0.9 collective-permute-done.15.got
  93.1 0.8 shard_map.79
  (14 shorter events, 0.2 us)
Async XLA Ops:
  0.0 1.0 %copy-start.5 = (f32[8,16,1024]{2,1,0:T(8,128)S(1)}, f32[8,16,1024]{2,1,0:T(8,128)}, u32[]{:S(2)}) copy-start(f32[8,16,1024]{2,1,0:T(8,128)} %field.3) | copy-start | bytes 1572868
  1.1 7.2 %collective-permute-start = (f32[4,16,1024]{2,1,0:T(8,128)S(1)}, f32[4,16,1024]{2,1,0:T(8,128)S(1)}, u32[]{:S(2)}, u32[]{:S(2)}) collective-permute-start(f32[4,16,1024]{2,1,0:T(8,128)S(1)} %get-tuple-element.40), channel_id=1, source_target_pairs={{0,16},{16,0},{32,48},{48,32},{64,80},{80,64},{96,112},{112,96},{1... | collective-permute-start | bytes 786440 | tf_op jit(solution)/shard_map/ppermute | solution.py:105
  4.4 6.1 %collective-permute-start.1 = (f32[4,16,1024]{2,1,0:T(8,128)S(1)}, f32[4,16,1024]{2,1,0:T(8,128)S(1)}, u32[]{:S(2)}, u32[]{:S(2)}) collective-permute-start(f32[4,16,1024]{2,1,0:T(8,128)S(1)} %get-tuple-element.41), channel_id=1, source_target_pairs={{0,240},{16,32},{32,16},{48,64},{64,48},{80,96},{96,80},{112,128},... | collective-permute-start | bytes 786440 | tf_op jit(solution)/shard_map/ppermute | solution.py:111
  4.7 1.7 %copy-start.1 = (f32[16,144,256]{2,1,0:T(8,128)S(1)}, f32[16,144,256]{2,1,0:T(8,128)}, u32[]{:S(2)}) copy-start(f32[16,144,256]{2,1,0:T(8,128)} %constant.7.clone.radial) | copy-start | bytes 7077892
  6.3 1.6 %copy-start.4 = (f32[16,16,2048]{2,1,0:T(8,128)S(1)}, f32[16,16,2048]{2,1,0:T(8,128)}, u32[]{:S(2)}) copy-start(f32[16,16,2048]{2,1,0:T(8,128)} %constant.8.clone.damping) | copy-start | bytes 6291460
  7.9 16.6 %copy-start.2 = (f32[8,16,1024]{2,1,0:T(8,128)S(1)}, f32[8,16,1024]{2,1,0:T(8,128)}, u32[]{:S(2)}) copy-start(f32[8,16,1024]{2,1,0:T(8,128)} %axial_rate.3) | copy-start | bytes 1572868
  7.9 16.6 %copy-start.3 = (f32[8,16,1024]{2,1,0:T(8,128)S(1)}, f32[8,16,1024]{2,1,0:T(8,128)}, u32[]{:S(2)}) copy-start(f32[8,16,1024]{2,1,0:T(8,128)} %swirl_rate.3) | copy-start | bytes 1572868
  8.3 16.2 %copy-start = (bf16[2,2,512,512]{3,2,1,0:T(8,128)(2,1)S(1)}, bf16[2,2,512,512]{3,2,1,0:T(8,128)(2,1)}, u32[]{:S(2)}) copy-start(bf16[2,2,512,512]{3,2,1,0:T(8,128)(2,1)} %constant.6.clone.azimuth) | copy-start | bytes 6291460
  26.7 6.7 %collective-permute-start.2 = (f32[2,16,512]{2,1,0:T(8,128)S(1)}, f32[2,16,512]{2,1,0:T(8,128)S(1)}, u32[]{:S(2)}, u32[]{:S(2)}) collective-permute-start(f32[2,16,512]{2,1,0:T(8,128)S(1)} %get-tuple-element.50), channel_id=1, source_target_pairs={{0,16},{16,0},{32,48},{48,32},{64,80},{80,64},{96,112},{112,96},{1... | collective-permute-start | bytes 196616 | tf_op jit(solution)/shard_map/ppermute | solution.py:105
  33.4 3.2 %collective-permute-start.3 = (f32[2,16,512]{2,1,0:T(8,128)S(1)}, f32[2,16,512]{2,1,0:T(8,128)S(1)}, u32[]{:S(2)}, u32[]{:S(2)}) collective-permute-start(f32[2,16,512]{2,1,0:T(8,128)S(1)} %get-tuple-element.51.block), channel_id=1, source_target_pairs={{0,32},{16,48},{32,0},{48,16},{64,96},{80,112},{96,64},{112,80},{1... | collective-permute-start | bytes 196616 | tf_op jit(solution)/shard_map/ppermute | solution.py:105
  36.6 6.0 %collective-permute-start.6 = (f32[2,16,512]{2,1,0:T(8,128)S(1)}, f32[2,16,512]{2,1,0:T(8,128)S(1)}, u32[]{:S(2)}, u32[]{:S(2)}) collective-permute-start(f32[2,16,512]{2,1,0:T(8,128)S(1)} %get-tuple-element.52), channel_id=1, source_target_pairs={{0,192},{16,208},{32,224},{48,240},{64,128},{80,144},{96,160},{112... | collective-permute-start | bytes 196616 | tf_op jit(solution)/shard_map/ppermute | solution.py:105
  40.5 8.2 %collective-permute-start.5 = (f32[2,16,512]{2,1,0:T(8,128)S(1)}, f32[2,16,512]{2,1,0:T(8,128)S(1)}, u32[]{:S(2)}, u32[]{:S(2)}) collective-permute-start(f32[2,16,512]{2,1,0:T(8,128)S(1)} %get-tuple-element.52), channel_id=1, source_target_pairs={{0,128},{16,144},{32,160},{48,176},{64,192},{80,208},{96,224},{112... | collective-permute-start | bytes 196616 | tf_op jit(solution)/shard_map/ppermute | solution.py:105
  42.1 8.2 %collective-permute-start.4 = (f32[2,16,512]{2,1,0:T(8,128)S(1)}, f32[2,16,512]{2,1,0:T(8,128)S(1)}, u32[]{:S(2)}, u32[]{:S(2)}) collective-permute-start(f32[2,16,512]{2,1,0:T(8,128)S(1)} %get-tuple-element.52), channel_id=1, source_target_pairs={{0,64},{16,80},{32,96},{48,112},{64,0},{80,16},{96,32},{112,48},{1... | collective-permute-start | bytes 196616 | tf_op jit(solution)/shard_map/ppermute | solution.py:105
  50.3 2.0 %collective-permute-start.7 = (f32[16,512]{1,0:T(8,128)S(1)}, f32[16,512]{1,0:T(8,128)S(1)}, u32[]{:S(2)}, u32[]{:S(2)}) collective-permute-start(f32[16,512]{1,0:T(8,128)S(1)} %get-tuple-element.58), channel_id=1, source_target_pairs={{0,16},{16,0},{32,48},{48,32},{64,80},{80,64},{96,112},{112,96},{1... | collective-permute-start | bytes 98312 | tf_op jit(solution)/shard_map/ppermute | solution.py:105
  52.4 1.7 %collective-permute-start.8 = (f32[4,16,1024]{2,1,0:T(8,128)S(1)}, f32[4,16,1024]{2,1,0:T(8,128)S(1)}, u32[]{:S(2)}, u32[]{:S(2)}) collective-permute-start(f32[4,16,1024]{2,1,0:T(8,128)S(1)} %get-tuple-element.60), channel_id=1, source_target_pairs={{0,16},{16,0},{32,48},{48,32},{64,80},{80,64},{96,112},{112,96},{1... | collective-permute-start | bytes 786440 | tf_op jit(solution)/shard_map/ppermute | solution.py:105
  52.9 6.1 %collective-permute-start.9 = (f32[4,16,1024]{2,1,0:T(8,128)S(1)}, f32[4,16,1024]{2,1,0:T(8,128)S(1)}, u32[]{:S(2)}, u32[]{:S(2)}) collective-permute-start(f32[4,16,1024]{2,1,0:T(8,128)S(1)} %get-tuple-element.61), channel_id=1, source_target_pairs={{0,240},{16,32},{32,16},{48,64},{64,48},{80,96},{96,80},{112,128},... | collective-permute-start | bytes 786440 | tf_op jit(solution)/shard_map/ppermute | solution.py:111
  73.2 4.3 %collective-permute-start.10 = (f32[1,16,512]{2,1,0:T(8,128)S(1)}, f32[1,16,512]{2,1,0:T(8,128)S(1)}, u32[]{:S(2)}, u32[]{:S(2)}) collective-permute-start(f32[1,16,512]{2,1,0:T(8,128)S(1)} %get-tuple-element.67), channel_id=1, source_target_pairs={{0,16},{16,0},{32,48},{48,32},{64,80},{80,64},{96,112},{112,96},{1... | collective-permute-start | bytes 98312 | tf_op jit(solution)/shard_map/ppermute | solution.py:105
  77.6 2.9 %collective-permute-start.11 = (f32[1,16,512]{2,1,0:T(8,128)S(1)}, f32[1,16,512]{2,1,0:T(8,128)S(1)}, u32[]{:S(2)}, u32[]{:S(2)}) collective-permute-start(f32[1,16,512]{2,1,0:T(8,128)S(1)} %get-tuple-element.68.block), channel_id=1, source_target_pairs={{0,32},{16,48},{32,0},{48,16},{64,96},{80,112},{96,64},{112,80},{1... | collective-permute-start | bytes 98312 | tf_op jit(solution)/shard_map/ppermute | solution.py:105
  80.4 5.7 %collective-permute-start.14 = (f32[1,16,512]{2,1,0:T(8,128)S(1)}, f32[1,16,512]{2,1,0:T(8,128)S(1)}, u32[]{:S(2)}, u32[]{:S(2)}) collective-permute-start(f32[1,16,512]{2,1,0:T(8,128)S(1)} %get-tuple-element.69), channel_id=1, source_target_pairs={{0,192},{16,208},{32,224},{48,240},{64,128},{80,144},{96,160},{112... | collective-permute-start | bytes 98312 | tf_op jit(solution)/shard_map/ppermute | solution.py:105
  83.2 6.8 %collective-permute-start.13 = (f32[1,16,512]{2,1,0:T(8,128)S(1)}, f32[1,16,512]{2,1,0:T(8,128)S(1)}, u32[]{:S(2)}, u32[]{:S(2)}) collective-permute-start(f32[1,16,512]{2,1,0:T(8,128)S(1)} %get-tuple-element.69), channel_id=1, source_target_pairs={{0,128},{16,144},{32,160},{48,176},{64,192},{80,208},{96,224},{112... | collective-permute-start | bytes 98312 | tf_op jit(solution)/shard_map/ppermute | solution.py:105
  85.0 5.0 %collective-permute-start.12 = (f32[1,16,512]{2,1,0:T(8,128)S(1)}, f32[1,16,512]{2,1,0:T(8,128)S(1)}, u32[]{:S(2)}, u32[]{:S(2)}) collective-permute-start(f32[1,16,512]{2,1,0:T(8,128)S(1)} %get-tuple-element.69), channel_id=1, source_target_pairs={{0,64},{16,80},{32,96},{48,112},{64,0},{80,16},{96,32},{112,48},{1... | collective-permute-start | bytes 98312 | tf_op jit(solution)/shard_map/ppermute | solution.py:105
  90.0 3.1 %collective-permute-start.15 = (f32[16,512]{1,0:T(8,128)S(1)}, f32[16,512]{1,0:T(8,128)S(1)}, u32[]{:S(2)}, u32[]{:S(2)}) collective-permute-start(f32[16,512]{1,0:T(8,128)S(1)} %get-tuple-element.74), channel_id=1, source_target_pairs={{0,16},{16,0},{32,48},{48,32},{64,80},{80,64},{96,112},{112,96},{1... | collective-permute-start | bytes 98312 | tf_op jit(solution)/shard_map/ppermute | solution.py:105

commit v4 on v3

--- a/solution.py
+++ b/solution.py
@@ -26,6 +26,7 @@
     -1.0 / 560.0,
 )
 HALO = 4
+FAR = ((7, 1), (3, 7), (5, 2), (4, 6))
 
 
 def split_bf16(table):
@@ -105,6 +106,11 @@
     return lax.ppermute(value, "ax", [(i, i ^ mask) for i in range(count)])
 
 
+def far_swap(value, masks):
+    count = lax.axis_size("ax")
+    return lax.ppermute(value, "ax", [(i, i ^ 2 * masks[1 - i % 2]) for i in range(count)])
+
+
 def chain_swap(value):
     count = lax.axis_size("ax")
     pairs = [(i, (i + 1) % count if i % 2 else (i - 1) % count) for i in range(count)]
@@ -191,7 +197,7 @@
     partial,
     decay,
     mine,
-    other,
+    other=None,
 ):
     planes, rows, points = partial.shape
     half = points // 2
@@ -223,6 +229,9 @@
             fade = factor if plane == 0 else factor * fade
             partial[plane, :, where] = value
             decay[plane, :, where] = fade
+        if other is None:
+            mine[:, where] = value
+            continue
         is_mine = lax.axis_index("ax") % 2 == side
         for index, last in enumerate((value, fade)[: mine.shape[0]]):
 
@@ -244,53 +253,73 @@
         chain[j] = jnp.where(odd, high, low)
 
 
-def chip_kernel(mine, got, *refs):
+def chip_kernel(mine, got, block, behind, spans):
     odd = lax.axis_index("ax") % 2 == 1
     value0, value1 = jnp.where(odd, got[0], mine[0]), jnp.where(odd, mine[0], got[0])
-    if mine.shape[0] == 2:
-        block, behind, spans = refs
-        span0, span1 = jnp.where(odd, got[1], mine[1]), jnp.where(odd, mine[1], got[1])
-        block[1] = span0 * span1
-        spans[0], spans[1] = span0, span1
-    else:
-        spans, block, behind = refs
-        span1 = spans[1]
+    span0, span1 = jnp.where(odd, got[1], mine[1]), jnp.where(odd, mine[1], got[1])
     block[0] = value1 + span1 * value0
+    block[1] = span0 * span1
     behind[...] = value0
-
-
-def couple_kernel(block, got, *refs):
+    spans[0], spans[1] = span0, span1
+
+
+def couple_kernel(block, got, joint, prefix, before):
     upper = (lax.axis_index("ax") // 2) % 2 == 1
-    if block.shape[0] == 2:
-        joint, prefix, gains = refs
-        joint[1] = block[1] * got[1]
-        gains[0] = jnp.where(upper, 1.0, got[1])
-        gains[1] = jnp.where(upper, block[1], 1.0)
-        gains[2] = jnp.where(upper, got[1], 1.0)
-    else:
-        gains, joint, prefix = refs
-    joint[0] = gains[0] * block[0] + gains[1] * got[0]
+    keep = jnp.where(upper, 1.0, got[1])
+    take = jnp.where(upper, block[1], 1.0)
+    joint[0] = keep * block[0] + take * got[0]
+    joint[1] = block[1] * got[1]
     prefix[...] = jnp.where(upper, got[0], 0.0)
-
-
-def enter_kernel(got1, got2, got3, prefix, behind, spans, gains, *refs):
+    before[...] = jnp.where(upper, got[1], 1.0)
+
+
+def enter_kernel(got1, got2, got3, prefix, before, behind, spans, mine, packed):
     place = lax.axis_index("ax")
     odd = place % 2 == 1
     quad = place // 4
-    if got1.shape[0] == 2:
-        mine, other, weights = refs
-        before = gains[2]
-        weights[0] = jnp.where(quad % 2 == 1, before, 0.0)
-        weights[1] = before * jnp.where(quad == 2, got3[1], jnp.where(quad == 3, got1[1], 0.0))
-        weights[2] = before * jnp.where(
-            quad == 2, 1.0, jnp.where(quad == 3, got1[1] * got2[1], 0.0)
-        )
-    else:
-        weights, mine, other = refs
-    into0 = prefix[...] + weights[0] * got1[0] + weights[1] * got2[0] + weights[2] * got3[0]
+    near = before[...]
+    weight1 = jnp.where(quad % 2 == 1, near, 0.0)
+    weight2 = near * jnp.where(quad == 2, got3[1], jnp.where(quad == 3, got1[1], 0.0))
+    weight3 = near * jnp.where(quad == 2, 1.0, jnp.where(quad == 3, got1[1] * got2[1], 0.0))
+    into0 = prefix[...] + weight1 * got1[0] + weight2 * got2[0] + weight3 * got3[0]
     into1 = spans[0] * into0 + behind[...]
     mine[...] = jnp.where(odd, into1, into0)
-    other[...] = jnp.where(odd, into0, into1)
+    packed[0] = jnp.where(odd, into0, into1)
+    start = near * jnp.where(quad % 2 == 1, got1[1], 1.0)
+    start = start * jnp.where(quad >= 2, got2[1] * got3[1], 1.0)
+    packed[1] = start
+    packed[2] = 1.0 / (start * (spans[0] * spans[1]))
+    packed[3], packed[4] = spans[0], spans[1]
+
+
+def widen_kernel(packed, got, scales):
+    half = packed.shape[2]
+    odd = lax.axis_index("ax") % 2 == 1
+    for index in range(scales.shape[0]):
+        for side in range(2):
+            own = odd == (side == 1)
+            value = jnp.where(own, packed[index + 1], got[index + 1])
+            scales[index, :, side * half : (side + 1) * half] = value
+
+
+def chip_again_kernel(total, got, scales, sent):
+    odd = lax.axis_index("ax") % 2 == 1
+    value0 = jnp.where(odd, got[...], total[...])
+    value1 = jnp.where(odd, total[...], got[...])
+    sent[...] = (value1 + scales[3] * value0) * scales[1]
+
+
+def gather_kernel(far0, far1, far2, far3, below):
+    place = lax.axis_index("ax")
+    odd = place % 2 == 1
+    chip = place // 2
+    total = jnp.zeros_like(below)
+    for far, (mask1, mask0) in zip((far0, far1, far2, far3), FAR):
+        take = chip ^ jnp.where(odd, mask1, mask0) < chip
+        if mask0 == FAR[0][0]:
+            take = jnp.logical_and(take, odd)
+        total = total + jnp.where(take, far[...], 0.0)
+    below[...] = total
 
 
 def finish_kernel(partial, decay, mine, got, field, pair, chain):
@@ -299,7 +328,7 @@
     odd = lax.axis_index("ax") % 2 == 1
     for side in range(2):
         where = slice(side * half, (side + 1) * half)
-        incoming = jnp.where(odd == (side == 1), mine[...], got[...])
+        incoming = jnp.where(odd == (side == 1), mine[...], got[0])
         ends = {}
         for plane in range(planes):
             value = partial[plane, :, where] + decay[plane, :, where] * incoming
@@ -311,17 +340,15 @@
             chain[j, :, where] = jnp.where(odd, high, low)
 
 
-def last_kernel(partial, decay, mine, got, out, field, sems):
-    planes, rows, points = partial.shape
-    half = points // 2
-    odd = lax.axis_index("ax") % 2 == 1
-    incoming = [jnp.where(odd == (side == 1), mine[...], got[...]) for side in range(2)]
+def last_kernel(partial, decay, below, got, total, before, scales, out, field, sems):
+    planes = partial.shape[0]
+    odd = lax.axis_index("ax") % 2 == 1
+    into0 = scales[0] * (below[...] + got[...])
+    value0 = jnp.where(odd, before[...], total[...])
+    incoming = jnp.where(odd, scales[2] * into0 + value0, into0)
     copies = []
     for plane in range(planes):
-        for side in range(2):
-            where = slice(side * half, (side + 1) * half)
-            value = partial[plane, :, where] + decay[plane, :, where] * incoming[side]
-            field[plane, :, where] = value
+        field[plane] = partial[plane] + decay[plane] * incoming
         if plane % 2 == 1:
             pair = pl.ds(plane - 1, 2)
             copy = pltpu.make_async_copy(field.at[pair], out.at[pair], sems.at[plane // 2])
@@ -378,10 +405,10 @@
         )
         got = lax.all_to_all(sent, "xs", split_axis=0, concat_axis=0, tiled=True)
         first = substep == 0
-        parts = shape(2 if first else 1, rows, half)
-        partial, decay, mine, other = call(
+        parts, plane = shape(2, rows, half), shape(rows, points)
+        partial, decay, *sides = call(
             middle_kernel,
-            (block, block, parts, parts),
+            (block, block, parts, parts) if first else (block, block, plane),
             explicit,
             got.reshape(groups * planes, points),
             matrix,
@@ -391,41 +418,40 @@
             swirl_rate,
             vmem=16,
         )
-        got = swap(other, 1)
         if first:
-            value, behind, spans = call(chip_kernel, (parts, one, parts), mine, got)
-        else:
-            value, behind = call(chip_kernel, (parts, one), mine, got, spans)
-        got = swap(value, 2)
-        if first:
-            out = (parts, one, shape(3, rows, half))
-            value, prefix, gains = call(couple_kernel, out, value, got)
-        else:
-            value, prefix = call(couple_kernel, (parts, one), value, got, gains)
-        far3, far2, far1 = swap(value, 12), swap(value, 8), swap(value, 4)
-        args = (far1, far2, far3, prefix, behind, spans, gains)
-        if first:
-            mine, other, weights = call(enter_kernel, (one, one, shape(3, rows, half)), *args)
-        else:
-            mine, other = call(enter_kernel, (one, one), *args, weights)
-        got = swap(other, 1)
-        if substep < SUBSTEPS - 1:
+            mine, other = sides
+            out = (parts, one, parts)
+            value, behind, spans = call(chip_kernel, out, mine, swap(other, 1))
+            value, prefix, before = call(couple_kernel, (parts, one, one), value, swap(value, 2))
+            far3, far2, far1 = swap(value, 12), swap(value, 8), swap(value, 4)
+            out = (one, shape(5, rows, half))
+            mine, packed = call(
+                enter_kernel, out, far1, far2, far3, prefix, before, behind, spans
+            )
+            got = swap(packed, 1)
             field, pair_end, chain_end = call(
                 finish_kernel, (block, ends, ends), partial, decay, mine, got
             )
             chain, pair = chain_swap(chain_end), swap(pair_end, 1)
             inner = call(inner_kernel, block, field)
+            scales = call(widen_kernel, shape(4, rows, points), packed, got)
+        else:
+            (total,) = sides
+            before = swap(total, 1)
+            sent = call(chip_again_kernel, plane, total, before, scales)
+            below = call(gather_kernel, plane, *(far_swap(sent, masks) for masks in FAR))
+            got = swap(below, 1)
     return pl.pallas_call(
         last_kernel,
         out_shape=block,
-        in_specs=[pl.BlockSpec(memory_space=pltpu.VMEM)] * 4,
+        in_specs=[pl.BlockSpec(memory_space=pltpu.VMEM)] * 7,
         out_specs=pl.BlockSpec(memory_space=pl.ANY),
         scratch_shapes=[
             pltpu.VMEM((planes, rows, points), jnp.float32),
             pltpu.SemaphoreType.DMA((planes // 2,)),
         ],
         compiler_params=pltpu.CompilerParams(vmem_limit_bytes=4 * 1024 * 1024),
-    )(partial, decay, mine, got)
+    )(partial, decay, below, got, total, before, scales)
 
 
 def solution(mesh):

time: 94.2 us -> 92.8 us (0.985)
  starting transfers between devices: 30.4 us -> 28.7 us
    ppermute x14 -> x10, starting transfers between devices: 29.4 us -> 19.6 us  [swap(): return lax.ppermute(value, 'ax', [(i, i ^ mask) for i in range(count)])]
    ppermute x0 -> x4, starting transfers between devices: none -> 8.11 us  [far_swap(): lax.ppermute(value, 'ax', [(i, i ^ 2 * masks[1 - i % 2]) for i in range(c...]
    ppermute x14 -> x10, waiting for transfers between devices: 19.8 us -> 14.8 us  [swap(): return lax.ppermute(value, 'ax', [(i, i ^ mask) for i in range(count)])]
    ppermute x0 -> x4, waiting for transfers between devices: none -> 4.39 us  [far_swap(): lax.ppermute(value, 'ax', [(i, i ^ 2 * masks[1 - i % 2]) for i in range(c...]
where the time goes in v4:
time: 92.8 us; the launch traced here: 92.6 us
  starting transfers between devices  28.7 us (31%)
  waiting for transfers between devices  26.2 us (28%)
  blocking collectives  26 us (28%)
  Pallas kernels  7.11 us (8%)
  local copies, waits for them, and re-layouts  4.31 us (5%)
    all_to_all x2, blocking collectives, body(): got = lax.all_to_all(sent, 'xs', split_axis=0, concat_axis=0, tiled=True)  26 us
    ppermute x10, starting transfers between devices, swap(): return lax.ppermute(value, 'ax', [(i, i ^ mask) for i in range(count)])  19.6 us
    ppermute x10, waiting for transfers between devices, swap(): return lax.ppermute(value, 'ax', [(i, i ^ mask) for i in range(count)])  14.8 us
    ppermute x4, starting transfers between devices, far_swap(): lax.ppermute(value, 'ax', [(i, i ^ 2 * masks[1 - i % 2]) for i in range(c...  8.11 us
    ppermute x2, waiting for transfers between devices, chain_swap(): return lax.ppermute(value, 'ax', pairs)  7.09 us
    pallas_call x14, Pallas kernels, call(): pl.pallas_call(kernel, out_shape=out_shape, in_specs=[pl.BlockSpec(memory...  5.9 us
    ppermute x4, waiting for transfers between devices, far_swap(): lax.ppermute(value, 'ax', [(i, i ^ 2 * masks[1 - i % 2]) for i in range(c...  4.39 us
    unnamed x12, local copies, waits for them, and re-layouts  4.31 us
  transfers between devices with their start and end apart: 16, of which 11 were waited for; matrix products, arithmetic and copies ran while one was open for 0% of the time, Pallas kernels for 1%

profile of v4, /device:TPU:1, one launch (start us, length us, event | category | flops | bytes accessed | tf_op | source)
XLA Modules:
  0.0 92.6 jit_solution(13213281498403941434)
XLA Ops:
  0.0 1.0 %copy-done.5 = f32[8,16,1024]{2,1,0:T(8,128)S(1)} copy-done((f32[8,16,1024]{2,1,0:T(8,128)S(1)}, f32[8,16,1024]{2,1,0:T(8,128)}, u32[]{:S(2)}) %copy-start.5) | copy-done | bytes 524312
  1.1 3.3 %collective-permute-start = (f32[4,16,1024]{2,1,0:T(8,128)S(1)}, f32[4,16,1024]{2,1,0:T(8,128)S(1)}, u32[]{:S(2)}, u32[]{:S(2)}) collective-permute-start(f32[4,16,1024]{2,1,0:T(8,128)S(1)} %get-tuple-element.32), channel_id=1, source_target_pairs={{0,16},{16,0},{32,48},{48,32},{64,80},{80,64},{96,112},{112,96},{1... | collective-permute-start | bytes 786440 | tf_op jit(solution)/shard_map/ppermute | solution.py:106
  4.4 0.0 collective-permute-start.1
  4.4 0.2 shard_map.64.inner
  4.7 0.0 copy-start.1
  4.7 1.7 %copy-done.1 = f32[16,144,256]{2,1,0:T(8,128)S(1)} copy-done((f32[16,144,256]{2,1,0:T(8,128)S(1)}, f32[16,144,256]{2,1,0:T(8,128)}, u32[]{:S(2)}) %copy-start.1) | copy-done | bytes 2359320
  6.3 1.6 %copy-done.4 = f32[16,16,2048]{2,1,0:T(8,128)S(1)} copy-done((f32[16,16,2048]{2,1,0:T(8,128)S(1)}, f32[16,16,2048]{2,1,0:T(8,128)}, u32[]{:S(2)}) %copy-start.4) | copy-done | bytes 2097176
  7.9 0.4 shard_map.66
  8.3 0.0 copy-start
  8.3 0.0 collective-permute-done.pair
  8.3 2.2 %collective-permute-done.1.chain = f32[4,16,1024]{2,1,0:T(8,128)S(1)} collective-permute-done((f32[4,16,1024]{2,1,0:T(8,128)S(1)}, f32[4,16,1024]{2,1,0:T(8,128)S(1)}, u32[]{:S(2)}, u32[]{:S(2)}) %collective-permute-start.1) | collective-permute-done | bytes 262176 | tf_op jit(solution)/shard_map/ppermute | solution.py:117
  10.5 0.4 shard_map.67
  10.9 13.6 %all_to_all.10 = f32[16,8,1024]{2,1,0:T(8,128)S(1)} all-to-all(f32[16,8,1024]{2,1,0:T(8,128)S(1)} %get-tuple-element.36), channel_id=1, replica_groups=mesh['ax'=16,'xs'=16] {'xs'}, dimensions={0} | all-to-all | bytes 1048576 | tf_op jit(solution)/shard_map/all_to_all | solution.py:406
  24.5 2.2 %shard_map.68 = (f32[8,16,1024]{2,1,0:T(8,128)S(1)}, f32[8,16,1024]{2,1,0:T(8,128)S(1)}, f32[2,16,512]{2,1,0:T(8,128)S(1)}, f32[2,16,512]{2,1,0:T(8,128)S(1)}) custom-call(f32[8,16,1024]{2,1,0:T(8,128)S(1)} %get-tuple-element.35.explicit, f32[128,1024]{1,0:T(8,128)S(1)} %bitcast.3, f32[128,256]{1,0:T(8,128)S(1)} %get-tuple-element.37.matrix, ...), custom_call_target="tpu_custom_call" | custom-call | tf_op jit(solution)/shard_map/pallas_call | solution.py:362
  26.7 5.8 %collective-permute-start.2 = (f32[2,16,512]{2,1,0:T(8,128)S(1)}, f32[2,16,512]{2,1,0:T(8,128)S(1)}, u32[]{:S(2)}, u32[]{:S(2)}) collective-permute-start(f32[2,16,512]{2,1,0:T(8,128)S(1)} %get-tuple-element.42), channel_id=1, source_target_pairs={{0,16},{16,0},{32,48},{48,32},{64,80},{80,64},{96,112},{112,96},{1... | collective-permute-start | bytes 196616 | tf_op jit(solution)/shard_map/ppermute | solution.py:106
  32.5 0.9 collective-permute-done.2.got
  33.4 0.1 collective-permute-start.3
  33.5 3.1 %collective-permute-done.3.got = f32[2,16,512]{2,1,0:T(8,128)S(1)} collective-permute-done((f32[2,16,512]{2,1,0:T(8,128)S(1)}, f32[2,16,512]{2,1,0:T(8,128)S(1)}, u32[]{:S(2)}, u32[]{:S(2)}) %collective-permute-start.3) | collective-permute-done | bytes 65568 | tf_op jit(solution)/shard_map/ppermute | solution.py:106
  36.6 3.8 %collective-permute-start.6 = (f32[2,16,512]{2,1,0:T(8,128)S(1)}, f32[2,16,512]{2,1,0:T(8,128)S(1)}, u32[]{:S(2)}, u32[]{:S(2)}) collective-permute-start(f32[2,16,512]{2,1,0:T(8,128)S(1)} %get-tuple-element.44), channel_id=1, source_target_pairs={{0,192},{16,208},{32,224},{48,240},{64,128},{80,144},{96,160},{112... | collective-permute-start | bytes 196616 | tf_op jit(solution)/shard_map/ppermute | solution.py:106
  40.5 1.6 %collective-permute-start.5 = (f32[2,16,512]{2,1,0:T(8,128)S(1)}, f32[2,16,512]{2,1,0:T(8,128)S(1)}, u32[]{:S(2)}, u32[]{:S(2)}) collective-permute-start(f32[2,16,512]{2,1,0:T(8,128)S(1)} %get-tuple-element.44), channel_id=1, source_target_pairs={{0,128},{16,144},{32,160},{48,176},{64,192},{80,208},{96,224},{112... | collective-permute-start | bytes 196616 | tf_op jit(solution)/shard_map/ppermute | solution.py:106
  42.1 0.6 collective-permute-start.4
  42.6 0.0 collective-permute-done.6.got3
  42.6 6.0 %collective-permute-done.5.got2 = f32[2,16,512]{2,1,0:T(8,128)S(1)} collective-permute-done((f32[2,16,512]{2,1,0:T(8,128)S(1)}, f32[2,16,512]{2,1,0:T(8,128)S(1)}, u32[]{:S(2)}, u32[]{:S(2)}) %collective-permute-start.5) | collective-permute-done | bytes 65568 | tf_op jit(solution)/shard_map/ppermute | solution.py:106
  48.6 1.6 %collective-permute-done.4.got1 = f32[2,16,512]{2,1,0:T(8,128)S(1)} collective-permute-done((f32[2,16,512]{2,1,0:T(8,128)S(1)}, f32[2,16,512]{2,1,0:T(8,128)S(1)}, u32[]{:S(2)}, u32[]{:S(2)}) %collective-permute-start.4) | collective-permute-done | bytes 65568 | tf_op jit(solution)/shard_map/ppermute | solution.py:106
  50.3 0.1 shard_map.71
  50.3 1.2 %collective-permute-start.7 = (f32[5,16,512]{2,1,0:T(8,128)S(1)}, f32[5,16,512]{2,1,0:T(8,128)S(1)}, u32[]{:S(2)}, u32[]{:S(2)}) collective-permute-start(f32[5,16,512]{2,1,0:T(8,128)S(1)} %get-tuple-element.50.packed), channel_id=1, source_target_pairs={{0,16},{16,0},{32,48},{48,32},{64,80},{80,64},{96,112},{112,96},{1... | collective-permute-start | bytes 491528 | tf_op jit(solution)/shard_map/ppermute | solution.py:106
  51.5 1.0 %collective-permute-done.7.got = f32[5,16,512]{2,1,0:T(8,128)S(1)} collective-permute-done((f32[5,16,512]{2,1,0:T(8,128)S(1)}, f32[5,16,512]{2,1,0:T(8,128)S(1)}, u32[]{:S(2)}, u32[]{:S(2)}) %collective-permute-start.7) | collective-permute-done | bytes 163872 | tf_op jit(solution)/shard_map/ppermute | solution.py:106
  52.5 0.1 shard_map.72
  52.6 0.5 collective-permute-start.8
  53.1 1.0 %collective-permute-start.9 = (f32[4,16,1024]{2,1,0:T(8,128)S(1)}, f32[4,16,1024]{2,1,0:T(8,128)S(1)}, u32[]{:S(2)}, u32[]{:S(2)}) collective-permute-start(f32[4,16,1024]{2,1,0:T(8,128)S(1)} %get-tuple-element.53), channel_id=1, source_target_pairs={{0,240},{16,32},{32,16},{48,64},{64,48},{80,96},{96,80},{112,128},... | collective-permute-start | bytes 786440 | tf_op jit(solution)/shard_map/ppermute | solution.py:117
  54.0 0.2 shard_map.73.inner
  54.3 0.0 collective-permute-done.8.pair
  54.3 4.9 %collective-permute-done.9.chain = f32[4,16,1024]{2,1,0:T(8,128)S(1)} collective-permute-done((f32[4,16,1024]{2,1,0:T(8,128)S(1)}, f32[4,16,1024]{2,1,0:T(8,128)S(1)}, u32[]{:S(2)}, u32[]{:S(2)}) %collective-permute-start.9) | collective-permute-done | bytes 262176 | tf_op jit(solution)/shard_map/ppermute | solution.py:117
  59.2 0.4 shard_map.74
  59.6 12.5 %all_to_all.11 = f32[16,8,1024]{2,1,0:T(8,128)S(1)} all-to-all(f32[16,8,1024]{2,1,0:T(8,128)S(1)} %get-tuple-element.55), channel_id=1, replica_groups=mesh['ax'=16,'xs'=16] {'xs'}, dimensions={0} | all-to-all | bytes 1048576 | tf_op jit(solution)/shard_map/all_to_all | solution.py:406
  72.0 2.1 %shard_map.75 = (f32[8,16,1024]{2,1,0:T(8,128)S(1)}, f32[8,16,1024]{2,1,0:T(8,128)S(1)}, f32[16,1024]{1,0:T(8,128)S(1)}) custom-call(f32[8,16,1024]{2,1,0:T(8,128)S(1)} %get-tuple-element.54.explicit, f32[128,1024]{1,0:T(8,128)S(1)} %bitcast.2, f32[128,256]{1,0:T(8,128)S(1)} %get-tuple-element.37.matrix, bf16[2,2,512,512]{3,2,1,0:T(8,128)(2,1)S(1)} %copy-done, ...), custom_call_target="tpu_custom_call" | custom-call | tf_op jit(solution)/shard_map/pallas_call | solution.py:362
  74.2 2.7 %collective-permute-start.10 = (f32[16,1024]{1,0:T(8,128)S(1)}, f32[16,1024]{1,0:T(8,128)S(1)}, u32[]{:S(2)}, u32[]{:S(2)}) collective-permute-start(f32[16,1024]{1,0:T(8,128)S(1)} %get-tuple-element.58.total), channel_id=1, source_target_pairs={{0,16},{16,0},{32,48},{48,32},{64,80},{80,64},{96,112},{112,96},{1... | collective-permute-start | bytes 196616 | tf_op jit(solution)/shard_map/ppermute | solution.py:106
  76.9 0.9 collective-permute-done.10.got.before
  77.8 4.1 %collective-permute-start.14 = (f32[16,1024]{1,0:T(8,128)S(1)}, f32[16,1024]{1,0:T(8,128)S(1)}, u32[]{:S(2)}, u32[]{:S(2)}) collective-permute-start(f32[16,1024]{1,0:T(8,128)S(1)} %shard_map.77), channel_id=1, source_target_pairs={{0,192},{16,144},{32,224},{48,176},{64,128},{80,208},{96,160},{112... | collective-permute-start | bytes 196616 | tf_op jit(solution)/shard_map/ppermute | solution.py:111
  81.9 1.2 %collective-permute-start.13 = (f32[16,1024]{1,0:T(8,128)S(1)}, f32[16,1024]{1,0:T(8,128)S(1)}, u32[]{:S(2)}, u32[]{:S(2)}) collective-permute-start(f32[16,1024]{1,0:T(8,128)S(1)} %shard_map.77), channel_id=1, source_target_pairs={{0,64},{16,176},{32,96},{48,144},{64,0},{80,240},{96,32},{112,208}... | collective-permute-start | bytes 196616 | tf_op jit(solution)/shard_map/ppermute | solution.py:111
  83.1 1.4 %collective-permute-start.12 = (f32[16,1024]{1,0:T(8,128)S(1)}, f32[16,1024]{1,0:T(8,128)S(1)}, u32[]{:S(2)}, u32[]{:S(2)}) collective-permute-start(f32[16,1024]{1,0:T(8,128)S(1)} %shard_map.77), channel_id=1, source_target_pairs={{0,224},{16,112},{32,192},{48,80},{64,160},{80,48},{96,128},{112,1... | collective-permute-start | bytes 196616 | tf_op jit(solution)/shard_map/ppermute | solution.py:111
  84.4 1.5 %collective-permute-start.11 = (f32[16,1024]{1,0:T(8,128)S(1)}, f32[16,1024]{1,0:T(8,128)S(1)}, u32[]{:S(2)}, u32[]{:S(2)}) collective-permute-start(f32[16,1024]{1,0:T(8,128)S(1)} %shard_map.77), channel_id=1, source_target_pairs={{0,32},{16,240},{32,0},{48,208},{64,96},{80,176},{96,64},{112,144}... | collective-permute-start | bytes 196616 | tf_op jit(solution)/shard_map/ppermute | solution.py:111
  85.9 3.7 %collective-permute-done.13.far2 = f32[16,1024]{1,0:T(8,128)S(1)} collective-permute-done((f32[16,1024]{1,0:T(8,128)S(1)}, f32[16,1024]{1,0:T(8,128)S(1)}, u32[]{:S(2)}, u32[]{:S(2)}) %collective-permute-start.13) | collective-permute-done | bytes 65568 | tf_op jit(solution)/shard_map/ppermute | solution.py:111
  89.7 0.0 collective-permute-done.12.far1
  89.7 0.6 collective-permute-done.11.far0
  90.4 0.1 collective-permute-start.15
  90.5 1.2 %collective-permute-done.15.got = f32[16,1024]{1,0:T(8,128)S(1)} collective-permute-done((f32[16,1024]{1,0:T(8,128)S(1)}, f32[16,1024]{1,0:T(8,128)S(1)}, u32[]{:S(2)}, u32[]{:S(2)}) %collective-permute-start.15) | collective-permute-done | bytes 65568 | tf_op jit(solution)/shard_map/ppermute | solution.py:106
  91.7 0.9 shard_map.79
  (14 shorter events, 0.2 us)
Async XLA Ops:
  0.0 1.0 %copy-start.5 = (f32[8,16,1024]{2,1,0:T(8,128)S(1)}, f32[8,16,1024]{2,1,0:T(8,128)}, u32[]{:S(2)}) copy-start(f32[8,16,1024]{2,1,0:T(8,128)} %field.3) | copy-start | bytes 1572868
  1.1 7.2 %collective-permute-start = (f32[4,16,1024]{2,1,0:T(8,128)S(1)}, f32[4,16,1024]{2,1,0:T(8,128)S(1)}, u32[]{:S(2)}, u32[]{:S(2)}) collective-permute-start(f32[4,16,1024]{2,1,0:T(8,128)S(1)} %get-tuple-element.32), channel_id=1, source_target_pairs={{0,16},{16,0},{32,48},{48,32},{64,80},{80,64},{96,112},{112,96},{1... | collective-permute-start | bytes 786440 | tf_op jit(solution)/shard_map/ppermute | solution.py:106
  4.4 6.1 %collective-permute-start.1 = (f32[4,16,1024]{2,1,0:T(8,128)S(1)}, f32[4,16,1024]{2,1,0:T(8,128)S(1)}, u32[]{:S(2)}, u32[]{:S(2)}) collective-permute-start(f32[4,16,1024]{2,1,0:T(8,128)S(1)} %get-tuple-element.33), channel_id=1, source_target_pairs={{0,240},{16,32},{32,16},{48,64},{64,48},{80,96},{96,80},{112,128},... | collective-permute-start | bytes 786440 | tf_op jit(solution)/shard_map/ppermute | solution.py:117
  4.7 1.7 %copy-start.1 = (f32[16,144,256]{2,1,0:T(8,128)S(1)}, f32[16,144,256]{2,1,0:T(8,128)}, u32[]{:S(2)}) copy-start(f32[16,144,256]{2,1,0:T(8,128)} %constant.7.clone.radial) | copy-start | bytes 7077892
  6.3 1.6 %copy-start.4 = (f32[16,16,2048]{2,1,0:T(8,128)S(1)}, f32[16,16,2048]{2,1,0:T(8,128)}, u32[]{:S(2)}) copy-start(f32[16,16,2048]{2,1,0:T(8,128)} %constant.8.clone.damping) | copy-start | bytes 6291460
  7.9 16.6 %copy-start.2 = (f32[8,16,1024]{2,1,0:T(8,128)S(1)}, f32[8,16,1024]{2,1,0:T(8,128)}, u32[]{:S(2)}) copy-start(f32[8,16,1024]{2,1,0:T(8,128)} %axial_rate.3) | copy-start | bytes 1572868
  7.9 16.6 %copy-start.3 = (f32[8,16,1024]{2,1,0:T(8,128)S(1)}, f32[8,16,1024]{2,1,0:T(8,128)}, u32[]{:S(2)}) copy-start(f32[8,16,1024]{2,1,0:T(8,128)} %swirl_rate.3) | copy-start | bytes 1572868
  8.3 16.2 %copy-start = (bf16[2,2,512,512]{3,2,1,0:T(8,128)(2,1)S(1)}, bf16[2,2,512,512]{3,2,1,0:T(8,128)(2,1)}, u32[]{:S(2)}) copy-start(bf16[2,2,512,512]{3,2,1,0:T(8,128)(2,1)} %constant.6.clone.azimuth) | copy-start | bytes 6291460
  26.7 6.7 %collective-permute-start.2 = (f32[2,16,512]{2,1,0:T(8,128)S(1)}, f32[2,16,512]{2,1,0:T(8,128)S(1)}, u32[]{:S(2)}, u32[]{:S(2)}) collective-permute-start(f32[2,16,512]{2,1,0:T(8,128)S(1)} %get-tuple-element.42), channel_id=1, source_target_pairs={{0,16},{16,0},{32,48},{48,32},{64,80},{80,64},{96,112},{112,96},{1... | collective-permute-start | bytes 196616 | tf_op jit(solution)/shard_map/ppermute | solution.py:106
  33.4 3.2 %collective-permute-start.3 = (f32[2,16,512]{2,1,0:T(8,128)S(1)}, f32[2,16,512]{2,1,0:T(8,128)S(1)}, u32[]{:S(2)}, u32[]{:S(2)}) collective-permute-start(f32[2,16,512]{2,1,0:T(8,128)S(1)} %get-tuple-element.43.block), channel_id=1, source_target_pairs={{0,32},{16,48},{32,0},{48,16},{64,96},{80,112},{96,64},{112,80},{1... | collective-permute-start | bytes 196616 | tf_op jit(solution)/shard_map/ppermute | solution.py:106
  36.6 6.0 %collective-permute-start.6 = (f32[2,16,512]{2,1,0:T(8,128)S(1)}, f32[2,16,512]{2,1,0:T(8,128)S(1)}, u32[]{:S(2)}, u32[]{:S(2)}) collective-permute-start(f32[2,16,512]{2,1,0:T(8,128)S(1)} %get-tuple-element.44), channel_id=1, source_target_pairs={{0,192},{16,208},{32,224},{48,240},{64,128},{80,144},{96,160},{112... | collective-permute-start | bytes 196616 | tf_op jit(solution)/shard_map/ppermute | solution.py:106
  40.5 8.2 %collective-permute-start.5 = (f32[2,16,512]{2,1,0:T(8,128)S(1)}, f32[2,16,512]{2,1,0:T(8,128)S(1)}, u32[]{:S(2)}, u32[]{:S(2)}) collective-permute-start(f32[2,16,512]{2,1,0:T(8,128)S(1)} %get-tuple-element.44), channel_id=1, source_target_pairs={{0,128},{16,144},{32,160},{48,176},{64,192},{80,208},{96,224},{112... | collective-permute-start | bytes 196616 | tf_op jit(solution)/shard_map/ppermute | solution.py:106
  42.1 8.2 %collective-permute-start.4 = (f32[2,16,512]{2,1,0:T(8,128)S(1)}, f32[2,16,512]{2,1,0:T(8,128)S(1)}, u32[]{:S(2)}, u32[]{:S(2)}) collective-permute-start(f32[2,16,512]{2,1,0:T(8,128)S(1)} %get-tuple-element.44), channel_id=1, source_target_pairs={{0,64},{16,80},{32,96},{48,112},{64,0},{80,16},{96,32},{112,48},{1... | collective-permute-start | bytes 196616 | tf_op jit(solution)/shard_map/ppermute | solution.py:106
  50.3 2.2 %collective-permute-start.7 = (f32[5,16,512]{2,1,0:T(8,128)S(1)}, f32[5,16,512]{2,1,0:T(8,128)S(1)}, u32[]{:S(2)}, u32[]{:S(2)}) collective-permute-start(f32[5,16,512]{2,1,0:T(8,128)S(1)} %get-tuple-element.50.packed), channel_id=1, source_target_pairs={{0,16},{16,0},{32,48},{48,32},{64,80},{80,64},{96,112},{112,96},{1... | collective-permute-start | bytes 491528 | tf_op jit(solution)/shard_map/ppermute | solution.py:106
  52.6 1.6 %collective-permute-start.8 = (f32[4,16,1024]{2,1,0:T(8,128)S(1)}, f32[4,16,1024]{2,1,0:T(8,128)S(1)}, u32[]{:S(2)}, u32[]{:S(2)}) collective-permute-start(f32[4,16,1024]{2,1,0:T(8,128)S(1)} %get-tuple-element.52), channel_id=1, source_target_pairs={{0,16},{16,0},{32,48},{48,32},{64,80},{80,64},{96,112},{112,96},{1... | collective-permute-start | bytes 786440 | tf_op jit(solution)/shard_map/ppermute | solution.py:106
  53.1 6.1 %collective-permute-start.9 = (f32[4,16,1024]{2,1,0:T(8,128)S(1)}, f32[4,16,1024]{2,1,0:T(8,128)S(1)}, u32[]{:S(2)}, u32[]{:S(2)}) collective-permute-start(f32[4,16,1024]{2,1,0:T(8,128)S(1)} %get-tuple-element.53), channel_id=1, source_target_pairs={{0,240},{16,32},{32,16},{48,64},{64,48},{80,96},{96,80},{112,128},... | collective-permute-start | bytes 786440 | tf_op jit(solution)/shard_map/ppermute | solution.py:117
  74.2 3.6 %collective-permute-start.10 = (f32[16,1024]{1,0:T(8,128)S(1)}, f32[16,1024]{1,0:T(8,128)S(1)}, u32[]{:S(2)}, u32[]{:S(2)}) collective-permute-start(f32[16,1024]{1,0:T(8,128)S(1)} %get-tuple-element.58.total), channel_id=1, source_target_pairs={{0,16},{16,0},{32,48},{48,32},{64,80},{80,64},{96,112},{112,96},{1... | collective-permute-start | bytes 196616 | tf_op jit(solution)/shard_map/ppermute | solution.py:106
  77.8 8.1 %collective-permute-start.14 = (f32[16,1024]{1,0:T(8,128)S(1)}, f32[16,1024]{1,0:T(8,128)S(1)}, u32[]{:S(2)}, u32[]{:S(2)}) collective-permute-start(f32[16,1024]{1,0:T(8,128)S(1)} %shard_map.77), channel_id=1, source_target_pairs={{0,192},{16,144},{32,224},{48,176},{64,128},{80,208},{96,160},{112... | collective-permute-start | bytes 196616 | tf_op jit(solution)/shard_map/ppermute | solution.py:111
  81.9 7.8 %collective-permute-start.13 = (f32[16,1024]{1,0:T(8,128)S(1)}, f32[16,1024]{1,0:T(8,128)S(1)}, u32[]{:S(2)}, u32[]{:S(2)}) collective-permute-start(f32[16,1024]{1,0:T(8,128)S(1)} %shard_map.77), channel_id=1, source_target_pairs={{0,64},{16,176},{32,96},{48,144},{64,0},{80,240},{96,32},{112,208}... | collective-permute-start | bytes 196616 | tf_op jit(solution)/shard_map/ppermute | solution.py:111
  83.1 6.6 %collective-permute-start.12 = (f32[16,1024]{1,0:T(8,128)S(1)}, f32[16,1024]{1,0:T(8,128)S(1)}, u32[]{:S(2)}, u32[]{:S(2)}) collective-permute-start(f32[16,1024]{1,0:T(8,128)S(1)} %shard_map.77), channel_id=1, source_target_pairs={{0,224},{16,112},{32,192},{48,80},{64,160},{80,48},{96,128},{112,1... | collective-permute-start | bytes 196616 | tf_op jit(solution)/shard_map/ppermute | solution.py:111
  84.4 5.9 %collective-permute-start.11 = (f32[16,1024]{1,0:T(8,128)S(1)}, f32[16,1024]{1,0:T(8,128)S(1)}, u32[]{:S(2)}, u32[]{:S(2)}) collective-permute-start(f32[16,1024]{1,0:T(8,128)S(1)} %shard_map.77), channel_id=1, source_target_pairs={{0,32},{16,240},{32,0},{48,208},{64,96},{80,176},{96,64},{112,144}... | collective-permute-start | bytes 196616 | tf_op jit(solution)/shard_map/ppermute | solution.py:111
  90.4 1.3 %collective-permute-start.15 = (f32[16,1024]{1,0:T(8,128)S(1)}, f32[16,1024]{1,0:T(8,128)S(1)}, u32[]{:S(2)}, u32[]{:S(2)}) collective-permute-start(f32[16,1024]{1,0:T(8,128)S(1)} %shard_map.78.below), channel_id=1, source_target_pairs={{0,16},{16,0},{32,48},{48,32},{64,80},{80,64},{96,112},{112,96},{1... | collective-permute-start | bytes 196616 | tf_op jit(solution)/shard_map/ppermute | solution.py:106

commit v5 on v4

--- a/solution.py
+++ b/solution.py
@@ -26,7 +26,7 @@
     -1.0 / 560.0,
 )
 HALO = 4
-FAR = ((7, 1), (3, 7), (5, 2), (4, 6))
+FAR = ((4, 6), (5, 2), (3, 7), (7, 1))
 
 
 def split_bf16(table):
@@ -316,7 +316,7 @@
     total = jnp.zeros_like(below)
     for far, (mask1, mask0) in zip((far0, far1, far2, far3), FAR):
         take = chip ^ jnp.where(odd, mask1, mask0) < chip
-        if mask0 == FAR[0][0]:
+        if mask0 in [masks[0] for masks in FAR]:
             take = jnp.logical_and(take, odd)
         total = total + jnp.where(take, far[...], 0.0)
     below[...] = total

time: 92.8 us -> 93.9 us (1.012)
    ppermute x4, waiting for transfers between devices: 4.39 us -> 5.39 us  [far_swap(): lax.ppermute(value, 'ax', [(i, i ^ 2 * masks[1 - i % 2]) for i in range(c...]
where the time goes in v5:
time: 93.9 us; the launch traced here: 93.6 us
  starting transfers between devices  29.1 us (31%)
  waiting for transfers between devices  26.9 us (29%)
  blocking collectives  26 us (28%)
  Pallas kernels  7.11 us (8%)
  local copies, waits for them, and re-layouts  4.31 us (5%)
    all_to_all x2, blocking collectives, body(): got = lax.all_to_all(sent, 'xs', split_axis=0, concat_axis=0, tiled=True)  26 us
    ppermute x10, starting transfers between devices, swap(): return lax.ppermute(value, 'ax', [(i, i ^ mask) for i in range(count)])  20.1 us
    ppermute x10, waiting for transfers between devices, swap(): return lax.ppermute(value, 'ax', [(i, i ^ mask) for i in range(count)])  14.4 us
    ppermute x4, starting transfers between devices, far_swap(): lax.ppermute(value, 'ax', [(i, i ^ 2 * masks[1 - i % 2]) for i in range(c...  8.11 us
    ppermute x2, waiting for transfers between devices, chain_swap(): return lax.ppermute(value, 'ax', pairs)  7.09 us
    pallas_call x14, Pallas kernels, call(): pl.pallas_call(kernel, out_shape=out_shape, in_specs=[pl.BlockSpec(memory...  5.89 us
    ppermute x4, waiting for transfers between devices, far_swap(): lax.ppermute(value, 'ax', [(i, i ^ 2 * masks[1 - i % 2]) for i in range(c...  5.39 us
    unnamed x12, local copies, waits for them, and re-layouts  4.31 us
  transfers between devices with their start and end apart: 16, of which 11 were waited for; matrix products, arithmetic and copies ran while one was open for 0% of the time, Pallas kernels for 1%

profile of v5, /device:TPU:1, one launch (start us, length us, event | category | flops | bytes accessed | tf_op | source)
XLA Modules:
  0.0 93.6 jit_solution(4720685997220594337)
XLA Ops:
  0.0 1.0 %copy-done.5 = f32[8,16,1024]{2,1,0:T(8,128)S(1)} copy-done((f32[8,16,1024]{2,1,0:T(8,128)S(1)}, f32[8,16,1024]{2,1,0:T(8,128)}, u32[]{:S(2)}) %copy-start.5) | copy-done | bytes 524312
  1.1 3.3 %collective-permute-start = (f32[4,16,1024]{2,1,0:T(8,128)S(1)}, f32[4,16,1024]{2,1,0:T(8,128)S(1)}, u32[]{:S(2)}, u32[]{:S(2)}) collective-permute-start(f32[4,16,1024]{2,1,0:T(8,128)S(1)} %get-tuple-element.32), channel_id=1, source_target_pairs={{0,16},{16,0},{32,48},{48,32},{64,80},{80,64},{96,112},{112,96},{1... | collective-permute-start | bytes 786440 | tf_op jit(solution)/shard_map/ppermute | solution.py:106
  4.4 0.0 collective-permute-start.1
  4.4 0.2 shard_map.64.inner
  4.7 0.0 copy-start.1
  4.7 1.7 %copy-done.1 = f32[16,144,256]{2,1,0:T(8,128)S(1)} copy-done((f32[16,144,256]{2,1,0:T(8,128)S(1)}, f32[16,144,256]{2,1,0:T(8,128)}, u32[]{:S(2)}) %copy-start.1) | copy-done | bytes 2359320
  6.3 1.6 %copy-done.4 = f32[16,16,2048]{2,1,0:T(8,128)S(1)} copy-done((f32[16,16,2048]{2,1,0:T(8,128)S(1)}, f32[16,16,2048]{2,1,0:T(8,128)}, u32[]{:S(2)}) %copy-start.4) | copy-done | bytes 2097176
  7.9 0.4 shard_map.66
  8.3 0.0 copy-start
  8.3 0.0 collective-permute-done.pair
  8.3 2.2 %collective-permute-done.1.chain = f32[4,16,1024]{2,1,0:T(8,128)S(1)} collective-permute-done((f32[4,16,1024]{2,1,0:T(8,128)S(1)}, f32[4,16,1024]{2,1,0:T(8,128)S(1)}, u32[]{:S(2)}, u32[]{:S(2)}) %collective-permute-start.1) | collective-permute-done | bytes 262176 | tf_op jit(solution)/shard_map/ppermute | solution.py:117
  10.5 0.4 shard_map.67
  10.9 13.6 %all_to_all.10 = f32[16,8,1024]{2,1,0:T(8,128)S(1)} all-to-all(f32[16,8,1024]{2,1,0:T(8,128)S(1)} %get-tuple-element.36), channel_id=1, replica_groups=mesh['ax'=16,'xs'=16] {'xs'}, dimensions={0} | all-to-all | bytes 1048576 | tf_op jit(solution)/shard_map/all_to_all | solution.py:406
  24.5 2.2 %shard_map.68 = (f32[8,16,1024]{2,1,0:T(8,128)S(1)}, f32[8,16,1024]{2,1,0:T(8,128)S(1)}, f32[2,16,512]{2,1,0:T(8,128)S(1)}, f32[2,16,512]{2,1,0:T(8,128)S(1)}) custom-call(f32[8,16,1024]{2,1,0:T(8,128)S(1)} %get-tuple-element.35.explicit, f32[128,1024]{1,0:T(8,128)S(1)} %bitcast.3, f32[128,256]{1,0:T(8,128)S(1)} %get-tuple-element.37.matrix, ...), custom_call_target="tpu_custom_call" | custom-call | tf_op jit(solution)/shard_map/pallas_call | solution.py:362
  26.7 5.8 %collective-permute-start.2 = (f32[2,16,512]{2,1,0:T(8,128)S(1)}, f32[2,16,512]{2,1,0:T(8,128)S(1)}, u32[]{:S(2)}, u32[]{:S(2)}) collective-permute-start(f32[2,16,512]{2,1,0:T(8,128)S(1)} %get-tuple-element.42), channel_id=1, source_target_pairs={{0,16},{16,0},{32,48},{48,32},{64,80},{80,64},{96,112},{112,96},{1... | collective-permute-start | bytes 196616 | tf_op jit(solution)/shard_map/ppermute | solution.py:106
  32.5 0.9 collective-permute-done.2.got
  33.4 0.1 collective-permute-start.3
  33.5 3.1 %collective-permute-done.3.got = f32[2,16,512]{2,1,0:T(8,128)S(1)} collective-permute-done((f32[2,16,512]{2,1,0:T(8,128)S(1)}, f32[2,16,512]{2,1,0:T(8,128)S(1)}, u32[]{:S(2)}, u32[]{:S(2)}) %collective-permute-start.3) | collective-permute-done | bytes 65568 | tf_op jit(solution)/shard_map/ppermute | solution.py:106
  36.6 3.8 %collective-permute-start.6 = (f32[2,16,512]{2,1,0:T(8,128)S(1)}, f32[2,16,512]{2,1,0:T(8,128)S(1)}, u32[]{:S(2)}, u32[]{:S(2)}) collective-permute-start(f32[2,16,512]{2,1,0:T(8,128)S(1)} %get-tuple-element.44), channel_id=1, source_target_pairs={{0,192},{16,208},{32,224},{48,240},{64,128},{80,144},{96,160},{112... | collective-permute-start | bytes 196616 | tf_op jit(solution)/shard_map/ppermute | solution.py:106
  40.5 1.6 %collective-permute-start.5 = (f32[2,16,512]{2,1,0:T(8,128)S(1)}, f32[2,16,512]{2,1,0:T(8,128)S(1)}, u32[]{:S(2)}, u32[]{:S(2)}) collective-permute-start(f32[2,16,512]{2,1,0:T(8,128)S(1)} %get-tuple-element.44), channel_id=1, source_target_pairs={{0,128},{16,144},{32,160},{48,176},{64,192},{80,208},{96,224},{112... | collective-permute-start | bytes 196616 | tf_op jit(solution)/shard_map/ppermute | solution.py:106
  42.1 0.6 collective-permute-start.4
  42.6 0.0 collective-permute-done.6.got3
  42.6 6.0 %collective-permute-done.5.got2 = f32[2,16,512]{2,1,0:T(8,128)S(1)} collective-permute-done((f32[2,16,512]{2,1,0:T(8,128)S(1)}, f32[2,16,512]{2,1,0:T(8,128)S(1)}, u32[]{:S(2)}, u32[]{:S(2)}) %collective-permute-start.5) | collective-permute-done | bytes 65568 | tf_op jit(solution)/shard_map/ppermute | solution.py:106
  48.6 1.6 %collective-permute-done.4.got1 = f32[2,16,512]{2,1,0:T(8,128)S(1)} collective-permute-done((f32[2,16,512]{2,1,0:T(8,128)S(1)}, f32[2,16,512]{2,1,0:T(8,128)S(1)}, u32[]{:S(2)}, u32[]{:S(2)}) %collective-permute-start.4) | collective-permute-done | bytes 65568 | tf_op jit(solution)/shard_map/ppermute | solution.py:106
  50.3 0.1 shard_map.71
  50.3 1.2 %collective-permute-start.7 = (f32[5,16,512]{2,1,0:T(8,128)S(1)}, f32[5,16,512]{2,1,0:T(8,128)S(1)}, u32[]{:S(2)}, u32[]{:S(2)}) collective-permute-start(f32[5,16,512]{2,1,0:T(8,128)S(1)} %get-tuple-element.50.packed), channel_id=1, source_target_pairs={{0,16},{16,0},{32,48},{48,32},{64,80},{80,64},{96,112},{112,96},{1... | collective-permute-start | bytes 491528 | tf_op jit(solution)/shard_map/ppermute | solution.py:106
  51.5 1.0 %collective-permute-done.7.got = f32[5,16,512]{2,1,0:T(8,128)S(1)} collective-permute-done((f32[5,16,512]{2,1,0:T(8,128)S(1)}, f32[5,16,512]{2,1,0:T(8,128)S(1)}, u32[]{:S(2)}, u32[]{:S(2)}) %collective-permute-start.7) | collective-permute-done | bytes 163872 | tf_op jit(solution)/shard_map/ppermute | solution.py:106
  52.5 0.1 shard_map.72
  52.6 0.5 collective-permute-start.8
  53.1 1.0 %collective-permute-start.9 = (f32[4,16,1024]{2,1,0:T(8,128)S(1)}, f32[4,16,1024]{2,1,0:T(8,128)S(1)}, u32[]{:S(2)}, u32[]{:S(2)}) collective-permute-start(f32[4,16,1024]{2,1,0:T(8,128)S(1)} %get-tuple-element.53), channel_id=1, source_target_pairs={{0,240},{16,32},{32,16},{48,64},{64,48},{80,96},{96,80},{112,128},... | collective-permute-start | bytes 786440 | tf_op jit(solution)/shard_map/ppermute | solution.py:117
  54.0 0.2 shard_map.73.inner
  54.3 0.0 collective-permute-done.8.pair
  54.3 4.9 %collective-permute-done.9.chain = f32[4,16,1024]{2,1,0:T(8,128)S(1)} collective-permute-done((f32[4,16,1024]{2,1,0:T(8,128)S(1)}, f32[4,16,1024]{2,1,0:T(8,128)S(1)}, u32[]{:S(2)}, u32[]{:S(2)}) %collective-permute-start.9) | collective-permute-done | bytes 262176 | tf_op jit(solution)/shard_map/ppermute | solution.py:117
  59.2 0.4 shard_map.74
  59.6 12.5 %all_to_all.11 = f32[16,8,1024]{2,1,0:T(8,128)S(1)} all-to-all(f32[16,8,1024]{2,1,0:T(8,128)S(1)} %get-tuple-element.55), channel_id=1, replica_groups=mesh['ax'=16,'xs'=16] {'xs'}, dimensions={0} | all-to-all | bytes 1048576 | tf_op jit(solution)/shard_map/all_to_all | solution.py:406
  72.0 2.1 %shard_map.75 = (f32[8,16,1024]{2,1,0:T(8,128)S(1)}, f32[8,16,1024]{2,1,0:T(8,128)S(1)}, f32[16,1024]{1,0:T(8,128)S(1)}) custom-call(f32[8,16,1024]{2,1,0:T(8,128)S(1)} %get-tuple-element.54.explicit, f32[128,1024]{1,0:T(8,128)S(1)} %bitcast.2, f32[128,256]{1,0:T(8,128)S(1)} %get-tuple-element.37.matrix, bf16[2,2,512,512]{3,2,1,0:T(8,128)(2,1)S(1)} %copy-done, ...), custom_call_target="tpu_custom_call" | custom-call | tf_op jit(solution)/shard_map/pallas_call | solution.py:362
  74.2 2.7 %collective-permute-start.10 = (f32[16,1024]{1,0:T(8,128)S(1)}, f32[16,1024]{1,0:T(8,128)S(1)}, u32[]{:S(2)}, u32[]{:S(2)}) collective-permute-start(f32[16,1024]{1,0:T(8,128)S(1)} %get-tuple-element.58.total), channel_id=1, source_target_pairs={{0,16},{16,0},{32,48},{48,32},{64,80},{80,64},{96,112},{112,96},{1... | collective-permute-start | bytes 196616 | tf_op jit(solution)/shard_map/ppermute | solution.py:106
  76.9 0.9 collective-permute-done.10.got.before
  77.8 2.6 %collective-permute-start.14 = (f32[16,1024]{1,0:T(8,128)S(1)}, f32[16,1024]{1,0:T(8,128)S(1)}, u32[]{:S(2)}, u32[]{:S(2)}) collective-permute-start(f32[16,1024]{1,0:T(8,128)S(1)} %shard_map.77), channel_id=1, source_target_pairs={{0,32},{16,240},{32,0},{48,208},{64,96},{80,176},{96,64},{112,144}... | collective-permute-start | bytes 196616 | tf_op jit(solution)/shard_map/ppermute | solution.py:111
  80.5 1.7 %collective-permute-start.13 = (f32[16,1024]{1,0:T(8,128)S(1)}, f32[16,1024]{1,0:T(8,128)S(1)}, u32[]{:S(2)}, u32[]{:S(2)}) collective-permute-start(f32[16,1024]{1,0:T(8,128)S(1)} %shard_map.77), channel_id=1, source_target_pairs={{0,224},{16,112},{32,192},{48,80},{64,160},{80,48},{96,128},{112,1... | collective-permute-start | bytes 196616 | tf_op jit(solution)/shard_map/ppermute | solution.py:111
  82.2 1.2 %collective-permute-start.12 = (f32[16,1024]{1,0:T(8,128)S(1)}, f32[16,1024]{1,0:T(8,128)S(1)}, u32[]{:S(2)}, u32[]{:S(2)}) collective-permute-start(f32[16,1024]{1,0:T(8,128)S(1)} %shard_map.77), channel_id=1, source_target_pairs={{0,64},{16,176},{32,96},{48,144},{64,0},{80,240},{96,32},{112,208}... | collective-permute-start | bytes 196616 | tf_op jit(solution)/shard_map/ppermute | solution.py:111
  83.4 2.6 %collective-permute-start.11 = (f32[16,1024]{1,0:T(8,128)S(1)}, f32[16,1024]{1,0:T(8,128)S(1)}, u32[]{:S(2)}, u32[]{:S(2)}) collective-permute-start(f32[16,1024]{1,0:T(8,128)S(1)} %shard_map.77), channel_id=1, source_target_pairs={{0,192},{16,144},{32,224},{48,176},{64,128},{80,208},{96,160},{112... | collective-permute-start | bytes 196616 | tf_op jit(solution)/shard_map/ppermute | solution.py:111
  85.9 0.0 collective-permute-done.14.far3
  86.0 3.2 %collective-permute-done.12.far1 = f32[16,1024]{1,0:T(8,128)S(1)} collective-permute-done((f32[16,1024]{1,0:T(8,128)S(1)}, f32[16,1024]{1,0:T(8,128)S(1)}, u32[]{:S(2)}, u32[]{:S(2)}) %collective-permute-start.12) | collective-permute-done | bytes 65568 | tf_op jit(solution)/shard_map/ppermute | solution.py:111
  89.2 2.1 %collective-permute-done.11.far0 = f32[16,1024]{1,0:T(8,128)S(1)} collective-permute-done((f32[16,1024]{1,0:T(8,128)S(1)}, f32[16,1024]{1,0:T(8,128)S(1)}, u32[]{:S(2)}, u32[]{:S(2)}) %collective-permute-start.11) | collective-permute-done | bytes 65568 | tf_op jit(solution)/shard_map/ppermute | solution.py:111
  91.4 0.5 collective-permute-start.15
  91.9 0.9 collective-permute-done.15.got
  92.8 0.9 shard_map.79
  (14 shorter events, 0.2 us)
Async XLA Ops:
  0.0 1.0 %copy-start.5 = (f32[8,16,1024]{2,1,0:T(8,128)S(1)}, f32[8,16,1024]{2,1,0:T(8,128)}, u32[]{:S(2)}) copy-start(f32[8,16,1024]{2,1,0:T(8,128)} %field.3) | copy-start | bytes 1572868
  1.1 7.2 %collective-permute-start = (f32[4,16,1024]{2,1,0:T(8,128)S(1)}, f32[4,16,1024]{2,1,0:T(8,128)S(1)}, u32[]{:S(2)}, u32[]{:S(2)}) collective-permute-start(f32[4,16,1024]{2,1,0:T(8,128)S(1)} %get-tuple-element.32), channel_id=1, source_target_pairs={{0,16},{16,0},{32,48},{48,32},{64,80},{80,64},{96,112},{112,96},{1... | collective-permute-start | bytes 786440 | tf_op jit(solution)/shard_map/ppermute | solution.py:106
  4.4 6.1 %collective-permute-start.1 = (f32[4,16,1024]{2,1,0:T(8,128)S(1)}, f32[4,16,1024]{2,1,0:T(8,128)S(1)}, u32[]{:S(2)}, u32[]{:S(2)}) collective-permute-start(f32[4,16,1024]{2,1,0:T(8,128)S(1)} %get-tuple-element.33), channel_id=1, source_target_pairs={{0,240},{16,32},{32,16},{48,64},{64,48},{80,96},{96,80},{112,128},... | collective-permute-start | bytes 786440 | tf_op jit(solution)/shard_map/ppermute | solution.py:117
  4.7 1.7 %copy-start.1 = (f32[16,144,256]{2,1,0:T(8,128)S(1)}, f32[16,144,256]{2,1,0:T(8,128)}, u32[]{:S(2)}) copy-start(f32[16,144,256]{2,1,0:T(8,128)} %constant.7.clone.radial) | copy-start | bytes 7077892
  6.3 1.6 %copy-start.4 = (f32[16,16,2048]{2,1,0:T(8,128)S(1)}, f32[16,16,2048]{2,1,0:T(8,128)}, u32[]{:S(2)}) copy-start(f32[16,16,2048]{2,1,0:T(8,128)} %constant.8.clone.damping) | copy-start | bytes 6291460
  7.9 16.6 %copy-start.2 = (f32[8,16,1024]{2,1,0:T(8,128)S(1)}, f32[8,16,1024]{2,1,0:T(8,128)}, u32[]{:S(2)}) copy-start(f32[8,16,1024]{2,1,0:T(8,128)} %axial_rate.3) | copy-start | bytes 1572868
  7.9 16.6 %copy-start.3 = (f32[8,16,1024]{2,1,0:T(8,128)S(1)}, f32[8,16,1024]{2,1,0:T(8,128)}, u32[]{:S(2)}) copy-start(f32[8,16,1024]{2,1,0:T(8,128)} %swirl_rate.3) | copy-start | bytes 1572868
  8.3 16.2 %copy-start = (bf16[2,2,512,512]{3,2,1,0:T(8,128)(2,1)S(1)}, bf16[2,2,512,512]{3,2,1,0:T(8,128)(2,1)}, u32[]{:S(2)}) copy-start(bf16[2,2,512,512]{3,2,1,0:T(8,128)(2,1)} %constant.6.clone.azimuth) | copy-start | bytes 6291460
  26.7 6.7 %collective-permute-start.2 = (f32[2,16,512]{2,1,0:T(8,128)S(1)}, f32[2,16,512]{2,1,0:T(8,128)S(1)}, u32[]{:S(2)}, u32[]{:S(2)}) collective-permute-start(f32[2,16,512]{2,1,0:T(8,128)S(1)} %get-tuple-element.42), channel_id=1, source_target_pairs={{0,16},{16,0},{32,48},{48,32},{64,80},{80,64},{96,112},{112,96},{1... | collective-permute-start | bytes 196616 | tf_op jit(solution)/shard_map/ppermute | solution.py:106
  33.4 3.2 %collective-permute-start.3 = (f32[2,16,512]{2,1,0:T(8,128)S(1)}, f32[2,16,512]{2,1,0:T(8,128)S(1)}, u32[]{:S(2)}, u32[]{:S(2)}) collective-permute-start(f32[2,16,512]{2,1,0:T(8,128)S(1)} %get-tuple-element.43.block), channel_id=1, source_target_pairs={{0,32},{16,48},{32,0},{48,16},{64,96},{80,112},{96,64},{112,80},{1... | collective-permute-start | bytes 196616 | tf_op jit(solution)/shard_map/ppermute | solution.py:106
  36.6 6.0 %collective-permute-start.6 = (f32[2,16,512]{2,1,0:T(8,128)S(1)}, f32[2,16,512]{2,1,0:T(8,128)S(1)}, u32[]{:S(2)}, u32[]{:S(2)}) collective-permute-start(f32[2,16,512]{2,1,0:T(8,128)S(1)} %get-tuple-element.44), channel_id=1, source_target_pairs={{0,192},{16,208},{32,224},{48,240},{64,128},{80,144},{96,160},{112... | collective-permute-start | bytes 196616 | tf_op jit(solution)/shard_map/ppermute | solution.py:106
  40.5 8.2 %collective-permute-start.5 = (f32[2,16,512]{2,1,0:T(8,128)S(1)}, f32[2,16,512]{2,1,0:T(8,128)S(1)}, u32[]{:S(2)}, u32[]{:S(2)}) collective-permute-start(f32[2,16,512]{2,1,0:T(8,128)S(1)} %get-tuple-element.44), channel_id=1, source_target_pairs={{0,128},{16,144},{32,160},{48,176},{64,192},{80,208},{96,224},{112... | collective-permute-start | bytes 196616 | tf_op jit(solution)/shard_map/ppermute | solution.py:106
  42.1 8.2 %collective-permute-start.4 = (f32[2,16,512]{2,1,0:T(8,128)S(1)}, f32[2,16,512]{2,1,0:T(8,128)S(1)}, u32[]{:S(2)}, u32[]{:S(2)}) collective-permute-start(f32[2,16,512]{2,1,0:T(8,128)S(1)} %get-tuple-element.44), channel_id=1, source_target_pairs={{0,64},{16,80},{32,96},{48,112},{64,0},{80,16},{96,32},{112,48},{1... | collective-permute-start | bytes 196616 | tf_op jit(solution)/shard_map/ppermute | solution.py:106
  50.3 2.2 %collective-permute-start.7 = (f32[5,16,512]{2,1,0:T(8,128)S(1)}, f32[5,16,512]{2,1,0:T(8,128)S(1)}, u32[]{:S(2)}, u32[]{:S(2)}) collective-permute-start(f32[5,16,512]{2,1,0:T(8,128)S(1)} %get-tuple-element.50.packed), channel_id=1, source_target_pairs={{0,16},{16,0},{32,48},{48,32},{64,80},{80,64},{96,112},{112,96},{1... | collective-permute-start | bytes 491528 | tf_op jit(solution)/shard_map/ppermute | solution.py:106
  52.6 1.6 %collective-permute-start.8 = (f32[4,16,1024]{2,1,0:T(8,128)S(1)}, f32[4,16,1024]{2,1,0:T(8,128)S(1)}, u32[]{:S(2)}, u32[]{:S(2)}) collective-permute-start(f32[4,16,1024]{2,1,0:T(8,128)S(1)} %get-tuple-element.52), channel_id=1, source_target_pairs={{0,16},{16,0},{32,48},{48,32},{64,80},{80,64},{96,112},{112,96},{1... | collective-permute-start | bytes 786440 | tf_op jit(solution)/shard_map/ppermute | solution.py:106
  53.1 6.1 %collective-permute-start.9 = (f32[4,16,1024]{2,1,0:T(8,128)S(1)}, f32[4,16,1024]{2,1,0:T(8,128)S(1)}, u32[]{:S(2)}, u32[]{:S(2)}) collective-permute-start(f32[4,16,1024]{2,1,0:T(8,128)S(1)} %get-tuple-element.53), channel_id=1, source_target_pairs={{0,240},{16,32},{32,16},{48,64},{64,48},{80,96},{96,80},{112,128},... | collective-permute-start | bytes 786440 | tf_op jit(solution)/shard_map/ppermute | solution.py:117
  74.2 3.6 %collective-permute-start.10 = (f32[16,1024]{1,0:T(8,128)S(1)}, f32[16,1024]{1,0:T(8,128)S(1)}, u32[]{:S(2)}, u32[]{:S(2)}) collective-permute-start(f32[16,1024]{1,0:T(8,128)S(1)} %get-tuple-element.58.total), channel_id=1, source_target_pairs={{0,16},{16,0},{32,48},{48,32},{64,80},{80,64},{96,112},{112,96},{1... | collective-permute-start | bytes 196616 | tf_op jit(solution)/shard_map/ppermute | solution.py:106
  77.8 8.1 %collective-permute-start.14 = (f32[16,1024]{1,0:T(8,128)S(1)}, f32[16,1024]{1,0:T(8,128)S(1)}, u32[]{:S(2)}, u32[]{:S(2)}) collective-permute-start(f32[16,1024]{1,0:T(8,128)S(1)} %shard_map.77), channel_id=1, source_target_pairs={{0,32},{16,240},{32,0},{48,208},{64,96},{80,176},{96,64},{112,144}... | collective-permute-start | bytes 196616 | tf_op jit(solution)/shard_map/ppermute | solution.py:111
  80.5 5.5 %collective-permute-start.13 = (f32[16,1024]{1,0:T(8,128)S(1)}, f32[16,1024]{1,0:T(8,128)S(1)}, u32[]{:S(2)}, u32[]{:S(2)}) collective-permute-start(f32[16,1024]{1,0:T(8,128)S(1)} %shard_map.77), channel_id=1, source_target_pairs={{0,224},{16,112},{32,192},{48,80},{64,160},{80,48},{96,128},{112,1... | collective-permute-start | bytes 196616 | tf_op jit(solution)/shard_map/ppermute | solution.py:111
  82.2 7.0 %collective-permute-start.12 = (f32[16,1024]{1,0:T(8,128)S(1)}, f32[16,1024]{1,0:T(8,128)S(1)}, u32[]{:S(2)}, u32[]{:S(2)}) collective-permute-start(f32[16,1024]{1,0:T(8,128)S(1)} %shard_map.77), channel_id=1, source_target_pairs={{0,64},{16,176},{32,96},{48,144},{64,0},{80,240},{96,32},{112,208}... | collective-permute-start | bytes 196616 | tf_op jit(solution)/shard_map/ppermute | solution.py:111
  83.4 8.0 %collective-permute-start.11 = (f32[16,1024]{1,0:T(8,128)S(1)}, f32[16,1024]{1,0:T(8,128)S(1)}, u32[]{:S(2)}, u32[]{:S(2)}) collective-permute-start(f32[16,1024]{1,0:T(8,128)S(1)} %shard_map.77), channel_id=1, source_target_pairs={{0,192},{16,144},{32,224},{48,176},{64,128},{80,208},{96,160},{112... | collective-permute-start | bytes 196616 | tf_op jit(solution)/shard_map/ppermute | solution.py:111
  91.4 1.4 %collective-permute-start.15 = (f32[16,1024]{1,0:T(8,128)S(1)}, f32[16,1024]{1,0:T(8,128)S(1)}, u32[]{:S(2)}, u32[]{:S(2)}) collective-permute-start(f32[16,1024]{1,0:T(8,128)S(1)} %shard_map.78.below), channel_id=1, source_target_pairs={{0,16},{16,0},{32,48},{48,32},{64,80},{80,64},{96,112},{112,96},{1... | collective-permute-start | bytes 196616 | tf_op jit(solution)/shard_map/ppermute | solution.py:106
